TPU v7x, 32 devices: a whole 2x2x4 slice. The times are simulated.
32 devices in a mesh: dp: 2 (over y), ctx: 4 (over z), tp: 4 (over x, core).
Axes of the slice: x: 2, y: 2, z: 4, core: 2. Of those that a mesh axis runs over, the one named last changes fastest.
Arguments:
- tokens: bfloat16 [4, 1024, 1024], P('dp', ('ctx', 'tp')), may hold values from -6 to 6
- segments: int32 [4, 1024], P('dp'), may hold values from 0 to 2, as said below
- ln1_gain: float32 [1024], replicated, may hold values from 0.25 to 1.75
- ln1_bias: float32 [1024], replicated, may hold values from -4 to 4
- qkv_weight: bfloat16 [1024, 3, 1024], P('dp', None, 'tp'), may hold values from -0.1875 to 0.1875
- qkv_bias: float32 [3, 1024], P(None, 'tp'), may hold values from -4 to 4
- out_weight: bfloat16 [1024, 1024], P('tp', 'dp'), may hold values from -1.5 to 1.5
- out_bias: float32 [1024], replicated, may hold values from -4 to 4
- ln2_gain: float32 [1024], replicated, may hold values from 0.25 to 1.75
- ln2_bias: float32 [1024], replicated, may hold values from -4 to 4
- fc_weight: bfloat16 [1024, 4096], P('dp', 'tp'), may hold values from -0.1875 to 0.1875
- fc_bias: float32 [4096], P('tp'), may hold values from -4 to 4
- proj_weight: bfloat16 [4096, 1024], P('tp', 'dp'), may hold values from -0.09375 to 0.09375
- proj_bias: float32 [1024], replicated, may hold values from -4 to 4
- grad_out: bfloat16 [4, 1024, 1024], P('dp', ('ctx', 'tp')), may hold values from -6 to 6
Outputs:
- block_out: bfloat16 [4, 1024, 1024], P('dp', ('ctx', 'tp'))
- tokens_grad: float32 [4, 1024, 1024], P('dp', ('ctx', 'tp'))
- ln1_gain_grad: float32 [1024], replicated
- ln1_bias_grad: float32 [1024], replicated
- qkv_weight_grad: float32 [1024, 3, 1024], P('dp', None, 'tp')
- qkv_bias_grad: float32 [3, 1024], P(None, 'tp')
- out_weight_grad: float32 [1024, 1024], P('tp', 'dp')
- out_bias_grad: float32 [1024], replicated
- ln2_gain_grad: float32 [1024], replicated
- ln2_bias_grad: float32 [1024], replicated
- fc_weight_grad: float32 [1024, 4096], P('dp', 'tp')
- fc_bias_grad: float32 [4096], P('tp')
- proj_weight_grad: float32 [4096, 1024], P('tp', 'dp')
- proj_bias_grad: float32 [1024], replicated
Inputs may be any that keep to these rules, and one draw needn't show every extreme that they name: `segments`: segment numbers never fall along a sequence, and each of 0, 1 and 2 occurs in every sequence.
All inputs are finite; a program needn't handle non-finite values.
Results may differ from a plain program's by a relative error of at most 0.012.
The roundings to bfloat16 on the way count: a program that leaves them out, or rounds other values in their place, can miss the bound.
Values may be sent and summed in bfloat16 or wider, within the bound.
A program may use at most 128 MiB of HBM per device.

v0:
```python
import jax
import jax.numpy as jnp
from jax import lax
from jax.sharding import PartitionSpec as P

HD = 64


EPSILON = 1e-05


def normalize(rows_in, gain_vec, bias_vec):
    row_mean = jnp.mean(rows_in, axis=-1, keepdims=True)
    centered = rows_in - row_mean
    spread = jnp.mean(centered * centered, axis=-1, keepdims=True)
    inverse = lax.rsqrt(spread + EPSILON)
    scaled = centered * inverse
    return (scaled * gain_vec + bias_vec, scaled, inverse)


def normalize_back(grad_rows, scaled, inverse, gain_vec):
    weighted = grad_rows * gain_vec
    centered = weighted - jnp.mean(weighted, axis=-1, keepdims=True)
    return (centered - scaled * jnp.mean(weighted * scaled, axis=-1, keepdims=True)) * inverse


def gelu_tanh(values_in):
    return jax.nn.gelu(values_in, approximate=True)


def rows_across(block_rows):
    return lax.all_gather(block_rows, "tp", axis=1, tiled=True)


def parts_across(partial_value):
    return lax.psum_scatter(partial_value, "tp", scatter_dimension=1, tiled=True)


def visible(segment, block_start, block_len):
    row_index = block_start + jnp.arange(block_len, dtype=jnp.int32)
    key_index = jnp.arange(segment.shape[0], dtype=jnp.int32)
    own_segment = lax.dynamic_slice_in_dim(segment, block_start, block_len)
    return (key_index[None, :] <= row_index[:, None]) & (segment[None, :] == own_segment[:, None])


def split_heads(query_rows, key_value_rows):
    block_len, width_tp = query_rows.shape
    head_count = width_tp // HD
    query_heads = query_rows.reshape(block_len, head_count, HD)
    key_heads = key_value_rows[:, 0].reshape(-1, head_count, HD)
    value_heads = key_value_rows[:, 1].reshape(-1, head_count, HD)
    return (query_heads, key_heads, value_heads)


def masked_scores(query_heads, key_heads, allowed):
    raw_scores = jnp.einsum(
        "qhe,khe->hqk", query_heads, key_heads, preferred_element_type=jnp.float32
    ) * HD ** (-0.5)
    return jnp.where(allowed[None], raw_scores, -1e30)


def shards(
    tokens,
    segments,
    ln1_gain,
    ln1_bias,
    qkv_weight,
    qkv_bias,
    out_weight,
    out_bias,
    ln2_gain,
    ln2_bias,
    fc_weight,
    fc_bias,
    proj_weight,
    proj_bias,
    grad_out,
):
    seq_count, shard_len, model_width = tokens.shape
    tp_count = lax.axis_size("tp")
    block_len = shard_len * tp_count
    block_start = lax.axis_index("ctx") * block_len
    weight_shards = (qkv_weight, out_weight, fc_weight, proj_weight)
    qkv_full, out_full, fc_full, proj_full = (
        lax.all_gather(weight_shards[0], "dp", axis=0, tiled=True),
        lax.all_gather(weight_shards[1], "dp", axis=1, tiled=True),
        lax.all_gather(weight_shards[2], "dp", axis=0, tiled=True),
        lax.all_gather(weight_shards[3], "dp", axis=1, tiled=True),
    )
    residual_in = tokens.astype(jnp.float32)
    normed_one, scaled_one, inverse_one = normalize(residual_in, ln1_gain, ln1_bias)
    attn_rows = rows_across(normed_one.astype(jnp.bfloat16)).reshape(-1, model_width)
    mixed_qkv = (
        jnp.einsum("td,dce->tce", attn_rows, qkv_full, preferred_element_type=jnp.float32)
        + qkv_bias
    )
    width_tp = mixed_qkv.shape[2]
    mixed_qkv = mixed_qkv.astype(jnp.bfloat16).reshape(seq_count, block_len, 3, width_tp)
    queries = mixed_qkv[:, :, 0]
    key_value = lax.all_gather(mixed_qkv[:, :, 1:], "ctx", axis=1, tiled=True)

    def attend_one(element):
        query_rows, key_value_rows, segment = element
        allowed = visible(segment, block_start, block_len)
        query_heads, key_heads, value_heads = split_heads(query_rows, key_value_rows)
        scores = masked_scores(query_heads, key_heads, allowed)
        highest = jnp.max(scores, axis=-1, keepdims=True)
        exponent = jnp.exp(scores - highest)
        denominator = jnp.sum(exponent, axis=-1, keepdims=True)
        attn_probs = (exponent / denominator).astype(jnp.bfloat16)
        attended_one = jnp.einsum(
            "hqk,khe->qhe", attn_probs, value_heads, preferred_element_type=jnp.float32
        )
        return (
            attended_one.reshape(block_len, width_tp).astype(jnp.bfloat16),
            highest + jnp.log(denominator),
        )

    attended, log_totals = lax.map(attend_one, (queries, key_value, segments))
    attended_flat = attended.reshape(-1, width_tp)
    branch = parts_across(
        jnp.dot(attended_flat, out_full, preferred_element_type=jnp.float32).reshape(
            seq_count, block_len, model_width
        )
    )
    middle = residual_in + branch + out_bias
    normed_two, scaled_two, inverse_two = normalize(middle, ln2_gain, ln2_bias)
    mlp_rows = rows_across(normed_two.astype(jnp.bfloat16)).reshape(-1, model_width)
    upward = jnp.dot(mlp_rows, fc_full, preferred_element_type=jnp.float32) + fc_bias
    hidden, gelu_back = jax.vjp(gelu_tanh, upward)
    hidden_low = hidden.astype(jnp.bfloat16)
    mlp_out = parts_across(
        jnp.dot(hidden_low, proj_full, preferred_element_type=jnp.float32).reshape(
            seq_count, block_len, model_width
        )
    )
    block_out = (middle + mlp_out + proj_bias).astype(jnp.bfloat16)
    qkv_full, out_full, fc_full, proj_full = (
        lax.all_gather(weight_shards[0], "dp", axis=0, tiled=True),
        lax.all_gather(weight_shards[1], "dp", axis=1, tiled=True),
        lax.all_gather(weight_shards[2], "dp", axis=0, tiled=True),
        lax.all_gather(weight_shards[3], "dp", axis=1, tiled=True),
    )
    grad_top = grad_out.astype(jnp.float32)
    grad_rows = rows_across(grad_out).reshape(-1, model_width)
    proj_grad = jnp.einsum("tf,td->fd", hidden_low, grad_rows, preferred_element_type=jnp.float32)
    grad_hidden = jnp.einsum("td,fd->tf", grad_rows, proj_full, preferred_element_type=jnp.float32)
    grad_up = gelu_back(grad_hidden)[0].astype(jnp.bfloat16)
    fc_bias_part = jnp.sum(grad_up, axis=0, dtype=jnp.float32)
    fc_grad = jnp.einsum("td,tf->df", mlp_rows, grad_up, preferred_element_type=jnp.float32)
    grad_normed_two = parts_across(
        jnp.einsum("tf,df->td", grad_up, fc_full, preferred_element_type=jnp.float32).reshape(
            seq_count, block_len, model_width
        )
    )
    grad_middle = grad_top + normalize_back(grad_normed_two, scaled_two, inverse_two, ln2_gain)
    middle_rows = rows_across(grad_middle.astype(jnp.bfloat16)).reshape(-1, model_width)
    out_grad = jnp.einsum(
        "th,td->hd", attended_flat, middle_rows, preferred_element_type=jnp.float32
    )
    grad_attended = (
        jnp.einsum("td,hd->th", middle_rows, out_full, preferred_element_type=jnp.float32)
        .astype(jnp.bfloat16)
        .reshape(seq_count, block_len, width_tp)
    )

    def attend_back(element):
        query_rows, key_value_rows, grad_att, log_total, segment = element
        allowed = visible(segment, block_start, block_len)
        query_heads, key_heads, value_heads = split_heads(query_rows, key_value_rows)
        head_count = query_heads.shape[1]
        key_len = key_heads.shape[0]
        grad_heads = grad_att.reshape(block_len, head_count, HD)
        attn_probs = jnp.exp(masked_scores(query_heads, key_heads, allowed) - log_total)
        grad_probs = jnp.einsum(
            "qhe,khe->hqk", grad_heads, value_heads, preferred_element_type=jnp.float32
        )
        inner_sum = jnp.sum(attn_probs * grad_probs, axis=-1, keepdims=True)
        grad_scores = (attn_probs * (grad_probs - inner_sum)).astype(jnp.bfloat16)
        grad_query = jnp.einsum(
            "hqk,khe->qhe", grad_scores, key_heads, preferred_element_type=jnp.float32
        ) * HD ** (-0.5)
        grad_key = jnp.einsum(
            "hqk,qhe->khe", grad_scores, query_heads, preferred_element_type=jnp.float32
        ) * HD ** (-0.5)
        grad_value = jnp.einsum(
            "hqk,qhe->khe",
            attn_probs.astype(jnp.bfloat16),
            grad_heads,
            preferred_element_type=jnp.float32,
        )
        grad_pair = jnp.stack(
            [grad_key.reshape(key_len, width_tp), grad_value.reshape(key_len, width_tp)], axis=1
        )
        return (grad_query.reshape(block_len, width_tp), grad_pair)

    grad_queries, grad_pairs = lax.map(
        attend_back, (queries, key_value, grad_attended, log_totals, segments)
    )
    grad_pairs_own = lax.psum_scatter(grad_pairs, "ctx", scatter_dimension=1, tiled=True)
    grad_mixed = (
        jnp.concatenate([grad_queries[:, :, None], grad_pairs_own], axis=2)
        .astype(jnp.bfloat16)
        .reshape(-1, 3, width_tp)
    )
    qkv_grad = jnp.einsum("td,tce->dce", attn_rows, grad_mixed, preferred_element_type=jnp.float32)
    qkv_bias_part = jnp.sum(grad_mixed, axis=0, dtype=jnp.float32)
    grad_normed_one = parts_across(
        jnp.einsum("tce,dce->td", grad_mixed, qkv_full, preferred_element_type=jnp.float32).reshape(
            seq_count, block_len, model_width
        )
    )
    tokens_grad = grad_middle + normalize_back(grad_normed_one, scaled_one, inverse_one, ln1_gain)
    local_grads = (qkv_grad, out_grad, fc_grad, proj_grad)
    grad_pieces = (
        lax.psum_scatter(local_grads[0], ("dp", "ctx"), scatter_dimension=0, tiled=True),
        lax.psum_scatter(local_grads[1], ("dp", "ctx"), scatter_dimension=1, tiled=True),
        lax.psum_scatter(local_grads[2], ("dp", "ctx"), scatter_dimension=0, tiled=True),
        lax.psum_scatter(local_grads[3], ("dp", "ctx"), scatter_dimension=1, tiled=True),
    )
    qkv_weight_grad, out_weight_grad, fc_weight_grad, proj_weight_grad = (
        lax.all_gather(grad_pieces[0], "ctx", axis=0, tiled=True),
        lax.all_gather(grad_pieces[1], "ctx", axis=1, tiled=True),
        lax.all_gather(grad_pieces[2], "ctx", axis=0, tiled=True),
        lax.all_gather(grad_pieces[3], "ctx", axis=1, tiled=True),
    )
    tp_index = lax.axis_index("tp")
    ff_tp = fc_bias.shape[0]
    qkv_bias_wide = lax.dynamic_update_slice(
        jnp.zeros((3, width_tp * tp_count), jnp.float32),
        qkv_bias_part,
        (jnp.int32(0), tp_index * width_tp),
    )
    fc_bias_wide = lax.dynamic_update_slice(
        jnp.zeros((ff_tp * tp_count,), jnp.float32), fc_bias_part, (tp_index * ff_tp,)
    )
    summed = lax.psum(
        (
            jnp.sum(grad_normed_one * scaled_one, axis=(0, 1)),
            jnp.sum(grad_normed_one, axis=(0, 1)),
            qkv_bias_wide,
            jnp.sum(grad_middle, axis=(0, 1)),
            jnp.sum(grad_normed_two * scaled_two, axis=(0, 1)),
            jnp.sum(grad_normed_two, axis=(0, 1)),
            fc_bias_wide,
            jnp.sum(grad_top, axis=(0, 1)),
        ),
        ("dp", "ctx", "tp"),
    )
    (
        ln1_gain_grad,
        ln1_bias_grad,
        qkv_bias_total,
        out_bias_grad,
        ln2_gain_grad,
        ln2_bias_grad,
        fc_bias_total,
        proj_bias_grad,
    ) = summed
    qkv_bias_grad = lax.dynamic_slice_in_dim(qkv_bias_total, tp_index * width_tp, width_tp, axis=1)
    fc_bias_grad = lax.dynamic_slice_in_dim(fc_bias_total, tp_index * ff_tp, ff_tp, axis=0)
    return (
        block_out,
        tokens_grad,
        ln1_gain_grad,
        ln1_bias_grad,
        qkv_weight_grad,
        qkv_bias_grad,
        out_weight_grad,
        out_bias_grad,
        ln2_gain_grad,
        ln2_bias_grad,
        fc_weight_grad,
        fc_bias_grad,
        proj_weight_grad,
        proj_bias_grad,
    )


def solution(mesh):
    placed = (
        P("dp", ("ctx", "tp"), None),
        P("dp", None),
        P(),
        P(),
        P("dp", None, "tp"),
        P(None, "tp"),
        P("tp", "dp"),
        P(),
        P(),
        P(),
        P("dp", "tp"),
        P("tp"),
        P("tp", "dp"),
        P(),
        P("dp", ("ctx", "tp"), None),
    )
    return jax.shard_map(
        shards,
        mesh=mesh,
        in_specs=placed,
        out_specs=(
            P("dp", ("ctx", "tp"), None),
            P("dp", ("ctx", "tp"), None),
            P(),
            P(),
            P("dp", None, "tp"),
            P(None, "tp"),
            P("tp", "dp"),
            P(),
            P(),
            P(),
            P("dp", "tp"),
            P("tp"),
            P("tp", "dp"),
            P(),
        ),
        check_vma=False,
    )
```

profile of v0, /device:TPU:0, one launch (start us, length us, event | category | flops | bytes accessed | tf_op | source)
XLA Modules:
  0.0 979.5 jit_solution(17976982900115814112)
XLA Ops:
  10.2 1.9 fusion.30
  12.2 27.3 %all-gather.14.cloned.1.call-done = bf16[1024,3,256]{2,0,1:T(8,128)(2,1)} async-done(((bf16[512,3,256]{2,0,1:T(8,128)(2,1)}), bf16[1024,3,256]{2,0,1:T(8,128)(2,1)}) %all-gather.14.cloned.1.call-update) | async-done | bytes 1572880 | tf_op jit(solution)/shard_map/all_gather | solution.py:85
  39.5 18.9 %all-gather.12.cloned.1.call-done = bf16[2,256,1024]{2,1,0:T(8,128)(2,1)} async-done(((bf16[2,64,1024]{2,1,0:T(8,128)(2,1)}), bf16[2,256,1024]{2,1,0:T(8,128)(2,1)}) %all-gather.12.cloned.1.call-update) | async-done | bytes 1048592 | tf_op jit(solution)/shard_map/all_gather | solution.py:32
  58.4 2.7 add_convert_fusion
  62.3 9.1 all_gather.46
  71.6 37.0 %all-gather.16.cloned.1.call-done = bf16[2,1024,2,256]{1,3,2,0:T(8,128)(2,1)} async-done(((bf16[2,256,2,256]{1,3,2,0:T(8,128)(2,1)}), bf16[2,1024,2,256]{1,3,2,0:T(8,128)(2,1)}) %all-gather.16.cloned.1.call-update) | async-done | bytes 2097168 | tf_op jit(solution)/shard_map/all_gather | solution.py:100
  108.6 11.3 %while.30 = (s32[]{:T(128)}, bf16[2,256,256]{1,2,0:T(8,128)(2,1)S(1)}, f32[2,4,256,1]{2,1,3,0:T(4,128)S(1)}, bf16[2,1024,2,256]{1,3,2,0:T(8,128)(2,1)}, s32[]{:T...) while((s32[]{:T(128)}, ...), condition=%wide.region_5.6_spmd, body=%wide.region_2.5_spmd.sunk | while | flops 281869568 | bytes 19711128 | solution.py:119
  109.0 1.3 dynamic-slice_bitcast_fusion.6
  112.7 1.6 fusion.112
  114.7 1.3 dynamic-slice_bitcast_fusion.6
  118.3 1.6 fusion.112
  120.0 1.8 fusion.38
  122.4 29.2 %reduce-scatter.10.cloned.1.call-done = f32[2,64,1024]{2,1,0:T(8,128)} async-done(((f32[2,256,1024]{2,1,0:T(8,128)}), f32[2,64,1024]{2,1,0:T(8,128)}) %reduce-scatter.10.cloned.1.call-update) | async-done | bytes 524304 | tf_op jit(solution)/shard_map/reduce_scatter | solution.py:36
  155.5 30.8 %all-gather.20.cloned.1.call-done = bf16[1024,1024]{1,0:T(8,128)(2,1)} async-done(((bf16[512,1024]{1,0:T(8,128)(2,1)}), bf16[1024,1024]{1,0:T(8,128)(2,1)}) %all-gather.20.cloned.1.call-update) | async-done | bytes 2097168 | tf_op jit(solution)/shard_map/all_gather | solution.py:87
  186.2 18.8 %all-gather.18.cloned.1.call-done = bf16[2,256,1024]{2,1,0:T(8,128)(2,1)} async-done(((bf16[2,64,1024]{2,1,0:T(8,128)(2,1)}), bf16[2,256,1024]{2,1,0:T(8,128)(2,1)}) %all-gather.18.cloned.1.call-update) | async-done | bytes 1048592 | tf_op jit(solution)/shard_map/all_gather | solution.py:32
  205.1 4.5 fusion.51
  209.6 13.9 %all-gather.24.cloned.1.call-done = bf16[2,256,1024]{2,1,0:T(8,128)(2,1)} async-done(((bf16[2,64,1024]{2,1,0:T(8,128)(2,1)}), bf16[2,256,1024]{2,1,0:T(8,128)(2,1)}) %all-gather.24.cloned.1.call-update) | async-done | bytes 1048592 | tf_op jit(solution)/shard_map/all_gather | solution.py:32
  223.5 34.8 %all-gather.22.cloned.1.call-done = bf16[1024,1024]{1,0:T(8,128)(2,1)} async-done(((bf16[1024,512]{1,0:T(8,128)(2,1)}), bf16[1024,1024]{1,0:T(8,128)(2,1)}) %all-gather.22.cloned.1.call-update) | async-done | bytes 2097168 | tf_op jit(solution)/shard_map/all_gather | solution.py:88
  258.2 5.2 convert_reduce_fusion
  263.4 2.6 fusion.52
  266.3 5.1 fusion.43
  271.4 26.2 %reduce-scatter.14.cloned.1.call-done = f32[2,64,1024]{2,1,0:T(8,128)} async-done(((f32[2,256,1024]{2,1,0:T(8,128)}), f32[2,64,1024]{2,1,0:T(8,128)}) %reduce-scatter.14.cloned.1.call-update) | async-done | bytes 524304 | tf_op jit(solution)/shard_map/reduce_scatter | solution.py:36
  297.6 1.3 multiply_reduce_fusion.1
  298.9 32.5 %reduce-scatter.12.cloned.1.call-done = f32[2,64,1024]{2,1,0:T(8,128)} async-done(((f32[2,256,1024]{2,1,0:T(8,128)}), f32[2,64,1024]{2,1,0:T(8,128)}) %reduce-scatter.12.cloned.1.call-update) | async-done | bytes 524304 | tf_op jit(solution)/shard_map/reduce_scatter | solution.py:36
  331.5 2.2 fusion.45
  334.5 16.8 %all-gather.26.cloned.1.call-done = bf16[2,256,1024]{2,1,0:T(8,128)(2,1)} async-done(((bf16[2,64,1024]{2,1,0:T(8,128)(2,1)}), bf16[2,256,1024]{2,1,0:T(8,128)(2,1)}) %all-gather.26.cloned.1.call-update) | async-done | bytes 1048592 | tf_op jit(solution)/shard_map/all_gather | solution.py:32
  351.3 2.4 convolution_convert_fusion
  353.7 29.5 %while.31 = (s32[]{:T(128)}, bf16[2,256,256]{2,1,0:T(8,128)(2,1)}, f32[2,1024,2,256]{3,1,2,0:T(8,128)}, bf16[2,1024,2,256]{1,3,2,0:T(8,128)(2,1)}, s32[]{:T(128)...) while((s32[]{:T(128)}, bf16[2,256,256]{2,1,0:T(8,128)(2,1)}, ...), condition=%wide.region_15.16_spmd, body=%wide.region_13.15_spmd.sunk | while | flops 688520448 | bytes 54965424 | solution.py:197
  355.2 1.3 dynamic-slice_bitcast_fusion.7
  357.3 1.3 fusion.126
  358.6 1.7 multiply_reduce_fusion.7
  360.3 1.3 multiply_convert_fusion.5
  362.8 1.5 maximum_bitcast_fusion.2
  364.3 1.9 copy.76
  367.0 1.5 constant_dynamic-update-slice_fusion.9
  369.9 1.3 dynamic-slice_bitcast_fusion.7
  372.1 1.3 fusion.126
  373.3 1.7 multiply_reduce_fusion.7
  375.1 1.3 multiply_convert_fusion.5
  377.6 1.5 maximum_bitcast_fusion.2
  379.1 1.9 copy.76
  381.8 1.5 constant_dynamic-update-slice_fusion.9
  384.4 5.2 fusion.42
  389.8 1.3 copy-done.3
  391.4 3.3 fusion.53
  394.7 65.5 %reduce-scatter.16.cloned.1.call-done = f32[2,256,2,256]{3,1,2,0:T(8,128)} async-done(((f32[2,1024,2,256]{3,1,2,0:T(8,128)}), f32[2,256,2,256]{3,1,2,0:T(8,128)}) %reduce-scatter.16.cloned.1.call-update) | async-done | bytes 1048592 | tf_op jit(solution)/shard_map/reduce_scatter | solution.py:200
  460.2 1.3 convert.12
  461.5 2.7 convolution_bitcast_fusion
  465.5 1.4 convolution_bitcast_fusion.2
  467.0 85.7 %reduce-scatter.26.cloned.1.call-done = f32[1024,128]{1,0:T(8,128)} async-done(((f32[1024,1024]{1,0:T(8,128)}), f32[1024,128]{1,0:T(8,128)}) %reduce-scatter.26.cloned.1.call-update) | async-done | bytes 524304 | tf_op jit(solution)/shard_map/reduce_scatter | solution.py:219
  552.8 91.5 %reduce-scatter.24.cloned.1.call-done = f32[128,1024]{1,0:T(8,128)} async-done(((f32[1024,1024]{1,0:T(8,128)}), f32[128,1024]{1,0:T(8,128)}) %reduce-scatter.24.cloned.1.call-update) | async-done | bytes 524304 | tf_op jit(solution)/shard_map/reduce_scatter | solution.py:218
  644.3 3.7 convolution_bitcast_fusion.1
  648.2 74.4 %reduce-scatter.20.cloned.1.call-done = f32[128,3,256]{2,0,1:T(8,128)} async-done(((f32[1024,3,256]{2,0,1:T(8,128)}), f32[128,3,256]{2,0,1:T(8,128)}) %reduce-scatter.20.cloned.1.call-update) | async-done | bytes 393232 | tf_op jit(solution)/shard_map/reduce_scatter | solution.py:216
  722.9 66.7 %reduce-scatter.22.cloned.1.call-done = f32[256,128]{1,0:T(8,128)} async-done(((f32[256,1024]{1,0:T(8,128)}), f32[256,128]{1,0:T(8,128)}) %reduce-scatter.22.cloned.1.call-update) | async-done | bytes 131088 | tf_op jit(solution)/shard_map/reduce_scatter | solution.py:217
  789.6 17.8 %all_gather.53 = f32[256,512]{1,0:T(8,128)S(1)} all-gather(f32[256,128]{1,0:T(8,128)} %reduce-scatter.22.cloned.1.call-done), channel_id=1, replica_groups=mesh['dp'=2,'ctx'=4,'tp'=4] {'ctx'}, dimensions={1}, use_global_device_ids=true | all-gather | bytes 655360 | tf_op jit(solution)/shard_map/all_gather | solution.py:223
  807.4 30.5 %all-gather.32.cloned.1.call-done = f32[1024,512]{1,0:T(8,128)} async-done(((f32[1024,128]{1,0:T(8,128)}), f32[1024,512]{1,0:T(8,128)}) %all-gather.32.cloned.1.call-update) | async-done | bytes 2097168 | tf_op jit(solution)/shard_map/all_gather | solution.py:225
  838.0 46.0 %all-gather.30.cloned.1.call-done = f32[512,1024]{1,0:T(8,128)} async-done(((f32[128,1024]{1,0:T(8,128)}), f32[512,1024]{1,0:T(8,128)}) %all-gather.30.cloned.1.call-update) | async-done | bytes 2097168 | tf_op jit(solution)/shard_map/all_gather | solution.py:224
  884.2 33.2 %reduce-scatter.18.cloned.1.call-done = f32[2,64,1024]{2,1,0:T(8,128)} async-done(((f32[2,256,1024]{2,1,0:T(8,128)}), f32[2,64,1024]{2,1,0:T(8,128)}) %reduce-scatter.18.cloned.1.call-update) | async-done | bytes 524304 | tf_op jit(solution)/shard_map/reduce_scatter | solution.py:36
  917.4 1.3 fusion.35
  918.8 43.3 %all-reduce = (f32[1024]{0:T(1024)}, f32[1024]{0:T(1024)}, f32[3,1024]{1,0:T(4,128)S(1)}, f32[1024]{0:T(1024)}, f32[1024]{0:T(1024)}, /*index=5*/f32[1024]{0:T(1024)}, f32[4096]{0:T(1024)S(1)}, f32[1024]{0:T(1024)}) all-reduce(f32[1024]{0:T(1024)S(1)} %get-tuple-element.328, ...), channel_id=1, replica_groups=mesh['dp'=2,'ctx'=4,'tp'=4] {'dp','ctx','tp'}, use_global_device_ids=true, to_apply=%region_21.22 | all-reduce | flops 13312 | bytes 106496 | tf_op jit(solution)/shard_map/psum | solution.py:237
  963.3 2.1 fusion.34
  965.4 2.8 copy.105
  969.0 1.3 copy.107
  971.3 1.3 copy.108
  (172 shorter events, 30.5 us)
Async XLA Ops:
  7.2 51.2 %copy-start.25 = (f32[3,256]{1,0:T(4,128)S(1)}, f32[3,256]{1,0:T(4,128)}, u32[]{:S(2)}) copy-start(f32[3,256]{1,0:T(4,128)} %param.24) | copy-start | bytes 9220
  7.2 32.3 %all-gather.14.cloned.1.call-start = ((), (), s32[]{:S(2)}) async-start(), calls=%async_computation.10 | async-start | bytes 2359296 | tf_op jit(solution)/shard_map/all_gather | solution.py:85
  7.9 50.5 %all-gather.12.cloned.1.call-start = ((), (), s32[]{:S(2)}) async-start(), calls=%async_computation.9 | async-start | bytes 1310720 | tf_op jit(solution)/shard_map/all_gather | solution.py:32
  9.0 49.4 %copy-start.15 = (f32[2,64]{1,0:T(2,128)}, f32[2,64]{1,0:T(2,128)S(1)}, u32[]{:S(2)}) copy-start(f32[2,64]{1,0:T(2,128)S(1)} %broadcast_multiply_fusion.5) | copy-start | bytes 1540
  10.2 48.2 %copy-start.17 = (f32[2,64]{1,0:T(2,128)}, f32[2,64]{1,0:T(2,128)S(1)}, u32[]{:S(2)}) copy-start(f32[2,64]{1,0:T(2,128)S(1)} %add_rsqrt_fusion.1) | copy-start | bytes 1540
  12.2 96.4 %all-gather.16.cloned.1.call-start = ((), (), s32[]{:S(2)}) async-start(), calls=%async_computation.11 | async-start | bytes 2621440 | tf_op jit(solution)/shard_map/all_gather | solution.py:100
  61.1 1.2 copy-start.11
  61.1 47.5 %copy-start.10 = (s32[2,1024]{1,0:T(2,128)S(1)}, s32[2,1024]{1,0:T(2,128)}, u32[]{:S(2)}) copy-start(s32[2,1024]{1,0:T(2,128)} %param.20) | copy-start | bytes 24580
  62.2 89.4 %reduce-scatter.10.cloned.1.call-start = ((), (), s32[]{:S(2)}) async-start(), calls=%async_computation.12 | async-start | bytes 2621440 | tf_op jit(solution)/shard_map/reduce_scatter | solution.py:36
  120.0 1.8 copy-start.6
  121.8 29.9 %copy-start = (bf16[2,64,1024]{2,1,0:T(8,128)(2,1)S(1)}, bf16[2,64,1024]{2,1,0:T(8,128)(2,1)}, u32[]{:S(2)}) copy-start(bf16[2,64,1024]{2,1,0:T(8,128)(2,1)} %param.19) | copy-start | bytes 786436
  121.8 29.9 %copy-start.19 = (f32[1024]{0:T(1024)S(1)}, f32[1024]{0:T(1024)}, u32[]{:S(2)}) copy-start(f32[1024]{0:T(1024)} %param.26) | copy-start | bytes 12292
  121.8 31.3 %copy-start.13 = (f32[1024]{0:T(1024)S(1)}, f32[1024]{0:T(1024)}, u32[]{:S(2)}) copy-start(f32[1024]{0:T(1024)} %param.27) | copy-start | bytes 12292
  121.8 31.3 %copy-start.20 = (f32[1024]{0:T(1024)S(1)}, f32[1024]{0:T(1024)}, u32[]{:S(2)}) copy-start(f32[1024]{0:T(1024)} %param.28) | copy-start | bytes 12292
  121.8 64.4 %all-gather.20.cloned.1.call-start = ((), (), s32[]{:S(2)}) async-start(), calls=%async_computation.14 | async-start | bytes 3145728 | tf_op jit(solution)/shard_map/all_gather | solution.py:87
  122.4 82.7 %all-gather.18.cloned.1.call-start = ((), (), s32[]{:S(2)}) async-start(), calls=%async_computation.13 | async-start | bytes 1310720 | tf_op jit(solution)/shard_map/all_gather | solution.py:32
  153.9 69.5 %all-gather.24.cloned.1.call-start = ((), (), s32[]{:S(2)}) async-start(), calls=%async_computation.17 | async-start | bytes 1310720 | tf_op jit(solution)/shard_map/all_gather | solution.py:32
  154.7 103.5 %all-gather.22.cloned.1.call-start = ((), (), s32[]{:S(2)}) async-start(), calls=%async_computation.15 | async-start | bytes 3145728 | tf_op jit(solution)/shard_map/all_gather | solution.py:88
  155.4 142.2 %reduce-scatter.14.cloned.1.call-start = ((), (), s32[]{:S(2)}) async-start(), calls=%async_computation.18 | async-start | bytes 2621440 | tf_op jit(solution)/shard_map/reduce_scatter | solution.py:36
  205.1 53.2 %copy-start.26 = (f32[1024]{0:T(1024)S(1)}, f32[1024]{0:T(1024)}, u32[]{:S(2)}) copy-start(f32[1024]{0:T(1024)} %param.30) | copy-start | bytes 12292
  258.2 5.2 copy-start.22
  263.4 2.6 copy-start.8
  266.1 65.4 %reduce-scatter.12.cloned.1.call-start = ((), (), s32[]{:S(2)}) async-start(), calls=%async_computation.16 | async-start | bytes 2621440 | tf_op jit(solution)/shard_map/reduce_scatter | solution.py:36
  271.3 60.1 %copy-start.4 = (bf16[2,64,1024]{2,1,0:T(8,128)(2,1)S(1)}, bf16[2,64,1024]{2,1,0:T(8,128)(2,1)}, u32[]{:S(2)}) copy-start(bf16[2,64,1024]{2,1,0:T(8,128)(2,1)} %param.33) | copy-start | bytes 786436
  271.3 60.1 %copy-start.21 = (f32[1024]{0:T(1024)S(1)}, f32[1024]{0:T(1024)}, u32[]{:S(2)}) copy-start(f32[1024]{0:T(1024)} %param.32) | copy-start | bytes 12292
  271.4 79.9 %all-gather.26.cloned.1.call-start = ((), (), s32[]{:S(2)}) async-start(), calls=%async_computation.19 | async-start | bytes 1310720 | tf_op jit(solution)/shard_map/all_gather | solution.py:32
  334.4 125.8 %reduce-scatter.16.cloned.1.call-start = ((), (), s32[]{:S(2)}) async-start(), calls=%async_computation.20 | async-start | bytes 5242880 | tf_op jit(solution)/shard_map/reduce_scatter | solution.py:200
  383.2 1.2 copy-start.24
  383.2 169.4 %reduce-scatter.26.cloned.1.call-start = ((), (), s32[]{:S(2)}) async-start(), calls=%async_computation.27 | async-start | bytes 4718592 | tf_op jit(solution)/shard_map/reduce_scatter | solution.py:219
  389.7 1.4 copy-start.3
  389.7 1.7 copy-start.9
  389.7 254.6 %reduce-scatter.24.cloned.1.call-start = ((), (), s32[]{:S(2)}) async-start(), calls=%async_computation.25 | async-start | bytes 4718592 | tf_op jit(solution)/shard_map/reduce_scatter | solution.py:218
  394.6 66.8 %copy-start.12 = (bf16[2,256,256]{2,1,0:T(8,128)(2,1)S(1)}, bf16[2,256,256]{2,1,0:T(8,128)(2,1)}, u32[]{:S(2)}) copy-start(bf16[2,256,256]{2,1,0:T(8,128)(2,1)} %get-tuple-element.304) | copy-start | bytes 786436
  394.6 66.8 %copy-start.23 = (bf16[2,256,1024]{2,1,0:T(8,128)(2,1)S(1)}, bf16[2,256,1024]{2,1,0:T(8,128)(2,1)}, u32[]{:S(2)}) copy-start(bf16[2,256,1024]{2,1,0:T(8,128)(2,1)} %all-gather.12.cloned.1.call-done) | copy-start | bytes 3145732
  394.7 327.9 %reduce-scatter.20.cloned.1.call-start = ((), (), s32[]{:S(2)}) async-start(), calls=%async_computation.22 | async-start | bytes 3538944 | tf_op jit(solution)/shard_map/reduce_scatter | solution.py:216
  464.2 1.2 copy-start.5
  464.2 1.3 copy-start.7
  464.2 325.4 %reduce-scatter.22.cloned.1.call-start = ((), (), s32[]{:S(2)}) async-start(), calls=%async_computation.24 | async-start | bytes 1179648 | tf_op jit(solution)/shard_map/reduce_scatter | solution.py:217
  466.9 371.1 %all-gather.32.cloned.1.call-start = ((), (), s32[]{:S(2)}) async-start(), calls=%async_computation.28 | async-start | bytes 2621440 | tf_op jit(solution)/shard_map/all_gather | solution.py:225
  552.7 331.3 %all-gather.30.cloned.1.call-start = ((), (), s32[]{:S(2)}) async-start(), calls=%async_computation.26 | async-start | bytes 2621440 | tf_op jit(solution)/shard_map/all_gather | solution.py:224
  644.3 273.1 %reduce-scatter.18.cloned.1.call-start = ((), (), s32[]{:S(2)}) async-start(), calls=%async_computation.21 | async-start | bytes 2621440 | tf_op jit(solution)/shard_map/reduce_scatter | solution.py:36
  648.1 269.4 %copy-start.14 = (f32[1024]{0:T(1024)S(1)}, f32[1024]{0:T(1024)}, u32[]{:S(2)}) copy-start(f32[1024]{0:T(1024)} %param.21) | copy-start | bytes 12292
  648.1 269.4 %copy-start.16 = (f32[2,64]{1,0:T(2,128)S(1)}, f32[2,64]{1,0:T(2,128)}, u32[]{:S(2)}) copy-start(f32[2,64]{1,0:T(2,128)} %copy-done.15) | copy-start | bytes 1540
  648.1 269.4 %copy-start.18 = (f32[2,64]{1,0:T(2,128)S(1)}, f32[2,64]{1,0:T(2,128)}, u32[]{:S(2)}) copy-start(f32[2,64]{1,0:T(2,128)} %copy-done.17) | copy-start | bytes 1540
  648.1 317.3 %all-gather.28.cloned.1.call-start = ((), (), s32[]{:S(2)}) async-start(), calls=%async_computation.23 | async-start | bytes 1966080 | tf_op jit(solution)/shard_map/all_gather | solution.py:222
  965.4 3.6 copy-start.2
  969.0 2.3 copy-start.1
Sparse Core Ops, SparseCore 0:
  9.6 29.8 all-gather.13
  41.6 16.7 all-gather.11
  62.3 46.2 all-gather.15
  121.9 29.6 reduce-scatter.9
  153.1 33.1 all-gather.19
  188.3 16.7 all-gather.17
  206.7 16.7 all-gather.23
  225.1 33.1 all-gather.21
  266.2 31.3 reduce-scatter.13
  300.0 31.4 reduce-scatter.11
  334.5 16.7 all-gather.25
  383.4 76.7 reduce-scatter.15
  463.8 88.8 reduce-scatter.25
  556.6 87.6 reduce-scatter.23
  647.7 74.7 reduce-scatter.19
  726.4 63.1 reduce-scatter.21
  791.1 46.8 all-gather.31
  839.5 44.4 all-gather.29
  887.3 30.1 reduce-scatter.17
  918.9 38.1 all-gather.27
where the time goes:
time: 981 us; the launch traced here: 980 us
  waiting for transfers between devices  783 us (80%)
  blocking collectives  70.3 us (7%)
  matrix products  55.7 us (6%)
  local copies, waits for them, and re-layouts  30.1 us (3%)
  other arithmetic  24.6 us (3%)
  between operations  14.6 us (1%)
    reduce_scatter x4, waiting for transfers between devices, parts_across(): lax.psum_scatter(partial_value, 'tp', scatter_dimension=1, tiled=True)  121 us
    reduce_scatter x1, waiting for transfers between devices, shards(): lax.psum_scatter(local_grads[2], ('dp', 'ctx'), scatter_dimension=0, tile...  91.5 us
    reduce_scatter x1, waiting for transfers between devices, shards(): lax.psum_scatter(local_grads[3], ('dp', 'ctx'), scatter_dimension=1, tile...  85.7 us
    reduce_scatter x1, waiting for transfers between devices, shards(): lax.psum_scatter(local_grads[0], ('dp', 'ctx'), scatter_dimension=0, tile...  74.4 us
    all_gather x4, waiting for transfers between devices, rows_across(): return lax.all_gather(block_rows, 'tp', axis=1, tiled=True)  68.4 us
    reduce_scatter x1, waiting for transfers between devices, shards(): lax.psum_scatter(local_grads[1], ('dp', 'ctx'), scatter_dimension=1, tile...  66.7 us
    reduce_scatter x1, waiting for transfers between devices, shards(): lax.psum_scatter(grad_pairs, 'ctx', scatter_dimension=1, tiled=True)  65.5 us
    all_gather x1, waiting for transfers between devices, shards(): lax.all_gather(grad_pieces[2], 'ctx', axis=0, tiled=True)  46 us
  transfers between devices with their start and end apart: 20, of which 19 were waited for; matrix products, arithmetic and copies ran while one was open for 4% of the time, Pallas kernels for 0%

commit v1 on v0

v1 whole, which is shorter than its diff:
```python
import jax
import jax.numpy as jnp
from jax import lax
from jax.experimental import pallas as pl
from jax.experimental.pallas import tpu as pltpu
from jax.sharding import PartitionSpec as P

HD = 64


EPSILON = 1e-05
F32 = jnp.float32
BF16 = jnp.bfloat16
SCALE = HD ** (-0.5)


def normalize(rows_in, gain_vec, bias_vec):
    row_mean = jnp.mean(rows_in, axis=-1, keepdims=True)
    centered = rows_in - row_mean
    spread = jnp.mean(centered * centered, axis=-1, keepdims=True)
    inverse = lax.rsqrt(spread + EPSILON)
    scaled = centered * inverse
    return (scaled * gain_vec + bias_vec, scaled, inverse)


def normalize_back(grad_rows, scaled, inverse, gain_vec):
    weighted = grad_rows * gain_vec
    centered = weighted - jnp.mean(weighted, axis=-1, keepdims=True)
    return (centered - scaled * jnp.mean(weighted * scaled, axis=-1, keepdims=True)) * inverse


def gelu_tanh(values_in):
    return jax.nn.gelu(values_in, approximate=True)


def shifted(value, axis_name, step):
    count = lax.axis_size(axis_name)
    return lax.ppermute(value, axis_name, [(i, (i + step) % count) for i in range(count)])


def turned(value, axis_name, axis):
    count = lax.axis_size(axis_name)
    return jnp.concatenate(
        [value] + [shifted(value, axis_name, count - k) for k in range(1, count)], axis=axis
    )


def turned_sum(partial_value, axis_name, axis):
    count = lax.axis_size(axis_name)
    pieces = jnp.split(partial_value, count, axis=axis)
    total = pieces[0]
    for k in range(1, count):
        total = total + shifted(pieces[k].astype(BF16), axis_name, k).astype(F32)
    return total


def rounded(value):
    return lax.reduce_precision(value, 8, 7).astype(BF16)


def sum_everywhere(value, axis_name, axis):
    count = lax.axis_size(axis_name)
    index = lax.axis_index(axis_name)
    size = value.shape[axis] // count

    def block_of(k):
        return lax.dynamic_slice_in_dim(value, lax.rem(index + k, count) * size, size, axis)

    total = block_of(0)
    for k in range(1, count):
        total = total + shifted(block_of(k).astype(BF16), axis_name, k).astype(F32)
    total = rounded(total)
    result = jnp.zeros(value.shape, F32)
    for k in range(count):
        piece = total if k == 0 else shifted(total, axis_name, count - k)
        result = lax.dynamic_update_slice_in_dim(
            result, piece.astype(F32), lax.rem(index + k, count) * size, axis
        )
    return result


def sum_small(value, axis_names):
    for axis_name in axis_names:
        count = lax.axis_size(axis_name)
        step = 1
        while step < count:
            value = value + lax.ppermute(
                value, axis_name, [(i, i ^ step) for i in range(count)]
            )
            step *= 2
    return value


def dot(a, b, contract):
    return lax.dot_general(a, b, (contract, ((), ())), preferred_element_type=F32)


def attend_kernel(q_ref, kv_ref, qpos_ref, qseg_ref, kpos_ref, kseg_ref, att_ref, log_ref):
    width = q_ref.shape[2]
    allowed = (kpos_ref[0] <= qpos_ref[0]) & (kseg_ref[0] == qseg_ref[0])
    for h in range(width // HD):
        cols = slice(h * HD, (h + 1) * HD)
        vcols = slice(width + h * HD, width + (h + 1) * HD)
        scores = dot(kv_ref[0, :, cols], q_ref[0, :, cols], ((1,), (1,))) * SCALE
        scores = jnp.where(allowed, scores, -1e30)
        highest = jnp.max(scores, axis=0, keepdims=True)
        exponent = jnp.exp(scores - highest)
        denominator = jnp.sum(exponent, axis=0, keepdims=True)
        probs = (exponent * (1.0 / denominator)).astype(BF16)
        att_ref[0, :, cols] = dot(probs, kv_ref[0, :, vcols], ((0,), (0,))).astype(BF16)
        log_ref[0, h : h + 1, :] = highest + jnp.log(denominator)


def attend_back_kernel(
    q_ref, kv_ref, ga_ref, log_ref, qpos_ref, qseg_ref, kpos_ref, kseg_ref, gq_ref, gkv_ref
):
    width = q_ref.shape[2]
    allowed = (kpos_ref[0] <= qpos_ref[0]) & (kseg_ref[0] == qseg_ref[0])
    for h in range(width // HD):
        cols = slice(h * HD, (h + 1) * HD)
        vcols = slice(width + h * HD, width + (h + 1) * HD)
        query = q_ref[0, :, cols]
        keys = kv_ref[0, :, cols]
        grad = ga_ref[0, :, cols]
        scores = dot(keys, query, ((1,), (1,))) * SCALE
        probs = jnp.exp(jnp.where(allowed, scores, -1e30) - log_ref[0, h : h + 1, :])
        grad_probs = dot(kv_ref[0, :, vcols], grad, ((1,), (1,)))
        inner = jnp.sum(probs * grad_probs, axis=0, keepdims=True)
        grad_scores = (probs * (grad_probs - inner)).astype(BF16)
        gq_ref[0, :, cols] = (dot(grad_scores, keys, ((0,), (0,))) * SCALE).astype(BF16)
        gkv_ref[0, :, cols] = (dot(grad_scores, query, ((1,), (0,))) * SCALE).astype(BF16)
        gkv_ref[0, :, vcols] = dot(probs.astype(BF16), grad, ((1,), (0,))).astype(BF16)


def per_sequence(kernel, outs, *operands):
    def spec(shape):
        return pl.BlockSpec((1,) + tuple(shape[1:]), lambda s: (s,) + (0,) * (len(shape) - 1))

    return pl.pallas_call(
        kernel,
        grid=(operands[0].shape[0],),
        in_specs=[spec(o.shape) for o in operands],
        out_specs=[spec(o.shape) for o in outs],
        out_shape=outs,
        compiler_params=pltpu.CompilerParams(vmem_limit_bytes=48 * 1024 * 1024),
        cost_estimate=pl.CostEstimate(flops=2 * 10**9, bytes_accessed=8 * 10**6, transcendentals=0),
    )(*operands)


def shards(
    tokens,
    segments,
    ln1_gain,
    ln1_bias,
    qkv_weight,
    qkv_bias,
    out_weight,
    out_bias,
    ln2_gain,
    ln2_bias,
    fc_weight,
    fc_bias,
    proj_weight,
    proj_bias,
    grad_out,
):
    seq_count, shard_len, model_width = tokens.shape
    tp_count, ctx_count, dp_count = (lax.axis_size(n) for n in ("tp", "ctx", "dp"))
    tp_index, ctx_index, dp_index = (lax.axis_index(n) for n in ("tp", "ctx", "dp"))
    block_len = shard_len * tp_count
    key_len = block_len * ctx_count
    width_tp = qkv_weight.shape[2]
    piece = model_width // dp_count
    own_rows = seq_count * shard_len

    def turn(value, back=False):
        if dp_count == 1:
            return value
        start = dp_index * piece
        if back:
            start = lax.rem(model_width - start, model_width)
        return lax.dynamic_slice_in_dim(
            jnp.concatenate([value, value], axis=-1), start, model_width, value.ndim - 1
        )

    residual_in = turn(tokens.reshape(own_rows, model_width)).astype(F32)
    grad_low = turn(grad_out.reshape(own_rows, model_width))
    ln1_gain, ln1_bias, out_bias, ln2_gain, ln2_bias, proj_bias = [
        turn(v) for v in (ln1_gain, ln1_bias, out_bias, ln2_gain, ln2_bias, proj_bias)
    ]

    normed_one, scaled_one, inverse_one = normalize(residual_in, ln1_gain, ln1_bias)
    attn_rows = turned(normed_one.astype(BF16), "tp", 0)
    qkv_flat = jnp.concatenate([qkv_weight[:, c] for c in range(3)], axis=1)
    qkv_full = turned(qkv_flat, "dp", 0)
    out_full = turned(out_weight, "dp", 1)
    fc_full = turned(fc_weight, "dp", 0)
    proj_full = turned(proj_weight, "dp", 1)
    grad_rows = turned(grad_low, "tp", 0)

    def by_sequence(rows):
        width = rows.shape[1]
        rows = rows.reshape(tp_count, seq_count, shard_len, width)
        return rows.transpose(1, 0, 2, 3).reshape(seq_count, block_len, width)

    def by_rows(rows):
        width = rows.shape[2]
        rows = rows.reshape(seq_count, tp_count, shard_len, width)
        return rows.transpose(1, 0, 2, 3).reshape(tp_count * own_rows, width)

    mixed = (dot(attn_rows, qkv_full, ((1,), (0,))) + qkv_bias.reshape(-1)).astype(BF16)
    mixed = by_sequence(mixed)
    queries = mixed[:, :, :width_tp]
    own_pairs = mixed[:, :, width_tp:]
    key_value = jnp.concatenate(
        [own_pairs]
        + [
            lax.ppermute(own_pairs, "ctx", [(i, i + k) for i in range(ctx_count - k)])
            for k in range(1, ctx_count)
        ],
        axis=1,
    )

    within = jnp.arange(shard_len, dtype=jnp.int32)
    block_of = lax.rem(jnp.arange(tp_count, dtype=jnp.int32) + tp_index, tp_count)
    own_order = (block_of[:, None] * shard_len + within[None, :]).reshape(-1)
    query_pos = ctx_index * block_len + own_order
    key_block = ctx_index - jnp.arange(ctx_count, dtype=jnp.int32)
    key_start = jnp.where(key_block >= 0, key_block, ctx_count) * block_len
    key_pos = (key_start[:, None] + own_order[None, :]).reshape(-1)
    key_seg = segments.reshape(seq_count, ctx_count, tp_count, shard_len)
    key_seg = lax.dynamic_slice_in_dim(
        jnp.concatenate([key_seg, key_seg], axis=2), tp_index, tp_count, 2
    )
    key_seg = key_seg[:, ::-1]
    key_seg = lax.dynamic_slice_in_dim(
        jnp.concatenate([key_seg, key_seg], axis=1), ctx_count - 1 - ctx_index, ctx_count, 1
    ).reshape(seq_count, key_len)
    query_seg = key_seg[:, :block_len]
    places = (
        jnp.broadcast_to(query_pos[None, None, :], (seq_count, 1, block_len)),
        query_seg[:, None, :],
        jnp.broadcast_to(key_pos[None, :, None], (seq_count, key_len, 1)),
        key_seg[:, :, None],
    )
    heads = width_tp // HD
    attended, log_totals = per_sequence(
        attend_kernel,
        [
            jax.ShapeDtypeStruct((seq_count, block_len, width_tp), BF16),
            jax.ShapeDtypeStruct((seq_count, heads, block_len), F32),
        ],
        queries,
        key_value,
        *places,
    )
    attended_flat = by_rows(attended)
    branch = turned_sum(dot(attended_flat, out_full, ((1,), (0,))), "tp", 0)
    middle = residual_in + branch + out_bias
    normed_two, scaled_two, inverse_two = normalize(middle, ln2_gain, ln2_bias)
    mlp_rows = turned(normed_two.astype(BF16), "tp", 0)
    upward = dot(mlp_rows, fc_full, ((1,), (0,))) + fc_bias
    hidden, gelu_back = jax.vjp(gelu_tanh, upward)
    hidden_low = hidden.astype(BF16)

    grad_hidden = dot(grad_rows, proj_full, ((1,), (1,)))
    grad_up = gelu_back(grad_hidden)[0].astype(BF16)
    fc_bias_part = jnp.sum(grad_up, axis=0, dtype=F32)
    grad_normed_two = turned_sum(dot(grad_up, fc_full, ((1,), (1,))), "tp", 0)
    mlp_out = turned_sum(dot(hidden_low, proj_full, ((1,), (0,))), "tp", 0)
    block_out = turn((middle + mlp_out + proj_bias).astype(BF16), True)

    def over_dp(full, axis):
        return turned_sum(full, "dp", axis)

    proj_grad = over_dp(dot(hidden_low, grad_rows, ((0,), (0,))), 1)
    fc_grad = over_dp(dot(mlp_rows, grad_up, ((0,), (0,))), 0)
    proj_weight_grad = sum_everywhere(proj_grad, "ctx", 0)
    fc_weight_grad = sum_everywhere(fc_grad, "ctx", 0)

    grad_top = grad_low.astype(F32)
    grad_middle = grad_top + normalize_back(grad_normed_two, scaled_two, inverse_two, ln2_gain)
    middle_rows = turned(grad_middle.astype(BF16), "tp", 0)
    grad_attended = by_sequence(dot(middle_rows, out_full, ((1,), (1,))).astype(BF16))
    out_grad = over_dp(dot(attended_flat, middle_rows, ((0,), (0,))), 1)
    out_weight_grad = sum_everywhere(out_grad, "ctx", 0)

    grad_queries, grad_pairs = per_sequence(
        attend_back_kernel,
        [
            jax.ShapeDtypeStruct((seq_count, block_len, width_tp), BF16),
            jax.ShapeDtypeStruct((seq_count, key_len, 2 * width_tp), BF16),
        ],
        queries,
        key_value,
        grad_attended,
        log_totals,
        *places,
    )

    def pair_block(k):
        return grad_pairs[:, k * block_len : (k + 1) * block_len]

    grad_pairs_own = pair_block(0).astype(F32)
    for k in range(1, ctx_count):
        grad_pairs_own = grad_pairs_own + lax.ppermute(
            pair_block(k), "ctx", [(i, i - k) for i in range(k, ctx_count)]
        ).astype(F32)
    grad_mixed = by_rows(
        jnp.concatenate([grad_queries, grad_pairs_own.astype(BF16)], axis=2)
    )
    qkv_bias_part = jnp.sum(grad_mixed, axis=0, dtype=F32)
    qkv_grad = over_dp(dot(attn_rows, grad_mixed, ((0,), (0,))), 0)
    qkv_grad = sum_everywhere(qkv_grad, "ctx", 0)
    qkv_weight_grad = jnp.stack(jnp.split(qkv_grad, 3, axis=1), axis=1)
    grad_normed_one = turned_sum(dot(grad_mixed, qkv_full, ((1,), (1,))), "tp", 0)
    tokens_grad = grad_middle + normalize_back(grad_normed_one, scaled_one, inverse_one, ln1_gain)

    shared = jnp.stack(
        [
            jnp.sum(grad_normed_one * scaled_one, axis=0),
            jnp.sum(grad_normed_one, axis=0),
            jnp.sum(grad_middle, axis=0),
            jnp.sum(grad_normed_two * scaled_two, axis=0),
            jnp.sum(grad_normed_two, axis=0),
            jnp.sum(grad_top, axis=0),
        ]
    )
    shared = sum_small(turn(shared, True), ("dp", "ctx", "tp"))
    split_biases = sum_small(jnp.concatenate([qkv_bias_part, fc_bias_part]), ("dp", "ctx"))
    qkv_bias_grad = split_biases[: 3 * width_tp].reshape(3, width_tp)
    fc_bias_grad = split_biases[3 * width_tp :]
    ln1_gain_grad, ln1_bias_grad, out_bias_grad, ln2_gain_grad, ln2_bias_grad, proj_bias_grad = [
        shared[i] for i in range(6)
    ]
    return (
        block_out.reshape(tokens.shape),
        turn(tokens_grad, True).reshape(tokens.shape),
        ln1_gain_grad,
        ln1_bias_grad,
        qkv_weight_grad,
        qkv_bias_grad,
        out_weight_grad,
        out_bias_grad,
        ln2_gain_grad,
        ln2_bias_grad,
        fc_weight_grad,
        fc_bias_grad,
        proj_weight_grad,
        proj_bias_grad,
    )


def solution(mesh):
    placed = (
        P("dp", ("ctx", "tp"), None),
        P("dp", None),
        P(),
        P(),
        P("dp", None, "tp"),
        P(None, "tp"),
        P("tp", "dp"),
        P(),
        P(),
        P(),
        P("dp", "tp"),
        P("tp"),
        P("tp", "dp"),
        P(),
        P("dp", ("ctx", "tp"), None),
    )
    return jax.shard_map(
        shards,
        mesh=mesh,
        in_specs=placed,
        out_specs=(
            P("dp", ("ctx", "tp"), None),
            P("dp", ("ctx", "tp"), None),
            P(),
            P(),
            P("dp", None, "tp"),
            P(None, "tp"),
            P("tp", "dp"),
            P(),
            P(),
            P(),
            P("dp", "tp"),
            P("tp"),
            P("tp", "dp"),
            P(),
        ),
        check_vma=False,
    )
```

time: 981 us -> 440 us (0.45)
  waiting for transfers between devices: 783 us -> 221 us
  starting transfers between devices: 1.21 us -> 136 us
  blocking collectives: 70.3 us -> 0 us
  matrix products: 55.7 us -> 21.1 us
  Pallas kernels: 0 us -> 16 us
  between operations: 14.6 us -> 1.89 us
    reduce_scatter x9 -> x0, waiting for transfers between devices: 505 us -> none  [the longest x4 121 us: parts_across(): lax.psum_scatter(partial_value, 'tp', scatter_dimension=1, tiled=True)]
    all_gather x11 -> x0, waiting for transfers between devices: 275 us -> none  [the longest x4 68.4 us: rows_across(): return lax.all_gather(block_rows, 'tp', axis=1, tiled=True)]
    ppermute x0 -> x70, waiting for transfers between devices: none -> 221 us  [the longest x56 168 us: shifted(): lax.ppermute(value, axis_name, [(i, (i + step) % count) for i in range(co...]
    ppermute x0 -> x70, starting transfers between devices: none -> 136 us  [the longest x56 114 us: shifted(): lax.ppermute(value, axis_name, [(i, (i + step) % count) for i in range(co...]
    psum x1 -> x0, blocking collectives: 43.3 us -> none  [shards(): lax.psum((jnp.sum(grad_normed_one * scaled_one, axis=(0, 1)), jnp.sum(gra...]
    dot_general x26 -> x12, matrix products: 55.7 us -> 21.1 us  [dot(): lax.dot_general(a, b, (contract, ((), ())), preferred_element_type=F32)]
    all_gather x2 -> x0, blocking collectives: 26.9 us -> none  [the longest x1 17.8 us: shards(): lax.all_gather(grad_pieces[1], 'ctx', axis=1, tiled=True)]
    pallas_call x0 -> x2, Pallas kernels: none -> 16 us  [per_sequence(): pl.pallas_call(kernel, grid=(operands[0].shape[0],), in_specs=[spec(o.sha...]
  transfers between devices with their start and end apart: 20 -> 70, of which waited for: 19 -> 38; matrix products, arithmetic and copies ran while one was open for 4% -> 12% of each run, Pallas kernels for 0% -> 4%
where the time goes in v1:
time: 440 us; the launch traced here: 439 us
  waiting for transfers between devices  221 us (50%)
  starting transfers between devices  136 us (31%)
  local copies, waits for them, and re-layouts  23 us (5%)
  matrix products  21.1 us (5%)
  other arithmetic  20.1 us (5%)
  Pallas kernels  16 us (4%)
    ppermute x56, waiting for transfers between devices, shifted(): lax.ppermute(value, axis_name, [(i, (i + step) % count) for i in range(co...  168 us
    ppermute x56, starting transfers between devices, shifted(): lax.ppermute(value, axis_name, [(i, (i + step) % count) for i in range(co...  114 us
    ppermute x8, waiting for transfers between devices, sum_small(): lax.ppermute(value, axis_name, [(i, i ^ step) for i in range(count)])  32.1 us
    dot_general x12, matrix products, dot(): lax.dot_general(a, b, (contract, ((), ())), preferred_element_type=F32)  21.1 us
    ppermute x3, waiting for transfers between devices, shards(): lax.ppermute(own_pairs, 'ctx', [(i, i + k) for i in range(ctx_count - k)])  20.8 us
    pallas_call x2, Pallas kernels, per_sequence(): pl.pallas_call(kernel, grid=(operands[0].shape[0],), in_specs=[spec(o.sha...  16 us
    ppermute x3, starting transfers between devices, shards(): lax.ppermute(own_pairs, 'ctx', [(i, i + k) for i in range(ctx_count - k)])  10.9 us
  transfers between devices with their start and end apart: 70, of which 38 were waited for; matrix products, arithmetic and copies ran while one was open for 12% of the time, Pallas kernels for 4%

profile of v1, /device:TPU:0, one launch (start us, length us, event | category | flops | bytes accessed | tf_op | source)
XLA Modules:
  0.0 439.1 jit_solution(3655576625290118829)
XLA Ops:
  3.7 2.6 collective-permute-start.1
  11.2 2.3 constant_dynamic-update-slice_fusion.3
  15.3 2.6 collective-permute-done
  17.9 11.7 %collective-permute-done.3 = bf16[512,768]{1,0:T(8,128)(2,1)} collective-permute-done((bf16[512,768]{1,0:T(8,128)(2,1)S(1)}, bf16[512,768]{1,0:T(8,128)(2,1)}, u32[]{:S(2)}, u32[]{:S(2)}) %collective-permute-start.3) | collective-permute-done | bytes 786464 | tf_op jit(solution)/shard_map/ppermute | solution.py:38
  29.6 2.2 add_convert_fusion
  32.0 6.3 %collective-permute-start.6 = (bf16[2,256,512]{2,1,0:T(8,128)(2,1)S(1)}, bf16[2,256,512]{2,1,0:T(8,128)(2,1)}, u32[]{:S(2)}, u32[]{:S(2)}) collective-permute-start(bf16[2,256,512]{2,1,0:T(8,128)(2,1)S(1)} %slice.84), channel_id=1, source_target_pairs={{0,12},{1,13},{2,14},{3,15},{16,28},{17,29},{18,30},{19,31}} | collective-permute-start | bytes 1572872 | tf_op jit(solution)/shard_map/ppermute | solution.py:218
  38.3 2.1 collective-permute-start.5
  40.4 2.5 collective-permute-start.4
  46.8 3.1 collective-permute-done.6
  49.8 11.2 %collective-permute-done.5 = bf16[2,256,512]{2,1,0:T(8,128)(2,1)} collective-permute-done((bf16[2,256,512]{2,1,0:T(8,128)(2,1)S(1)}, bf16[2,256,512]{2,1,0:T(8,128)(2,1)}, u32[]{:S(2)}, u32[]{:S(2)}) %collective-permute-start.5) | collective-permute-done | bytes 524320 | tf_op jit(solution)/shard_map/ppermute | solution.py:218
  61.1 6.5 %collective-permute-done.4 = bf16[2,256,512]{2,1,0:T(8,128)(2,1)} collective-permute-done((bf16[2,256,512]{2,1,0:T(8,128)(2,1)S(1)}, bf16[2,256,512]{2,1,0:T(8,128)(2,1)}, u32[]{:S(2)}, u32[]{:S(2)}) %collective-permute-start.4) | collective-permute-done | bytes 524320 | tf_op jit(solution)/shard_map/ppermute | solution.py:218
  69.5 6.0 %shard_map.254 = (bf16[2,256,256]{2,1,0:T(8,128)(2,1)S(1)}, f32[2,4,256]{2,1,0:T(4,128)S(1)}) custom-call(bf16[2,256,256]{2,1,0:T(8,128)(2,1)S(1)} %slice.83.q_ref, bf16[2,1024,512]{2,1,0:T(8,128)(2,1)S(1)} %pad_maximum_fusion.kv_ref, s32[2,1,256]{2,1,0:T(1,128)S(1)} %broadcast_in_dim.16.qpos_ref, s32[2,1,256]{2,1,0:T(1,128)S(1)} %broadcast_in_dim.17.qseg_ref, ...), custom_call_target="tpu_custom_call" | custom-call | flops 2000000000 | bytes 8000000 | tf_op jit(solution)/shard_map/pallas_call | solution.py:139
  78.3 2.1 collective-permute-start.9
  83.6 4.2 collective-permute-start.21
  87.8 5.5 %collective-permute-done.9 = bf16[128,1024]{1,0:T(8,128)(2,1)S(1)} collective-permute-done((bf16[128,1024]{1,0:T(8,128)(2,1)}, bf16[128,1024]{1,0:T(8,128)(2,1)S(1)}, u32[]{:S(2)}, u32[]{:S(2)}) %collective-permute-start.9) | collective-permute-done | bytes 262176 | tf_op jit(solution)/shard_map/ppermute | solution.py:38
  98.2 1.8 collective-permute-start.20
  104.3 3.2 collective-permute-done.11
  110.3 4.6 %collective-permute-done.20 = bf16[128,1024]{1,0:T(8,128)(2,1)S(1)} collective-permute-done((bf16[128,1024]{1,0:T(8,128)(2,1)S(1)}, bf16[128,1024]{1,0:T(8,128)(2,1)S(1)}, u32[]{:S(2)}, u32[]{:S(2)}) %collective-permute-start.20) | collective-permute-done | bytes 262176 | tf_op jit(solution)/shard_map/ppermute | solution.py:38
  115.2 3.7 convert_reduce_fusion
  120.3 2.0 collective-permute-start.24
  122.3 2.1 collective-permute-start.23
  124.4 1.8 collective-permute-start.18
  129.0 2.6 collective-permute-start.16
  131.6 5.5 %collective-permute-done.23 = bf16[128,1024]{1,0:T(8,128)(2,1)S(1)} collective-permute-done((bf16[128,1024]{1,0:T(8,128)(2,1)S(1)}, bf16[128,1024]{1,0:T(8,128)(2,1)S(1)}, u32[]{:S(2)}, u32[]{:S(2)}) %collective-permute-start.23) | collective-permute-done | bytes 262176 | tf_op jit(solution)/shard_map/ppermute | solution.py:38
  140.2 7.7 %collective-permute-done.17 = bf16[128,1024]{1,0:T(8,128)(2,1)S(1)} collective-permute-done((bf16[128,1024]{1,0:T(8,128)(2,1)S(1)}, bf16[128,1024]{1,0:T(8,128)(2,1)S(1)}, u32[]{:S(2)}, u32[]{:S(2)}) %collective-permute-start.17) | collective-permute-done | bytes 262176 | tf_op jit(solution)/shard_map/ppermute | solution.py:38
  153.1 3.3 collective-permute-done.27
  157.6 2.8 collective-permute-done.25
  163.9 5.2 %collective-permute-done.49 = bf16[256,512]{1,0:T(8,128)(2,1)S(1)} collective-permute-done((bf16[256,512]{1,0:T(8,128)(2,1)S(1)}, bf16[256,512]{1,0:T(8,128)(2,1)S(1)}, u32[]{:S(2)}, u32[]{:S(2)}) %collective-permute-start.49) | collective-permute-done | bytes 262176 | tf_op jit(solution)/shard_map/ppermute | solution.py:38
  169.2 6.6 %collective-permute-start.52 = (bf16[64,512]{1,0:T(8,128)(2,1)S(1)}, bf16[64,512]{1,0:T(8,128)(2,1)S(1)}, u32[]{:S(2)}, u32[]{:S(2)}) collective-permute-start(bf16[64,512]{1,0:T(8,128)(2,1)S(1)} %get-tuple-element.79), channel_id=1, source_target_pairs={{0,12},{4,0},{8,4},{12,8},{1,13},{5,1},{9,5},{13,9},{2,14},{6,2},{... | collective-permute-start | bytes 196616 | tf_op jit(solution)/shard_map/ppermute | solution.py:38
  175.8 10.3 %collective-permute-start.51 = (bf16[64,512]{1,0:T(8,128)(2,1)S(1)}, bf16[64,512]{1,0:T(8,128)(2,1)S(1)}, u32[]{:S(2)}, u32[]{:S(2)}) collective-permute-start(bf16[64,512]{1,0:T(8,128)(2,1)S(1)} %get-tuple-element.80), channel_id=1, source_target_pairs={{0,8},{4,12},{8,0},{12,4},{1,9},{5,13},{9,1},{13,5},{2,10},{6,14},... | collective-permute-start | bytes 196616 | tf_op jit(solution)/shard_map/ppermute | solution.py:38
  186.1 1.9 collective-permute-start.50
  188.1 10.1 %shard_map.255 = (bf16[2,256,256]{2,1,0:T(8,128)(2,1)S(1)}, bf16[2,1024,512]{2,1,0:T(8,128)(2,1)S(1)}) custom-call(bf16[2,256,256]{2,1,0:T(8,128)(2,1)S(1)} %slice.83.q_ref, bf16[2,1024,512]{2,1,0:T(8,128)(2,1)} %copy-done, bf16[2,256,256]{2,1,0:T(8,128)(2,1)S(1)} %bitcast.60, f32[2,4,256]{2,1,0:T(4,128)S(1)} %get-tuple-element.19.log_ref, ...), custom_call_target="tpu_custom_call" | custom-call | flops 2000000000 | bytes 8000000 | tf_op jit(solution)/shard_map/pallas_call | solution.py:139
  198.3 1.9 collective-permute-start.53
  204.3 4.3 collective-permute-start.54
  208.6 44.8 %collective-permute-done.54 = bf16[64,512]{1,0:T(8,128)(2,1)S(1)} collective-permute-done((bf16[64,512]{1,0:T(8,128)(2,1)S(1)}, bf16[64,512]{1,0:T(8,128)(2,1)S(1)}, u32[]{:S(2)}, u32[]{:S(2)}) %collective-permute-start.54) | collective-permute-done | bytes 65568 | tf_op jit(solution)/shard_map/ppermute | solution.py:38
  253.5 6.0 %collective-permute-done.55 = bf16[64,512]{1,0:T(8,128)(2,1)S(1)} collective-permute-done((bf16[64,512]{1,0:T(8,128)(2,1)S(1)}, bf16[64,512]{1,0:T(8,128)(2,1)S(1)}, u32[]{:S(2)}, u32[]{:S(2)}) %collective-permute-start.55) | collective-permute-done | bytes 65568 | tf_op jit(solution)/shard_map/ppermute | solution.py:38
  263.3 3.5 fusion.83
  268.6 2.0 fusion.42
  272.4 1.9 slice_add_fusion.1
  274.3 11.5 %collective-permute-done.63 = bf16[1024,512]{1,0:T(8,128)(2,1)S(1)} collective-permute-done((bf16[1024,512]{1,0:T(8,128)(2,1)}, bf16[1024,512]{1,0:T(8,128)(2,1)S(1)}, u32[]{:S(2)}, u32[]{:S(2)}) %collective-permute-start.63) | collective-permute-done | bytes 1048608 | tf_op jit(solution)/shard_map/ppermute | solution.py:38
  287.7 13.0 %collective-permute-done.46 = f32[1792]{0:T(1024)S(1)} collective-permute-done((f32[1792]{0:T(1024)S(1)}, f32[1792]{0:T(1024)S(1)}, u32[]{:S(2)}, u32[]{:S(2)}) %collective-permute-start.46) | collective-permute-done | bytes 7200 | tf_op jit(solution)/shard_map/ppermute | solution.py:87
  301.7 2.6 collective-permute-done.47
  305.3 3.8 collective-permute-done.48
  316.5 2.4 collective-permute-done.34
  320.6 3.7 collective-permute-done.35
  324.3 2.2 collective-permute-start.36
  327.3 3.9 collective-permute-done.36
  331.2 2.3 collective-permute-start.66
  336.0 3.4 collective-permute-start.60
  341.3 15.4 %collective-permute-done.65 = bf16[256,512]{1,0:T(8,128)(2,1)S(1)} collective-permute-done((bf16[256,512]{1,0:T(8,128)(2,1)S(1)}, bf16[256,512]{1,0:T(8,128)(2,1)S(1)}, u32[]{:S(2)}, u32[]{:S(2)}) %collective-permute-start.65) | collective-permute-done | bytes 262176 | tf_op jit(solution)/shard_map/ppermute | solution.py:38
  357.9 2.8 collective-permute-done.38
  360.6 3.8 collective-permute-start.67
  365.1 11.4 %collective-permute-start.68 = (bf16[256,512]{1,0:T(8,128)(2,1)S(1)}, bf16[256,512]{1,0:T(8,128)(2,1)S(1)}, u32[]{:S(2)}, u32[]{:S(2)}) collective-permute-start(bf16[256,512]{1,0:T(8,128)(2,1)S(1)} %get-tuple-element.31), channel_id=1, source_target_pairs={{0,8},{4,12},{8,0},{12,4},{1,9},{5,13},{9,1},{13,5},{2,10},{6,14},... | collective-permute-start | bytes 786440 | tf_op jit(solution)/shard_map/ppermute | solution.py:38
  376.5 5.1 %collective-permute-done.61 = bf16[128,1024]{1,0:T(8,128)(2,1)S(1)} collective-permute-done((bf16[128,1024]{1,0:T(8,128)(2,1)S(1)}, bf16[128,1024]{1,0:T(8,128)(2,1)S(1)}, u32[]{:S(2)}, u32[]{:S(2)}) %collective-permute-start.61) | collective-permute-done | bytes 262176 | tf_op jit(solution)/shard_map/ppermute | solution.py:38
  381.6 4.0 collective-permute-start.69
  385.9 1.9 slice_add_fusion.2
  387.9 2.9 collective-permute-start.42
  390.8 11.0 %collective-permute-start.41 = (bf16[128,768]{1,0:T(8,128)(2,1)S(1)}, bf16[128,768]{1,0:T(8,128)(2,1)S(1)}, u32[]{:S(2)}, u32[]{:S(2)}) collective-permute-start(bf16[128,768]{1,0:T(8,128)(2,1)S(1)} %get-tuple-element.62), channel_id=1, source_target_pairs={{0,8},{4,12},{8,0},{12,4},{1,9},{5,13},{9,1},{13,5},{2,10},{6,14},... | collective-permute-start | bytes 589832 | tf_op jit(solution)/shard_map/ppermute | solution.py:38
  401.8 1.9 collective-permute-start.40
  403.8 1.8 collective-permute-done.68
  405.7 11.3 %collective-permute-done.41 = bf16[128,768]{1,0:T(8,128)(2,1)S(1)} collective-permute-done((bf16[128,768]{1,0:T(8,128)(2,1)S(1)}, bf16[128,768]{1,0:T(8,128)(2,1)S(1)}, u32[]{:S(2)}, u32[]{:S(2)}) %collective-permute-start.41) | collective-permute-done | bytes 196640 | tf_op jit(solution)/shard_map/ppermute | solution.py:38
  418.4 4.6 %collective-permute-start.44 = (bf16[128,768]{1,0:T(8,128)(2,1)S(1)}, bf16[128,768]{1,0:T(8,128)(2,1)S(1)}, u32[]{:S(2)}, u32[]{:S(2)}) collective-permute-start(bf16[128,768]{1,0:T(8,128)(2,1)S(1)} %get-tuple-element.37), channel_id=1, source_target_pairs={{0,8},{4,12},{8,0},{12,4},{1,9},{5,13},{9,1},{13,5},{2,10},{6,14},... | collective-permute-start | bytes 589832 | tf_op jit(solution)/shard_map/ppermute | solution.py:38
  423.0 2.0 collective-permute-start.45
  425.8 11.8 %collective-permute-done.44 = bf16[128,768]{1,0:T(8,128)(2,1)S(1)} collective-permute-done((bf16[128,768]{1,0:T(8,128)(2,1)S(1)}, bf16[128,768]{1,0:T(8,128)(2,1)S(1)}, u32[]{:S(2)}, u32[]{:S(2)}) %collective-permute-start.44) | collective-permute-done | bytes 196640 | tf_op jit(solution)/shard_map/ppermute | solution.py:38
  (293 shorter events, 86.2 us)
Async XLA Ops:
  3.2 10.6 %collective-permute-start.2 = (bf16[128,1024]{1,0:T(8,128)(2,1)S(1)}, bf16[128,1024]{1,0:T(8,128)(2,1)S(1)}, u32[]{:S(2)}, u32[]{:S(2)}) collective-permute-start(bf16[128,1024]{1,0:T(8,128)(2,1)S(1)} %fusion.14), channel_id=1, source_target_pairs={{0,1},{1,2},{2,3},{3,0},{4,5},{5,6},{6,7},{7,4},{8,9},{9,10},{10,1... | collective-permute-start | bytes 786440 | tf_op jit(solution)/shard_map/ppermute | solution.py:38
  3.7 11.6 %collective-permute-start.1 = (bf16[128,1024]{1,0:T(8,128)(2,1)S(1)}, bf16[128,1024]{1,0:T(8,128)(2,1)S(1)}, u32[]{:S(2)}, u32[]{:S(2)}) collective-permute-start(bf16[128,1024]{1,0:T(8,128)(2,1)S(1)} %fusion.14), channel_id=1, source_target_pairs={{0,2},{1,3},{2,0},{3,1},{4,6},{5,7},{6,4},{7,5},{8,10},{9,11},{10,... | collective-permute-start | bytes 786440 | tf_op jit(solution)/shard_map/ppermute | solution.py:38
  6.2 11.7 %collective-permute-start = (bf16[128,1024]{1,0:T(8,128)(2,1)S(1)}, bf16[128,1024]{1,0:T(8,128)(2,1)}, u32[]{:S(2)}, u32[]{:S(2)}) collective-permute-start(bf16[128,1024]{1,0:T(8,128)(2,1)S(1)} %fusion.14), channel_id=1, source_target_pairs={{0,3},{1,0},{2,1},{3,2},{4,7},{5,4},{6,5},{7,6},{8,11},{9,8},{10,9... | collective-permute-start | bytes 786440 | tf_op jit(solution)/shard_map/ppermute | solution.py:38
  8.9 20.7 %collective-permute-start.3 = (bf16[512,768]{1,0:T(8,128)(2,1)S(1)}, bf16[512,768]{1,0:T(8,128)(2,1)}, u32[]{:S(2)}, u32[]{:S(2)}) collective-permute-start(bf16[512,768]{1,0:T(8,128)(2,1)S(1)} %pad_maximum_fusion.7), channel_id=1, source_target_pairs={{0,16},{16,0},{1,17},{17,1},{2,18},{18,2},{3,19},{19,3},{4,20},{20... | collective-permute-start | bytes 2359304 | tf_op jit(solution)/shard_map/ppermute | solution.py:38
  10.5 33.7 %collective-permute-start.7 = (bf16[256,512]{1,0:T(8,128)(2,1)S(1)}, bf16[256,512]{1,0:T(8,128)(2,1)}, u32[]{:S(2)}, u32[]{:S(2)}) collective-permute-start(bf16[256,512]{1,0:T(8,128)(2,1)S(1)} %copy-done.30), channel_id=1, source_target_pairs={{0,16},{16,0},{1,17},{17,1},{2,18},{18,2},{3,19},{19,3},{4,20},{20... | collective-permute-start | bytes 786440 | tf_op jit(solution)/shard_map/ppermute | solution.py:38
  13.7 81.4 %collective-permute-start.14 = (bf16[512,1024]{1,0:T(8,128)(2,1)}, bf16[512,1024]{1,0:T(8,128)(2,1)}, u32[]{:S(2)}, u32[]{:S(2)}) collective-permute-start(bf16[512,1024]{1,0:T(8,128)(2,1)} %param.25), channel_id=1, source_target_pairs={{0,16},{16,0},{1,17},{17,1},{2,18},{18,2},{3,19},{19,3},{4,20},{20... | collective-permute-start | bytes 3145736 | tf_op jit(solution)/shard_map/ppermute | solution.py:38
  32.0 17.9 %collective-permute-start.6 = (bf16[2,256,512]{2,1,0:T(8,128)(2,1)S(1)}, bf16[2,256,512]{2,1,0:T(8,128)(2,1)}, u32[]{:S(2)}, u32[]{:S(2)}) collective-permute-start(bf16[2,256,512]{2,1,0:T(8,128)(2,1)S(1)} %slice.84), channel_id=1, source_target_pairs={{0,12},{1,13},{2,14},{3,15},{16,28},{17,29},{18,30},{19,31}} | collective-permute-start | bytes 1572872 | tf_op jit(solution)/shard_map/ppermute | solution.py:218
  38.3 22.8 %collective-permute-start.5 = (bf16[2,256,512]{2,1,0:T(8,128)(2,1)S(1)}, bf16[2,256,512]{2,1,0:T(8,128)(2,1)}, u32[]{:S(2)}, u32[]{:S(2)}) collective-permute-start(bf16[2,256,512]{2,1,0:T(8,128)(2,1)S(1)} %slice.84), channel_id=1, source_target_pairs={{0,8},{4,12},{1,9},{5,13},{2,10},{6,14},{3,11},{7,15},{16,24},{20,... | collective-permute-start | bytes 1572872 | tf_op jit(solution)/shard_map/ppermute | solution.py:218
  40.4 27.3 %collective-permute-start.4 = (bf16[2,256,512]{2,1,0:T(8,128)(2,1)S(1)}, bf16[2,256,512]{2,1,0:T(8,128)(2,1)}, u32[]{:S(2)}, u32[]{:S(2)}) collective-permute-start(bf16[2,256,512]{2,1,0:T(8,128)(2,1)S(1)} %slice.84), channel_id=1, source_target_pairs={{0,4},{4,8},{8,12},{1,5},{5,9},{9,13},{2,6},{6,10},{10,14},{3,7},{... | collective-permute-start | bytes 1572872 | tf_op jit(solution)/shard_map/ppermute | solution.py:218
  44.2 54.0 %collective-permute-start.15 = (bf16[1024,512]{1,0:T(8,128)(2,1)}, bf16[1024,512]{1,0:T(8,128)(2,1)}, u32[]{:S(2)}, u32[]{:S(2)}) collective-permute-start(bf16[1024,512]{1,0:T(8,128)(2,1)} %param.27), channel_id=1, source_target_pairs={{0,16},{16,0},{1,17},{17,1},{2,18},{18,2},{3,19},{19,3},{4,20},{20... | collective-permute-start | bytes 3145736 | tf_op jit(solution)/shard_map/ppermute | solution.py:38
  78.3 15.1 %collective-permute-start.9 = (bf16[128,1024]{1,0:T(8,128)(2,1)}, bf16[128,1024]{1,0:T(8,128)(2,1)S(1)}, u32[]{:S(2)}, u32[]{:S(2)}) collective-permute-start(bf16[128,1024]{1,0:T(8,128)(2,1)} %get-tuple-element.74), channel_id=1, source_target_pairs={{0,2},{1,3},{2,0},{3,1},{4,6},{5,7},{6,4},{7,5},{8,10},{9,11},{10,... | collective-permute-start | bytes 786440 | tf_op jit(solution)/shard_map/ppermute | solution.py:38
  80.4 13.0 %collective-permute-start.8 = (bf16[128,1024]{1,0:T(8,128)(2,1)}, bf16[128,1024]{1,0:T(8,128)(2,1)S(1)}, u32[]{:S(2)}, u32[]{:S(2)}) collective-permute-start(bf16[128,1024]{1,0:T(8,128)(2,1)} %get-tuple-element.72), channel_id=1, source_target_pairs={{0,1},{1,2},{2,3},{3,0},{4,5},{5,6},{6,7},{7,4},{8,9},{9,10},{10,1... | collective-permute-start | bytes 786440 | tf_op jit(solution)/shard_map/ppermute | solution.py:38
  83.6 26.7 %collective-permute-start.21 = (bf16[128,1024]{1,0:T(8,128)(2,1)S(1)}, bf16[128,1024]{1,0:T(8,128)(2,1)S(1)}, u32[]{:S(2)}, u32[]{:S(2)}) collective-permute-start(bf16[128,1024]{1,0:T(8,128)(2,1)S(1)} %get-tuple-element.39), channel_id=1, source_target_pairs={{0,1},{1,2},{2,3},{3,0},{4,5},{5,6},{6,7},{7,4},{8,9},{9,10},{10,1... | collective-permute-start | bytes 786440 | tf_op jit(solution)/shard_map/ppermute | solution.py:38
  95.0 8.0 %collective-permute-start.13 = (bf16[128,1024]{1,0:T(8,128)(2,1)S(1)}, bf16[128,1024]{1,0:T(8,128)(2,1)S(1)}, u32[]{:S(2)}, u32[]{:S(2)}) collective-permute-start(bf16[128,1024]{1,0:T(8,128)(2,1)S(1)} %add_convert_fusion.2), channel_id=1, source_target_pairs={{0,1},{1,2},{2,3},{3,0},{4,5},{5,6},{6,7},{7,4},{8,9},{9,10},{10,1... | collective-permute-start | bytes 786440 | tf_op jit(solution)/shard_map/ppermute | solution.py:38
  95.1 9.2 %collective-permute-start.12 = (bf16[128,1024]{1,0:T(8,128)(2,1)S(1)}, bf16[128,1024]{1,0:T(8,128)(2,1)S(1)}, u32[]{:S(2)}, u32[]{:S(2)}) collective-permute-start(bf16[128,1024]{1,0:T(8,128)(2,1)S(1)} %add_convert_fusion.2), channel_id=1, source_target_pairs={{0,2},{1,3},{2,0},{3,1},{4,6},{5,7},{6,4},{7,5},{8,10},{9,11},{10,... | collective-permute-start | bytes 786440 | tf_op jit(solution)/shard_map/ppermute | solution.py:38
  95.2 12.3 %collective-permute-start.11 = (bf16[128,1024]{1,0:T(8,128)(2,1)S(1)}, bf16[128,1024]{1,0:T(8,128)(2,1)S(1)}, u32[]{:S(2)}, u32[]{:S(2)}) collective-permute-start(bf16[128,1024]{1,0:T(8,128)(2,1)S(1)} %add_convert_fusion.2), channel_id=1, source_target_pairs={{0,3},{1,0},{2,1},{3,2},{4,7},{5,4},{6,5},{7,6},{8,11},{9,8},{10,9... | collective-permute-start | bytes 786440 | tf_op jit(solution)/shard_map/ppermute | solution.py:38
  98.2 16.8 %collective-permute-start.20 = (bf16[128,1024]{1,0:T(8,128)(2,1)S(1)}, bf16[128,1024]{1,0:T(8,128)(2,1)S(1)}, u32[]{:S(2)}, u32[]{:S(2)}) collective-permute-start(bf16[128,1024]{1,0:T(8,128)(2,1)S(1)} %get-tuple-element.39), channel_id=1, source_target_pairs={{0,2},{1,3},{2,0},{3,1},{4,6},{5,7},{6,4},{7,5},{8,10},{9,11},{10,... | collective-permute-start | bytes 786440 | tf_op jit(solution)/shard_map/ppermute | solution.py:38
  103.1 12.1 %collective-permute-start.19 = (bf16[128,1024]{1,0:T(8,128)(2,1)S(1)}, bf16[128,1024]{1,0:T(8,128)(2,1)S(1)}, u32[]{:S(2)}, u32[]{:S(2)}) collective-permute-start(bf16[128,1024]{1,0:T(8,128)(2,1)S(1)} %get-tuple-element.39), channel_id=1, source_target_pairs={{0,3},{1,0},{2,1},{3,2},{4,7},{5,4},{6,5},{7,6},{8,11},{9,8},{10,9... | collective-permute-start | bytes 786440 | tf_op jit(solution)/shard_map/ppermute | solution.py:38
  120.3 8.7 %collective-permute-start.24 = (bf16[128,1024]{1,0:T(8,128)(2,1)S(1)}, bf16[128,1024]{1,0:T(8,128)(2,1)S(1)}, u32[]{:S(2)}, u32[]{:S(2)}) collective-permute-start(bf16[128,1024]{1,0:T(8,128)(2,1)S(1)} %get-tuple-element.67), channel_id=1, source_target_pairs={{0,3},{1,0},{2,1},{3,2},{4,7},{5,4},{6,5},{7,6},{8,11},{9,8},{10,9... | collective-permute-start | bytes 786440 | tf_op jit(solution)/shard_map/ppermute | solution.py:38
  122.3 14.8 %collective-permute-start.23 = (bf16[128,1024]{1,0:T(8,128)(2,1)S(1)}, bf16[128,1024]{1,0:T(8,128)(2,1)S(1)}, u32[]{:S(2)}, u32[]{:S(2)}) collective-permute-start(bf16[128,1024]{1,0:T(8,128)(2,1)S(1)} %get-tuple-element.68), channel_id=1, source_target_pairs={{0,2},{1,3},{2,0},{3,1},{4,6},{5,7},{6,4},{7,5},{8,10},{9,11},{10,... | collective-permute-start | bytes 786440 | tf_op jit(solution)/shard_map/ppermute | solution.py:38
  124.4 14.2 %collective-permute-start.22 = (bf16[128,1024]{1,0:T(8,128)(2,1)S(1)}, bf16[128,1024]{1,0:T(8,128)(2,1)S(1)}, u32[]{:S(2)}, u32[]{:S(2)}) collective-permute-start(bf16[128,1024]{1,0:T(8,128)(2,1)S(1)} %get-tuple-element.66), channel_id=1, source_target_pairs={{0,1},{1,2},{2,3},{3,0},{4,5},{5,6},{6,7},{7,4},{8,9},{9,10},{10,1... | collective-permute-start | bytes 786440 | tf_op jit(solution)/shard_map/ppermute | solution.py:38
  124.4 15.8 %collective-permute-start.18 = (bf16[128,1024]{1,0:T(8,128)(2,1)S(1)}, bf16[128,1024]{1,0:T(8,128)(2,1)S(1)}, u32[]{:S(2)}, u32[]{:S(2)}) collective-permute-start(bf16[128,1024]{1,0:T(8,128)(2,1)S(1)} %get-tuple-element.70), channel_id=1, source_target_pairs={{0,3},{1,0},{2,1},{3,2},{4,7},{5,4},{6,5},{7,6},{8,11},{9,8},{10,9... | collective-permute-start | bytes 786440 | tf_op jit(solution)/shard_map/ppermute | solution.py:38
  126.2 21.7 %collective-permute-start.17 = (bf16[128,1024]{1,0:T(8,128)(2,1)S(1)}, bf16[128,1024]{1,0:T(8,128)(2,1)S(1)}, u32[]{:S(2)}, u32[]{:S(2)}) collective-permute-start(bf16[128,1024]{1,0:T(8,128)(2,1)S(1)} %get-tuple-element.71), channel_id=1, source_target_pairs={{0,2},{1,3},{2,0},{3,1},{4,6},{5,7},{6,4},{7,5},{8,10},{9,11},{10,... | collective-permute-start | bytes 786440 | tf_op jit(solution)/shard_map/ppermute | solution.py:38
  129.0 18.9 %collective-permute-start.16 = (bf16[128,1024]{1,0:T(8,128)(2,1)S(1)}, bf16[128,1024]{1,0:T(8,128)(2,1)S(1)}, u32[]{:S(2)}, u32[]{:S(2)}) collective-permute-start(bf16[128,1024]{1,0:T(8,128)(2,1)S(1)} %get-tuple-element.69), channel_id=1, source_target_pairs={{0,1},{1,2},{2,3},{3,0},{4,5},{5,6},{6,7},{7,4},{8,9},{9,10},{10,1... | collective-permute-start | bytes 786440 | tf_op jit(solution)/shard_map/ppermute | solution.py:38
  137.1 134.8 %collective-permute-start.56 = (bf16[512,1024]{1,0:T(8,128)(2,1)}, bf16[512,1024]{1,0:T(8,128)(2,1)}, u32[]{:S(2)}, u32[]{:S(2)}) collective-permute-start(bf16[512,1024]{1,0:T(8,128)(2,1)} %split.191), channel_id=1, source_target_pairs={{0,16},{16,0},{1,17},{17,1},{2,18},{18,2},{3,19},{19,3},{4,20},{20... | collective-permute-start | bytes 3145736 | tf_op jit(solution)/shard_map/ppermute | solution.py:38
  148.3 8.0 %collective-permute-start.27 = (bf16[128,1024]{1,0:T(8,128)(2,1)S(1)}, bf16[128,1024]{1,0:T(8,128)(2,1)S(1)}, u32[]{:S(2)}, u32[]{:S(2)}) collective-permute-start(bf16[128,1024]{1,0:T(8,128)(2,1)S(1)} %convert_element_type.265), channel_id=1, source_target_pairs={{0,1},{1,2},{2,3},{3,0},{4,5},{5,6},{6,7},{7,4},{8,9},{9,10},{10,1... | collective-permute-start | bytes 786440 | tf_op jit(solution)/shard_map/ppermute | solution.py:38
  148.4 9.2 %collective-permute-start.26 = (bf16[128,1024]{1,0:T(8,128)(2,1)S(1)}, bf16[128,1024]{1,0:T(8,128)(2,1)S(1)}, u32[]{:S(2)}, u32[]{:S(2)}) collective-permute-start(bf16[128,1024]{1,0:T(8,128)(2,1)S(1)} %convert_element_type.265), channel_id=1, source_target_pairs={{0,2},{1,3},{2,0},{3,1},{4,6},{5,7},{6,4},{7,5},{8,10},{9,11},{10,... | collective-permute-start | bytes 786440 | tf_op jit(solution)/shard_map/ppermute | solution.py:38
  148.7 11.7 %collective-permute-start.25 = (bf16[128,1024]{1,0:T(8,128)(2,1)S(1)}, bf16[128,1024]{1,0:T(8,128)(2,1)S(1)}, u32[]{:S(2)}, u32[]{:S(2)}) collective-permute-start(bf16[128,1024]{1,0:T(8,128)(2,1)S(1)} %convert_element_type.265), channel_id=1, source_target_pairs={{0,3},{1,0},{2,1},{3,2},{4,7},{5,4},{6,5},{7,6},{8,11},{9,8},{10,9... | collective-permute-start | bytes 786440 | tf_op jit(solution)/shard_map/ppermute | solution.py:38
  160.9 8.2 %collective-permute-start.49 = (bf16[256,512]{1,0:T(8,128)(2,1)S(1)}, bf16[256,512]{1,0:T(8,128)(2,1)S(1)}, u32[]{:S(2)}, u32[]{:S(2)}) collective-permute-start(bf16[256,512]{1,0:T(8,128)(2,1)S(1)} %split.193), channel_id=1, source_target_pairs={{0,16},{16,0},{1,17},{17,1},{2,18},{18,2},{3,19},{19,3},{4,20},{20... | collective-permute-start | bytes 786440 | tf_op jit(solution)/shard_map/ppermute | solution.py:38
  169.2 28.9 %collective-permute-start.52 = (bf16[64,512]{1,0:T(8,128)(2,1)S(1)}, bf16[64,512]{1,0:T(8,128)(2,1)S(1)}, u32[]{:S(2)}, u32[]{:S(2)}) collective-permute-start(bf16[64,512]{1,0:T(8,128)(2,1)S(1)} %get-tuple-element.79), channel_id=1, source_target_pairs={{0,12},{4,0},{8,4},{12,8},{1,13},{5,1},{9,5},{13,9},{2,14},{6,2},{... | collective-permute-start | bytes 196616 | tf_op jit(solution)/shard_map/ppermute | solution.py:38
  175.8 22.3 %collective-permute-start.51 = (bf16[64,512]{1,0:T(8,128)(2,1)S(1)}, bf16[64,512]{1,0:T(8,128)(2,1)S(1)}, u32[]{:S(2)}, u32[]{:S(2)}) collective-permute-start(bf16[64,512]{1,0:T(8,128)(2,1)S(1)} %get-tuple-element.80), channel_id=1, source_target_pairs={{0,8},{4,12},{8,0},{12,4},{1,9},{5,13},{9,1},{13,5},{2,10},{6,14},... | collective-permute-start | bytes 196616 | tf_op jit(solution)/shard_map/ppermute | solution.py:38
  186.1 12.0 %collective-permute-start.50 = (bf16[64,512]{1,0:T(8,128)(2,1)S(1)}, bf16[64,512]{1,0:T(8,128)(2,1)S(1)}, u32[]{:S(2)}, u32[]{:S(2)}) collective-permute-start(bf16[64,512]{1,0:T(8,128)(2,1)S(1)} %get-tuple-element.78), channel_id=1, source_target_pairs={{0,4},{4,8},{8,12},{12,0},{1,5},{5,9},{9,13},{13,1},{2,6},{6,10},{... | collective-permute-start | bytes 196616 | tf_op jit(solution)/shard_map/ppermute | solution.py:38
  198.3 6.0 %collective-permute-start.53 = (bf16[64,512]{1,0:T(8,128)(2,1)S(1)}, bf16[64,512]{1,0:T(8,128)(2,1)S(1)}, u32[]{:S(2)}, u32[]{:S(2)}) collective-permute-start(bf16[64,512]{1,0:T(8,128)(2,1)S(1)} %get-tuple-element.35), channel_id=1, source_target_pairs={{0,12},{4,0},{8,4},{12,8},{1,13},{5,1},{9,5},{13,9},{2,14},{6,2},{... | collective-permute-start | bytes 196616 | tf_op jit(solution)/shard_map/ppermute | solution.py:38
  200.4 60.7 %collective-permute-start.30 = (bf16[2,256,512]{2,1,0:T(8,128)(2,1)S(1)}, bf16[2,256,512]{2,1,0:T(8,128)(2,1)S(1)}, u32[]{:S(2)}, u32[]{:S(2)}) collective-permute-start(bf16[2,256,512]{2,1,0:T(8,128)(2,1)S(1)} %get-tuple-element.55), channel_id=1, source_target_pairs={{12,0},{13,1},{14,2},{15,3},{28,16},{29,17},{30,18},{31,19}} | collective-permute-start | bytes 1572872 | tf_op jit(solution)/shard_map/ppermute | solution.py:306
  201.7 59.4 %collective-permute-start.29 = (bf16[2,256,512]{2,1,0:T(8,128)(2,1)S(1)}, bf16[2,256,512]{2,1,0:T(8,128)(2,1)S(1)}, u32[]{:S(2)}, u32[]{:S(2)}) collective-permute-start(bf16[2,256,512]{2,1,0:T(8,128)(2,1)S(1)} %get-tuple-element.56), channel_id=1, source_target_pairs={{8,0},{12,4},{9,1},{13,5},{10,2},{14,6},{11,3},{15,7},{24,16},{28,... | collective-permute-start | bytes 1572872 | tf_op jit(solution)/shard_map/ppermute | solution.py:306
  203.0 58.9 %collective-permute-start.28 = (bf16[2,256,512]{2,1,0:T(8,128)(2,1)S(1)}, bf16[2,256,512]{2,1,0:T(8,128)(2,1)S(1)}, u32[]{:S(2)}, u32[]{:S(2)}) collective-permute-start(bf16[2,256,512]{2,1,0:T(8,128)(2,1)S(1)} %get-tuple-element.54), channel_id=1, source_target_pairs={{4,0},{8,4},{12,8},{5,1},{9,5},{13,9},{6,2},{10,6},{14,10},{7,3},{... | collective-permute-start | bytes 1572872 | tf_op jit(solution)/shard_map/ppermute | solution.py:306
  204.3 49.1 %collective-permute-start.54 = (bf16[64,512]{1,0:T(8,128)(2,1)S(1)}, bf16[64,512]{1,0:T(8,128)(2,1)S(1)}, u32[]{:S(2)}, u32[]{:S(2)}) collective-permute-start(bf16[64,512]{1,0:T(8,128)(2,1)S(1)} %get-tuple-element.35), channel_id=1, source_target_pairs={{0,8},{4,12},{8,0},{12,4},{1,9},{5,13},{9,1},{13,5},{2,10},{6,14},... | collective-permute-start | bytes 196616 | tf_op jit(solution)/shard_map/ppermute | solution.py:38
  253.5 6.1 %collective-permute-start.55 = (bf16[64,512]{1,0:T(8,128)(2,1)S(1)}, bf16[64,512]{1,0:T(8,128)(2,1)S(1)}, u32[]{:S(2)}, u32[]{:S(2)}) collective-permute-start(bf16[64,512]{1,0:T(8,128)(2,1)S(1)} %get-tuple-element.35), channel_id=1, source_target_pairs={{0,4},{4,8},{8,12},{12,0},{1,5},{5,9},{9,13},{13,1},{2,6},{6,10},{... | collective-permute-start | bytes 196616 | tf_op jit(solution)/shard_map/ppermute | solution.py:38
  259.5 26.3 %collective-permute-start.63 = (bf16[1024,512]{1,0:T(8,128)(2,1)}, bf16[1024,512]{1,0:T(8,128)(2,1)S(1)}, u32[]{:S(2)}, u32[]{:S(2)}) collective-permute-start(bf16[1024,512]{1,0:T(8,128)(2,1)} %split.190), channel_id=1, source_target_pairs={{0,16},{16,0},{1,17},{17,1},{2,18},{18,2},{3,19},{19,3},{4,20},{20... | collective-permute-start | bytes 3145736 | tf_op jit(solution)/shard_map/ppermute | solution.py:38
  267.6 42.6 %collective-permute-start.33 = (bf16[128,1024]{1,0:T(8,128)(2,1)}, bf16[128,1024]{1,0:T(8,128)(2,1)}, u32[]{:S(2)}, u32[]{:S(2)}) collective-permute-start(bf16[128,1024]{1,0:T(8,128)(2,1)} %get-tuple-element.64), channel_id=1, source_target_pairs={{0,3},{1,0},{2,1},{3,2},{4,7},{5,4},{6,5},{7,6},{8,11},{9,8},{10,9... | collective-permute-start | bytes 786440 | tf_op jit(solution)/shard_map/ppermute | solution.py:38
  267.7 44.0 %collective-permute-start.32 = (bf16[128,1024]{1,0:T(8,128)(2,1)}, bf16[128,1024]{1,0:T(8,128)(2,1)}, u32[]{:S(2)}, u32[]{:S(2)}) collective-permute-start(bf16[128,1024]{1,0:T(8,128)(2,1)} %get-tuple-element.65), channel_id=1, source_target_pairs={{0,2},{1,3},{2,0},{3,1},{4,6},{5,7},{6,4},{7,5},{8,10},{9,11},{10,... | collective-permute-start | bytes 786440 | tf_op jit(solution)/shard_map/ppermute | solution.py:38
  268.4 44.0 %collective-permute-start.31 = (bf16[128,1024]{1,0:T(8,128)(2,1)S(1)}, bf16[128,1024]{1,0:T(8,128)(2,1)S(1)}, u32[]{:S(2)}, u32[]{:S(2)}) collective-permute-start(bf16[128,1024]{1,0:T(8,128)(2,1)S(1)} %get-tuple-element.63), channel_id=1, source_target_pairs={{0,1},{1,2},{2,3},{3,0},{4,5},{5,6},{6,7},{7,4},{8,9},{9,10},{10,1... | collective-permute-start | bytes 786440 | tf_op jit(solution)/shard_map/ppermute | solution.py:38
  271.8 114.1 %collective-permute-start.39 = (bf16[512,768]{1,0:T(8,128)(2,1)}, bf16[512,768]{1,0:T(8,128)(2,1)}, u32[]{:S(2)}, u32[]{:S(2)}) collective-permute-start(bf16[512,768]{1,0:T(8,128)(2,1)} %split.192), channel_id=1, source_target_pairs={{0,16},{16,0},{1,17},{17,1},{2,18},{18,2},{3,19},{19,3},{4,20},{20... | collective-permute-start | bytes 2359304 | tf_op jit(solution)/shard_map/ppermute | solution.py:38
  285.8 14.9 %collective-permute-start.46 = (f32[1792]{0:T(1024)S(1)}, f32[1792]{0:T(1024)S(1)}, u32[]{:S(2)}, u32[]{:S(2)}) collective-permute-start(f32[1792]{0:T(1024)S(1)} %pad_maximum_fusion.21), channel_id=1, source_target_pairs={{0,16},{16,0},{1,17},{17,1},{2,18},{18,2},{3,19},{19,3},{4,20},{20... | collective-permute-start | bytes 21512 | tf_op jit(solution)/shard_map/ppermute | solution.py:87
  309.1 24.5 %collective-permute-start.59 = (bf16[128,1024]{1,0:T(8,128)(2,1)}, bf16[128,1024]{1,0:T(8,128)(2,1)}, u32[]{:S(2)}, u32[]{:S(2)}) collective-permute-start(bf16[128,1024]{1,0:T(8,128)(2,1)} %get-tuple-element.52), channel_id=1, source_target_pairs={{0,12},{4,0},{8,4},{12,8},{1,13},{5,1},{9,5},{13,9},{2,14},{6,2},{... | collective-permute-start | bytes 786440 | tf_op jit(solution)/shard_map/ppermute | solution.py:38
  310.3 23.4 %collective-permute-start.58 = (bf16[128,1024]{1,0:T(8,128)(2,1)}, bf16[128,1024]{1,0:T(8,128)(2,1)}, u32[]{:S(2)}, u32[]{:S(2)}) collective-permute-start(bf16[128,1024]{1,0:T(8,128)(2,1)} %get-tuple-element.53), channel_id=1, source_target_pairs={{0,8},{4,12},{8,0},{12,4},{1,9},{5,13},{9,1},{13,5},{2,10},{6,14},... | collective-permute-start | bytes 786440 | tf_op jit(solution)/shard_map/ppermute | solution.py:38
  311.7 22.6 %collective-permute-start.57 = (bf16[128,1024]{1,0:T(8,128)(2,1)}, bf16[128,1024]{1,0:T(8,128)(2,1)}, u32[]{:S(2)}, u32[]{:S(2)}) collective-permute-start(bf16[128,1024]{1,0:T(8,128)(2,1)} %get-tuple-element.51), channel_id=1, source_target_pairs={{0,4},{4,8},{8,12},{12,0},{1,5},{5,9},{9,13},{13,1},{2,6},{6,10},{... | collective-permute-start | bytes 786440 | tf_op jit(solution)/shard_map/ppermute | solution.py:38
  318.9 5.4 %collective-permute-start.35 = (f32[6,1024]{1,0:T(8,128)S(1)}, f32[6,1024]{1,0:T(8,128)S(1)}, u32[]{:S(2)}, u32[]{:S(2)}) collective-permute-start(f32[6,1024]{1,0:T(8,128)S(1)} %fusion.96), channel_id=1, source_target_pairs={{0,4},{4,0},{8,12},{12,8},{1,5},{5,1},{9,13},{13,9},{2,6},{6,2},{1... | collective-permute-start | bytes 73736 | tf_op jit(solution)/shard_map/ppermute | solution.py:87
  324.3 6.9 %collective-permute-start.36 = (f32[6,1024]{1,0:T(8,128)S(1)}, f32[6,1024]{1,0:T(8,128)S(1)}, u32[]{:S(2)}, u32[]{:S(2)}) collective-permute-start(f32[6,1024]{1,0:T(8,128)S(1)} %add.428), channel_id=1, source_target_pairs={{0,8},{4,12},{8,0},{12,4},{1,9},{5,13},{9,1},{13,5},{2,10},{6,14},... | collective-permute-start | bytes 73736 | tf_op jit(solution)/shard_map/ppermute | solution.py:87
  331.2 9.1 %collective-permute-start.66 = (bf16[256,512]{1,0:T(8,128)(2,1)S(1)}, bf16[256,512]{1,0:T(8,128)(2,1)S(1)}, u32[]{:S(2)}, u32[]{:S(2)}) collective-permute-start(bf16[256,512]{1,0:T(8,128)(2,1)S(1)} %copy-done.28), channel_id=1, source_target_pairs={{0,12},{4,0},{8,4},{12,8},{1,13},{5,1},{9,5},{13,9},{2,14},{6,2},{... | collective-permute-start | bytes 786440 | tf_op jit(solution)/shard_map/ppermute | solution.py:38
  333.6 23.1 %collective-permute-start.65 = (bf16[256,512]{1,0:T(8,128)(2,1)S(1)}, bf16[256,512]{1,0:T(8,128)(2,1)S(1)}, u32[]{:S(2)}, u32[]{:S(2)}) collective-permute-start(bf16[256,512]{1,0:T(8,128)(2,1)S(1)} %copy-done.27), channel_id=1, source_target_pairs={{0,8},{4,12},{8,0},{12,4},{1,9},{5,13},{9,1},{13,5},{2,10},{6,14},... | collective-permute-start | bytes 786440 | tf_op jit(solution)/shard_map/ppermute | solution.py:38
  333.7 23.0 %collective-permute-start.64 = (bf16[256,512]{1,0:T(8,128)(2,1)S(1)}, bf16[256,512]{1,0:T(8,128)(2,1)S(1)}, u32[]{:S(2)}, u32[]{:S(2)}) collective-permute-start(bf16[256,512]{1,0:T(8,128)(2,1)S(1)} %copy-done.26), channel_id=1, source_target_pairs={{0,4},{4,8},{8,12},{12,0},{1,5},{5,9},{9,13},{13,1},{2,6},{6,10},{... | collective-permute-start | bytes 786440 | tf_op jit(solution)/shard_map/ppermute | solution.py:38
  336.0 29.1 %collective-permute-start.60 = (bf16[128,1024]{1,0:T(8,128)(2,1)S(1)}, bf16[128,1024]{1,0:T(8,128)(2,1)S(1)}, u32[]{:S(2)}, u32[]{:S(2)}) collective-permute-start(bf16[128,1024]{1,0:T(8,128)(2,1)S(1)} %get-tuple-element.33), channel_id=1, source_target_pairs={{0,12},{4,0},{8,4},{12,8},{1,13},{5,1},{9,5},{13,9},{2,14},{6,2},{... | collective-permute-start | bytes 786440 | tf_op jit(solution)/shard_map/ppermute | solution.py:38
  340.3 41.3 %collective-permute-start.61 = (bf16[128,1024]{1,0:T(8,128)(2,1)S(1)}, bf16[128,1024]{1,0:T(8,128)(2,1)S(1)}, u32[]{:S(2)}, u32[]{:S(2)}) collective-permute-start(bf16[128,1024]{1,0:T(8,128)(2,1)S(1)} %get-tuple-element.33), channel_id=1, source_target_pairs={{0,8},{4,12},{8,0},{12,4},{1,9},{5,13},{9,1},{13,5},{2,10},{6,14},... | collective-permute-start | bytes 786440 | tf_op jit(solution)/shard_map/ppermute | solution.py:38
  356.7 29.0 %collective-permute-start.62 = (bf16[128,1024]{1,0:T(8,128)(2,1)S(1)}, bf16[128,1024]{1,0:T(8,128)(2,1)S(1)}, u32[]{:S(2)}, u32[]{:S(2)}) collective-permute-start(bf16[128,1024]{1,0:T(8,128)(2,1)S(1)} %get-tuple-element.33), channel_id=1, source_target_pairs={{0,4},{4,8},{8,12},{12,0},{1,5},{5,9},{9,13},{13,1},{2,6},{6,10},{... | collective-permute-start | bytes 786440 | tf_op jit(solution)/shard_map/ppermute | solution.py:38
  360.6 25.2 %collective-permute-start.67 = (bf16[256,512]{1,0:T(8,128)(2,1)S(1)}, bf16[256,512]{1,0:T(8,128)(2,1)S(1)}, u32[]{:S(2)}, u32[]{:S(2)}) collective-permute-start(bf16[256,512]{1,0:T(8,128)(2,1)S(1)} %get-tuple-element.31), channel_id=1, source_target_pairs={{0,12},{4,0},{8,4},{12,8},{1,13},{5,1},{9,5},{13,9},{2,14},{6,2},{... | collective-permute-start | bytes 786440 | tf_op jit(solution)/shard_map/ppermute | solution.py:38
  365.1 40.5 %collective-permute-start.68 = (bf16[256,512]{1,0:T(8,128)(2,1)S(1)}, bf16[256,512]{1,0:T(8,128)(2,1)S(1)}, u32[]{:S(2)}, u32[]{:S(2)}) collective-permute-start(bf16[256,512]{1,0:T(8,128)(2,1)S(1)} %get-tuple-element.31), channel_id=1, source_target_pairs={{0,8},{4,12},{8,0},{12,4},{1,9},{5,13},{9,1},{13,5},{2,10},{6,14},... | collective-permute-start | bytes 786440 | tf_op jit(solution)/shard_map/ppermute | solution.py:38
  381.6 36.7 %collective-permute-start.69 = (bf16[256,512]{1,0:T(8,128)(2,1)S(1)}, bf16[256,512]{1,0:T(8,128)(2,1)S(1)}, u32[]{:S(2)}, u32[]{:S(2)}) collective-permute-start(bf16[256,512]{1,0:T(8,128)(2,1)S(1)} %get-tuple-element.31), channel_id=1, source_target_pairs={{0,4},{4,8},{8,12},{12,0},{1,5},{5,9},{9,13},{13,1},{2,6},{6,10},{... | collective-permute-start | bytes 786440 | tf_op jit(solution)/shard_map/ppermute | solution.py:38
  387.9 17.8 %collective-permute-start.42 = (bf16[128,768]{1,0:T(8,128)(2,1)S(1)}, bf16[128,768]{1,0:T(8,128)(2,1)S(1)}, u32[]{:S(2)}, u32[]{:S(2)}) collective-permute-start(bf16[128,768]{1,0:T(8,128)(2,1)S(1)} %get-tuple-element.61), channel_id=1, source_target_pairs={{0,12},{4,0},{8,4},{12,8},{1,13},{5,1},{9,5},{13,9},{2,14},{6,2},{... | collective-permute-start | bytes 589832 | tf_op jit(solution)/shard_map/ppermute | solution.py:38
  390.8 26.2 %collective-permute-start.41 = (bf16[128,768]{1,0:T(8,128)(2,1)S(1)}, bf16[128,768]{1,0:T(8,128)(2,1)S(1)}, u32[]{:S(2)}, u32[]{:S(2)}) collective-permute-start(bf16[128,768]{1,0:T(8,128)(2,1)S(1)} %get-tuple-element.62), channel_id=1, source_target_pairs={{0,8},{4,12},{8,0},{12,4},{1,9},{5,13},{9,1},{13,5},{2,10},{6,14},... | collective-permute-start | bytes 589832 | tf_op jit(solution)/shard_map/ppermute | solution.py:38
  401.8 15.2 %collective-permute-start.40 = (bf16[128,768]{1,0:T(8,128)(2,1)S(1)}, bf16[128,768]{1,0:T(8,128)(2,1)S(1)}, u32[]{:S(2)}, u32[]{:S(2)}) collective-permute-start(bf16[128,768]{1,0:T(8,128)(2,1)S(1)} %get-tuple-element.60), channel_id=1, source_target_pairs={{0,4},{4,8},{8,12},{12,0},{1,5},{5,9},{9,13},{13,1},{2,6},{6,10},{... | collective-permute-start | bytes 589832 | tf_op jit(solution)/shard_map/ppermute | solution.py:38
  417.2 8.6 %collective-permute-start.43 = (bf16[128,768]{1,0:T(8,128)(2,1)S(1)}, bf16[128,768]{1,0:T(8,128)(2,1)S(1)}, u32[]{:S(2)}, u32[]{:S(2)}) collective-permute-start(bf16[128,768]{1,0:T(8,128)(2,1)S(1)} %get-tuple-element.37), channel_id=1, source_target_pairs={{0,12},{4,0},{8,4},{12,8},{1,13},{5,1},{9,5},{13,9},{2,14},{6,2},{... | collective-permute-start | bytes 589832 | tf_op jit(solution)/shard_map/ppermute | solution.py:38
  418.4 19.3 %collective-permute-start.44 = (bf16[128,768]{1,0:T(8,128)(2,1)S(1)}, bf16[128,768]{1,0:T(8,128)(2,1)S(1)}, u32[]{:S(2)}, u32[]{:S(2)}) collective-permute-start(bf16[128,768]{1,0:T(8,128)(2,1)S(1)} %get-tuple-element.37), channel_id=1, source_target_pairs={{0,8},{4,12},{8,0},{12,4},{1,9},{5,13},{9,1},{13,5},{2,10},{6,14},... | collective-permute-start | bytes 589832 | tf_op jit(solution)/shard_map/ppermute | solution.py:38
  423.0 14.7 %collective-permute-start.45 = (bf16[128,768]{1,0:T(8,128)(2,1)S(1)}, bf16[128,768]{1,0:T(8,128)(2,1)S(1)}, u32[]{:S(2)}, u32[]{:S(2)}) collective-permute-start(bf16[128,768]{1,0:T(8,128)(2,1)S(1)} %get-tuple-element.37), channel_id=1, source_target_pairs={{0,4},{4,8},{8,12},{12,0},{1,5},{5,9},{9,13},{13,1},{2,6},{6,10},{... | collective-permute-start | bytes 589832 | tf_op jit(solution)/shard_map/ppermute | solution.py:38
  (50 other events, 542.2 us)

commit v2 on v1

v2 whole, which is shorter than its diff:
```python
import functools

import jax
import jax.numpy as jnp
from jax import lax
from jax.experimental import pallas as pl
from jax.experimental.pallas import tpu as pltpu
from jax.sharding import PartitionSpec as P

HD = 64


EPSILON = 1e-05
F32 = jnp.float32
BF16 = jnp.bfloat16
SCALE = HD ** (-0.5)


def normalize(rows_in, gain_vec, bias_vec):
    row_mean = jnp.mean(rows_in, axis=-1, keepdims=True)
    centered = rows_in - row_mean
    spread = jnp.mean(centered * centered, axis=-1, keepdims=True)
    inverse = lax.rsqrt(spread + EPSILON)
    scaled = centered * inverse
    return (scaled * gain_vec + bias_vec, scaled, inverse)


def normalize_back(grad_rows, scaled, inverse, gain_vec):
    weighted = grad_rows * gain_vec
    centered = weighted - jnp.mean(weighted, axis=-1, keepdims=True)
    return (centered - scaled * jnp.mean(weighted * scaled, axis=-1, keepdims=True)) * inverse


def gelu_tanh(values_in):
    return jax.nn.gelu(values_in, approximate=True)


def shifted(value, axis_name, step):
    count = lax.axis_size(axis_name)
    return lax.ppermute(value, axis_name, [(i, (i + step) % count) for i in range(count)])


def turned(value, axis_name, axis):
    count = lax.axis_size(axis_name)
    return jnp.concatenate(
        [value] + [shifted(value, axis_name, count - k) for k in range(1, count)], axis=axis
    )


def turned_sum(partial_value, axis_name, axis):
    count = lax.axis_size(axis_name)
    pieces = jnp.split(partial_value, count, axis=axis)
    total = pieces[0]
    for k in range(1, count):
        total = total + shifted(pieces[k].astype(BF16), axis_name, k).astype(F32)
    return total


def rounded(value):
    return lax.reduce_precision(value, 8, 7).astype(BF16)


def sum_everywhere(value, axis_name, axis):
    count = lax.axis_size(axis_name)
    index = lax.axis_index(axis_name)
    steps = [1 << i for i in range(count.bit_length() - 1)]

    def swap(piece, step):
        return lax.ppermute(piece, axis_name, [(i, i ^ step) for i in range(count)])

    for step in steps:
        bit = lax.rem(index // step, 2)
        size = value.shape[axis] // 2
        other = lax.dynamic_slice_in_dim(value, (1 - bit) * size, size, axis).astype(BF16)
        own = lax.dynamic_slice_in_dim(value, bit * size, size, axis)
        value = own + swap(other, step).astype(F32)
    value = rounded(value)
    for step in reversed(steps):
        bit = lax.rem(index // step, 2)
        size = value.shape[axis]
        other = swap(value, step)
        low = jnp.where(bit == 0, value, other)
        high = jnp.where(bit == 0, other, value)
        value = jnp.concatenate([low, high], axis=axis)
    return value.astype(F32)


def greet(axis_name, count, index):
    barrier = pltpu.get_barrier_semaphore()
    for k in range(1, count):
        pl.semaphore_signal(
            barrier,
            inc=1,
            device_id={axis_name: lax.rem(index + k, count)},
            device_id_type=pl.DeviceIdType.MESH,
        )
    pl.semaphore_wait(barrier, count - 1)


def gather_kernel(axis_name, count, x_ref, o_ref, send_sem, recv_sem, own_sem):
    index = lax.axis_index(axis_name)
    own = pltpu.make_async_copy(x_ref, o_ref.at[0], own_sem)
    own.start()
    greet(axis_name, count, index)
    copies = []
    for k in range(1, count):
        copies.append(
            pltpu.make_async_remote_copy(
                src_ref=x_ref,
                dst_ref=o_ref.at[k],
                send_sem=send_sem.at[k],
                recv_sem=recv_sem.at[k],
                device_id={axis_name: lax.rem(index + count - k, count)},
                device_id_type=pl.DeviceIdType.MESH,
            )
        )
        copies[-1].start()
    for copy in copies:
        copy.wait()
    own.wait()


def scatter_kernel(axis_name, count, x_ref, o_ref, send_sem, recv_sem, own_sem):
    index = lax.axis_index(axis_name)
    own = pltpu.make_async_copy(x_ref.at[0], o_ref.at[0], own_sem)
    own.start()
    greet(axis_name, count, index)
    copies = []
    for k in range(1, count):
        copies.append(
            pltpu.make_async_remote_copy(
                src_ref=x_ref.at[k],
                dst_ref=o_ref.at[k],
                send_sem=send_sem.at[k],
                recv_sem=recv_sem.at[k],
                device_id={axis_name: lax.rem(index + k, count)},
                device_id_type=pl.DeviceIdType.MESH,
            )
        )
        copies[-1].start()
    for copy in copies:
        copy.wait()
    own.wait()


def swap_kernel(axis_name, count, x_ref, o_ref, send_sem, recv_sem, own_sem):
    index = lax.axis_index(axis_name)
    own = pltpu.make_async_copy(x_ref.at[index], o_ref.at[index], own_sem)
    own.start()
    greet(axis_name, count, index)
    copies = []
    for k in range(1, count):
        target = lax.rem(index + k, count)
        copies.append(
            pltpu.make_async_remote_copy(
                src_ref=x_ref.at[target],
                dst_ref=o_ref.at[index],
                send_sem=send_sem.at[k],
                recv_sem=recv_sem.at[k],
                device_id={axis_name: target},
                device_id_type=pl.DeviceIdType.MESH,
            )
        )
        copies[-1].start()
    for copy in copies:
        copy.wait()
    own.wait()


def exchange(kernel, value, axis_name, collective_id):
    count = lax.axis_size(axis_name)
    shape = value.shape if value.ndim == 3 else (count,) + value.shape
    return pl.pallas_call(
        functools.partial(kernel, axis_name, count),
        out_shape=jax.ShapeDtypeStruct(shape, value.dtype),
        in_specs=[pl.BlockSpec(memory_space=pl.ANY)],
        out_specs=pl.BlockSpec(memory_space=pl.ANY),
        scratch_shapes=[
            pltpu.SemaphoreType.DMA((count,)),
            pltpu.SemaphoreType.DMA((count,)),
            pltpu.SemaphoreType.DMA,
        ],
        compiler_params=pltpu.CompilerParams(collective_id=collective_id, has_side_effects=True),
        cost_estimate=pl.CostEstimate(flops=0, bytes_accessed=10 * 10**6, transcendentals=0),
    )(value)


def gathered(rows):
    return exchange(gather_kernel, rows, "tp", 0).reshape(-1, rows.shape[1])


def scattered_sum(partial_value):
    count = lax.axis_size("tp")
    pieces = partial_value.reshape(count, -1, partial_value.shape[1]).astype(BF16)
    return jnp.sum(exchange(scatter_kernel, pieces, "tp", 1).astype(F32), axis=0)


def sum_small(value, axis_names):
    for axis_name in axis_names:
        count = lax.axis_size(axis_name)
        step = 1
        while step < count:
            value = value + lax.ppermute(
                value, axis_name, [(i, i ^ step) for i in range(count)]
            )
            step *= 2
    return value


def dot(a, b, contract):
    return lax.dot_general(a, b, (contract, ((), ())), preferred_element_type=F32)


def attend_kernel(qkv_ref, qpos_ref, qseg_ref, kpos_ref, kseg_ref, att_ref, log_ref):
    blocks, block_len, width = qkv_ref.shape
    width //= 3
    heads = width // HD
    for i in range(blocks):
        keep = (i + 1) * block_len
        allowed = (kpos_ref[:keep] <= qpos_ref[i : i + 1]) & (kseg_ref[:keep] == qseg_ref[i : i + 1])
        for h in range(heads):
            cols = slice(h * HD, (h + 1) * HD)
            kcols = slice(width + h * HD, width + (h + 1) * HD)
            vcols = slice(2 * width + h * HD, 2 * width + (h + 1) * HD)
            keys = qkv_ref[: i + 1, :, kcols].reshape(keep, HD)
            values = qkv_ref[: i + 1, :, vcols].reshape(keep, HD)
            scores = dot(keys, qkv_ref[i, :, cols], ((1,), (1,))) * SCALE
            scores = jnp.where(allowed, scores, -1e30)
            highest = jnp.max(scores, axis=0, keepdims=True)
            exponent = jnp.exp(scores - highest)
            denominator = jnp.sum(exponent, axis=0, keepdims=True)
            probs = (exponent * (1.0 / denominator)).astype(BF16)
            att_ref[i, :, cols] = dot(probs, values, ((0,), (0,))).astype(BF16)
            row = i * heads + h
            log_ref[row : row + 1, :] = highest + jnp.log(denominator)


def attend_back_kernel(
    qkv_ref, ga_ref, log_ref, qpos_ref, qseg_ref, kpos_ref, kseg_ref, grad_ref, gk_ref, gv_ref
):
    blocks, block_len, width = qkv_ref.shape
    width //= 3
    heads = width // HD
    for i in reversed(range(blocks)):
        keep = (i + 1) * block_len
        allowed = (kpos_ref[:keep] <= qpos_ref[i : i + 1]) & (kseg_ref[:keep] == qseg_ref[i : i + 1])
        for h in range(heads):
            cols = slice(h * HD, (h + 1) * HD)
            kcols = slice(width + h * HD, width + (h + 1) * HD)
            vcols = slice(2 * width + h * HD, 2 * width + (h + 1) * HD)
            query = qkv_ref[i, :, cols]
            keys = qkv_ref[: i + 1, :, kcols].reshape(keep, HD)
            values = qkv_ref[: i + 1, :, vcols].reshape(keep, HD)
            grad = ga_ref[i, :, cols]
            row = i * heads + h
            scores = dot(keys, query, ((1,), (1,))) * SCALE
            probs = jnp.exp(jnp.where(allowed, scores, -1e30) - log_ref[row : row + 1, :])
            grad_probs = dot(values, grad, ((1,), (1,)))
            inner = jnp.sum(probs * grad_probs, axis=0, keepdims=True)
            grad_scores = (probs * (grad_probs - inner)).astype(BF16)
            grad_ref[i, :, cols] = (dot(grad_scores, keys, ((0,), (0,))) * SCALE).astype(BF16)
            grad_keys = dot(grad_scores, query, ((1,), (0,))) * SCALE
            grad_values = dot(probs.astype(BF16), grad, ((1,), (0,)))
            if i == blocks - 1:
                gk_ref[:keep, cols] = grad_keys
                gv_ref[:keep, cols] = grad_values
            else:
                gk_ref[:keep, cols] += grad_keys
                gv_ref[:keep, cols] += grad_values
    shape = (blocks, block_len, width)
    grad_ref[:, :, width : 2 * width] = gk_ref[...].reshape(shape).astype(BF16)
    grad_ref[:, :, 2 * width :] = gv_ref[...].reshape(shape).astype(BF16)


def local_call(kernel, outs, scratch, *operands):
    whole = pl.BlockSpec(memory_space=pltpu.VMEM)
    return pl.pallas_call(
        kernel,
        in_specs=[whole] * len(operands),
        out_specs=[whole] * len(outs),
        out_shape=outs,
        scratch_shapes=scratch,
        compiler_params=pltpu.CompilerParams(vmem_limit_bytes=48 * 1024 * 1024),
        cost_estimate=pl.CostEstimate(flops=4 * 10**9, bytes_accessed=8 * 10**6, transcendentals=0),
    )(*operands)


def shards(
    tokens,
    segments,
    ln1_gain,
    ln1_bias,
    qkv_weight,
    qkv_bias,
    out_weight,
    out_bias,
    ln2_gain,
    ln2_bias,
    fc_weight,
    fc_bias,
    proj_weight,
    proj_bias,
    grad_out,
):
    seq_count, shard_len, model_width = tokens.shape
    tp_count, ctx_count, dp_count = (lax.axis_size(n) for n in ("tp", "ctx", "dp"))
    tp_index, ctx_index, dp_index = (lax.axis_index(n) for n in ("tp", "ctx", "dp"))
    block_len = shard_len * tp_count
    key_len = block_len * ctx_count
    width_tp = qkv_weight.shape[2]
    piece = model_width // dp_count
    own_rows = seq_count * shard_len

    def turn(value, back=False):
        if dp_count == 1:
            return value
        start = dp_index * piece
        if back:
            start = lax.rem(model_width - start, model_width)
        return lax.dynamic_slice_in_dim(
            jnp.concatenate([value, value], axis=-1), start, model_width, value.ndim - 1
        )

    residual_in = turn(tokens.reshape(own_rows, model_width)).astype(F32)
    grad_low = turn(grad_out.reshape(own_rows, model_width))
    ln1_gain, ln1_bias, out_bias, ln2_gain, ln2_bias, proj_bias = [
        turn(v) for v in (ln1_gain, ln1_bias, out_bias, ln2_gain, ln2_bias, proj_bias)
    ]

    normed_one, scaled_one, inverse_one = normalize(residual_in, ln1_gain, ln1_bias)
    attn_rows = gathered(normed_one.astype(BF16))
    qkv_flat = jnp.concatenate([qkv_weight[:, c] for c in range(3)], axis=1)
    qkv_full = turned(qkv_flat, "dp", 0)
    out_full = turned(out_weight, "dp", 1)
    fc_full = turned(fc_weight, "dp", 0)
    proj_full = turned(proj_weight, "dp", 1)
    grad_rows = turned(grad_low, "tp", 0)

    per_seq = ctx_count // seq_count
    group_width = width_tp // per_seq

    def by_group(rows, parts):
        rows = rows.reshape(tp_count, seq_count, shard_len, parts, per_seq, group_width)
        rows = rows.transpose(1, 4, 0, 2, 3, 5)
        return rows.reshape(ctx_count, block_len, parts * group_width)

    def by_rows(groups, parts):
        groups = groups.reshape(seq_count, per_seq, tp_count, shard_len, parts, group_width)
        groups = groups.transpose(2, 0, 3, 4, 1, 5)
        return groups.reshape(tp_count * own_rows, parts * width_tp)

    mixed = (dot(attn_rows, qkv_full, ((1,), (0,))) + qkv_bias.reshape(-1)).astype(BF16)
    mixed = exchange(swap_kernel, by_group(mixed, 3), "ctx", 2)

    within = jnp.arange(shard_len, dtype=jnp.int32)
    block_of = lax.rem(jnp.arange(tp_count, dtype=jnp.int32) + tp_index, tp_count)
    own_order = (block_of[:, None] * shard_len + within[None, :]).reshape(-1)
    places = jnp.arange(ctx_count, dtype=jnp.int32)[:, None] * block_len + own_order[None, :]
    document = lax.dynamic_index_in_dim(segments, ctx_index // per_seq, 0, False)
    document = document.reshape(ctx_count, tp_count, shard_len)
    document = lax.dynamic_slice_in_dim(
        jnp.concatenate([document, document], axis=1), tp_index, tp_count, 1
    ).reshape(ctx_count, block_len)
    places = (places, document, places.reshape(key_len, 1), document.reshape(key_len, 1))
    attended, log_totals = local_call(
        attend_kernel,
        [
            jax.ShapeDtypeStruct((ctx_count, block_len, group_width), BF16),
            jax.ShapeDtypeStruct((ctx_count * (group_width // HD), block_len), F32),
        ],
        [],
        mixed,
        *places,
    )
    attended_flat = by_rows(exchange(swap_kernel, attended, "ctx", 3), 1)
    branch = scattered_sum(dot(attended_flat, out_full, ((1,), (0,))))
    middle = residual_in + branch + out_bias
    normed_two, scaled_two, inverse_two = normalize(middle, ln2_gain, ln2_bias)
    mlp_rows = gathered(normed_two.astype(BF16))
    upward = dot(mlp_rows, fc_full, ((1,), (0,))) + fc_bias
    hidden, gelu_back = jax.vjp(gelu_tanh, upward)
    hidden_low = hidden.astype(BF16)

    grad_hidden = dot(grad_rows, proj_full, ((1,), (1,)))
    grad_up = gelu_back(grad_hidden)[0].astype(BF16)
    fc_bias_part = jnp.sum(grad_up, axis=0, dtype=F32)
    grad_normed_two = scattered_sum(dot(grad_up, fc_full, ((1,), (1,))))
    mlp_out = turned_sum(dot(hidden_low, proj_full, ((1,), (0,))), "tp", 0)
    block_out = turn((middle + mlp_out + proj_bias).astype(BF16), True)

    def over_dp(full, axis):
        return turned_sum(full, "dp", axis)

    proj_grad = over_dp(dot(hidden_low, grad_rows, ((0,), (0,))), 1)
    fc_grad = over_dp(dot(mlp_rows, grad_up, ((0,), (0,))), 0)
    proj_weight_grad = sum_everywhere(proj_grad, "ctx", 0)
    fc_weight_grad = sum_everywhere(fc_grad, "ctx", 0)

    grad_top = grad_low.astype(F32)
    grad_middle = grad_top + normalize_back(grad_normed_two, scaled_two, inverse_two, ln2_gain)
    middle_rows = gathered(grad_middle.astype(BF16))
    grad_attended = by_group(dot(middle_rows, out_full, ((1,), (1,))).astype(BF16), 1)
    grad_attended = exchange(swap_kernel, grad_attended, "ctx", 3)
    out_grad = over_dp(dot(attended_flat, middle_rows, ((0,), (0,))), 1)
    out_weight_grad = sum_everywhere(out_grad, "ctx", 0)

    (grad_groups,) = local_call(
        attend_back_kernel,
        [jax.ShapeDtypeStruct(mixed.shape, BF16)],
        [pltpu.VMEM((key_len, group_width), F32)] * 2,
        mixed,
        grad_attended,
        log_totals,
        *places,
    )
    grad_mixed = by_rows(exchange(swap_kernel, grad_groups, "ctx", 2), 3)
    qkv_bias_part = jnp.sum(grad_mixed, axis=0, dtype=F32)
    qkv_grad = over_dp(dot(attn_rows, grad_mixed, ((0,), (0,))), 0)
    qkv_grad = sum_everywhere(qkv_grad, "ctx", 0)
    qkv_weight_grad = jnp.stack(jnp.split(qkv_grad, 3, axis=1), axis=1)
    grad_normed_one = scattered_sum(dot(grad_mixed, qkv_full, ((1,), (1,))))
    tokens_grad = grad_middle + normalize_back(grad_normed_one, scaled_one, inverse_one, ln1_gain)

    shared = jnp.stack(
        [
            jnp.sum(grad_normed_one * scaled_one, axis=0),
            jnp.sum(grad_normed_one, axis=0),
            jnp.sum(grad_middle, axis=0),
            jnp.sum(grad_normed_two * scaled_two, axis=0),
            jnp.sum(grad_normed_two, axis=0),
            jnp.sum(grad_top, axis=0),
        ]
    )
    shared = sum_small(turn(shared, True), ("dp", "ctx", "tp"))
    split_biases = sum_small(jnp.concatenate([qkv_bias_part, fc_bias_part]), ("dp", "ctx"))
    qkv_bias_grad = split_biases[: 3 * width_tp].reshape(3, width_tp)
    fc_bias_grad = split_biases[3 * width_tp :]
    ln1_gain_grad, ln1_bias_grad, out_bias_grad, ln2_gain_grad, ln2_bias_grad, proj_bias_grad = [
        shared[i] for i in range(6)
    ]
    return (
        block_out.reshape(tokens.shape),
        turn(tokens_grad, True).reshape(tokens.shape),
        ln1_gain_grad,
        ln1_bias_grad,
        qkv_weight_grad,
        qkv_bias_grad,
        out_weight_grad,
        out_bias_grad,
        ln2_gain_grad,
        ln2_bias_grad,
        fc_weight_grad,
        fc_bias_grad,
        proj_weight_grad,
        proj_bias_grad,
    )


def solution(mesh):
    placed = (
        P("dp", ("ctx", "tp"), None),
        P("dp", None),
        P(),
        P(),
        P("dp", None, "tp"),
        P(None, "tp"),
        P("tp", "dp"),
        P(),
        P(),
        P(),
        P("dp", "tp"),
        P("tp"),
        P("tp", "dp"),
        P(),
        P("dp", ("ctx", "tp"), None),
    )
    return jax.shard_map(
        shards,
        mesh=mesh,
        in_specs=placed,
        out_specs=(
            P("dp", ("ctx", "tp"), None),
            P("dp", ("ctx", "tp"), None),
            P(),
            P(),
            P("dp", None, "tp"),
            P(None, "tp"),
            P("tp", "dp"),
            P(),
            P(),
            P(),
            P("dp", "tp"),
            P("tp"),
            P("tp", "dp"),
            P(),
        ),
        check_vma=False,
    )
```

time: 440 us -> 419 us (0.952); the launches traced: 439 us -> 414 us
  Pallas kernels: 16 us -> 152 us
  waiting for transfers between devices: 221 us -> 117 us
  starting transfers between devices: 136 us -> 41.4 us
  local copies, waits for them, and re-layouts: 23 us -> 40 us
  matrix products: 21.1 us -> 33.4 us
  other arithmetic: 20.1 us -> 27.4 us
    ppermute x56 -> x14, waiting for transfers between devices: 168 us -> 11.6 us  [shifted(): lax.ppermute(value, axis_name, [(i, (i + step) % count) for i in range(co...]
    pallas_call x2 -> x12, Pallas kernels: 16 us -> 152 us  [the longest x10 142 us: exchange(): pl.pallas_call(functools.partial(kernel, axis_name, count), out_shape=jax...]
    ppermute x56 -> x14, starting transfers between devices: 114 us -> 13.1 us  [shifted(): lax.ppermute(value, axis_name, [(i, (i + step) % count) for i in range(co...]
    ppermute x6 -> x16, waiting for transfers between devices: 20.8 us -> 104 us  [swap(): return lax.ppermute(piece, axis_name, [(i, i ^ step) for i in range(count)])]
    ppermute x8, waiting for transfers between devices: 32.1 us -> 1.61 us  [sum_small(): lax.ppermute(value, axis_name, [(i, i ^ step) for i in range(count)])]
    dot_general x12, matrix products: 21.1 us -> 33.4 us  [dot(): lax.dot_general(a, b, (contract, ((), ())), preferred_element_type=F32)]
    reshape x6 -> x10, local copies, waits for them, and re-layouts: 0.32 us -> 10.1 us  [the longest x2 3.88 us: by_rows(): groups.reshape(seq_count, per_seq, tp_count, shard_len, parts, group_width)]
    convert_element_type x4 -> x11, other arithmetic: 0.71 us -> 6.88 us  [the longest x4 4.13 us: sum_everywhere(): return value.astype(F32)]
  transfers between devices with their start and end apart: 70 -> 38, of which waited for: 38 -> 17; matrix products, arithmetic and copies ran while one was open for 12% -> 19% of each run, Pallas kernels for 4% -> 33%
where the time goes in v2:
time: 419 us; the launch traced here: 414 us
  Pallas kernels  152 us (36%)
  waiting for transfers between devices  117 us (28%)
  starting transfers between devices  41.4 us (10%)
  local copies, waits for them, and re-layouts  40 us (10%)
  matrix products  33.4 us (8%)
  other arithmetic  27.4 us (7%)
    pallas_call x10, Pallas kernels, exchange(): pl.pallas_call(functools.partial(kernel, axis_name, count), out_shape=jax...  142 us
    ppermute x16, waiting for transfers between devices, swap(): return lax.ppermute(piece, axis_name, [(i, i ^ step) for i in range(count)])  104 us
    dot_general x12, matrix products, dot(): lax.dot_general(a, b, (contract, ((), ())), preferred_element_type=F32)  33.4 us
    ppermute x16, starting transfers between devices, swap(): return lax.ppermute(piece, axis_name, [(i, i ^ step) for i in range(count)])  19 us
    ppermute x14, starting transfers between devices, shifted(): lax.ppermute(value, axis_name, [(i, (i + step) % count) for i in range(co...  13.1 us
    unnamed x83, local copies, waits for them, and re-layouts  11.8 us
    ppermute x14, waiting for transfers between devices, shifted(): lax.ppermute(value, axis_name, [(i, (i + step) % count) for i in range(co...  11.6 us
    pallas_call x2, Pallas kernels, local_call(): pl.pallas_call(kernel, in_specs=[whole] * len(operands), out_specs=[whole...  10.1 us
  transfers between devices with their start and end apart: 38, of which 17 were waited for; matrix products, arithmetic and copies ran while one was open for 19% of the time, Pallas kernels for 33%

profile of v2, /device:TPU:0, one launch (start us, length us, event | category | flops | bytes accessed | tf_op | source)
XLA Modules:
  0.0 413.5 jit_solution(11924555585217359983)
XLA Ops:
  2.9 3.0 collective-permute-start
  6.0 1.9 collective-permute-start.2
  8.3 2.3 constant_dynamic-update-slice_fusion.3
  13.3 16.3 %shard_map.254 = bf16[4,128,1024]{2,1,0:T(8,128)(2,1)} custom-call(bf16[128,1024]{1,0:T(8,128)(2,1)} %fusion.19.x_ref), custom_call_target="tpu_custom_call" | custom-call | bytes 10000000 | tf_op jit(solution)/shard_map/pallas_call | solution.py:173
  29.9 1.7 constant_dynamic-update-slice_fusion.1
  31.6 2.3 constant_dynamic-update-slice_fusion.5
  34.2 1.7 constant_dynamic-update-slice_fusion
  35.9 3.0 add_convert_fusion
  38.9 2.0 reshape.202
  42.9 18.5 %shard_map.255.qkv_ref = bf16[4,256,384]{2,1,0:T(8,128)(2,1)} custom-call(bf16[4,256,384]{2,1,0:T(8,128)(2,1)} %reshape.203.x_ref), custom_call_target="tpu_custom_call" | custom-call | bytes 10000000 | tf_op jit(solution)/shard_map/pallas_call | solution.py:173
  62.5 3.5 shard_map.256
  66.8 12.5 %shard_map.257 = bf16[4,256,128]{2,1,0:T(8,128)(2,1)} custom-call(bf16[4,256,128]{2,1,0:T(8,128)(2,1)} %copy-done.6), custom_call_target="tpu_custom_call" | custom-call | bytes 10000000 | tf_op jit(solution)/shard_map/pallas_call | solution.py:173
  80.7 2.5 convolution_convert_fusion.1.x_ref
  83.1 13.7 %shard_map.258 = bf16[4,128,1024]{2,1,0:T(8,128)(2,1)} custom-call(bf16[4,128,1024]{2,1,0:T(8,128)(2,1)} %convolution_convert_fusion.1.x_ref), custom_call_target="tpu_custom_call" | custom-call | bytes 10000000 | tf_op jit(solution)/shard_map/pallas_call | solution.py:173
  99.5 15.1 %shard_map.259 = bf16[4,128,1024]{2,1,0:T(8,128)(2,1)} custom-call(bf16[128,1024]{1,0:T(8,128)(2,1)} %add_convert_fusion.1.x_ref), custom_call_target="tpu_custom_call" | custom-call | bytes 10000000 | tf_op jit(solution)/shard_map/pallas_call | solution.py:173
  114.6 2.4 constant_dynamic-update-slice_fusion.2
  117.0 3.0 fusion.69
  120.1 2.1 constant_dynamic-update-slice_fusion.4
  122.2 3.2 fusion.68
  125.4 3.8 convert_reduce_fusion.4
  129.2 2.3 convolution_convert_fusion
  131.5 3.5 fusion.71
  135.0 13.7 %shard_map.260 = bf16[4,128,1024]{2,1,0:T(8,128)(2,1)} custom-call(bf16[4,128,1024]{2,1,0:T(8,128)(2,1)} %bitcast.94), custom_call_target="tpu_custom_call" | custom-call | bytes 10000000 | tf_op jit(solution)/shard_map/pallas_call | solution.py:173
  148.7 1.7 convert_reduce_fusion.2
  150.7 2.0 collective-permute-start.6
  153.2 2.7 split.105
  157.4 2.7 fusion.40
  162.0 3.5 collective-permute-done.5
  165.5 2.1 fusion.61
  169.1 14.7 %shard_map.261 = bf16[4,128,1024]{2,1,0:T(8,128)(2,1)} custom-call(bf16[128,1024]{1,0:T(8,128)(2,1)} %convert_element_type.173.x_ref), custom_call_target="tpu_custom_call" | custom-call | bytes 10000000 | tf_op jit(solution)/shard_map/pallas_call | solution.py:173
  183.7 1.8 convolution_convert_fusion.2
  186.4 8.4 %shard_map.262.ga_ref = bf16[4,256,128]{2,1,0:T(8,128)(2,1)} custom-call(bf16[4,256,128]{2,1,0:T(8,128)(2,1)} %bitcast.96), custom_call_target="tpu_custom_call" | custom-call | bytes 10000000 | tf_op jit(solution)/shard_map/pallas_call | solution.py:173
  195.8 6.5 %shard_map.263.x_ref = bf16[4,256,384]{2,1,0:T(8,128)(2,1)S(1)} custom-call(bf16[4,256,384]{2,1,0:T(8,128)(2,1)S(1)} %copy-done.3, bf16[4,256,128]{2,1,0:T(8,128)(2,1)S(1)} %copy-done.5, f32[8,256]{1,0:T(8,128)S(1)} %get-tuple-element.17.log_ref, s32[4,256]{1,0:T(4,128)S(1)} %get-tuple-element.71.qpos_ref, s32[4,256]{1,0:T(4,128)S(1)} %reshape.205.qseg_ref, ...), custom_call_target="tpu_custom_call" | custom-call | flops 4000000000 | bytes 8000000 | tf_op jit(solution)/shard_map/pallas_call | solution.py:277
  203.2 16.6 %shard_map.264 = bf16[4,256,384]{2,1,0:T(8,128)(2,1)} custom-call(bf16[4,256,384]{2,1,0:T(8,128)(2,1)} %copy-done.4), custom_call_target="tpu_custom_call" | custom-call | bytes 10000000 | tf_op jit(solution)/shard_map/pallas_call | solution.py:173
  219.8 2.7 reshape.213
  226.8 3.4 fusion.9.x_ref
  230.1 12.5 %shard_map.265 = bf16[4,128,1024]{2,1,0:T(8,128)(2,1)} custom-call(bf16[4,128,1024]{2,1,0:T(8,128)(2,1)} %fusion.9.x_ref), custom_call_target="tpu_custom_call" | custom-call | bytes 10000000 | tf_op jit(solution)/shard_map/pallas_call | solution.py:173
  242.7 1.7 convert_reduce_fusion
  245.6 1.6 collective-permute-start.10
  247.2 2.5 fusion.70
  250.3 1.8 fusion.37
  252.1 1.7 collective-permute-start.23
  253.8 3.8 collective-permute-start.11
  261.1 3.7 collective-permute-start.24
  265.0 3.8 collective-permute-done.24
  268.9 1.7 collective-permute-start.25
  281.2 2.4 collective-permute-start.27
  284.2 2.3 collective-permute-done.27
  287.4 8.1 %collective-permute-done.15 = bf16[512,768]{1,0:T(8,128)(2,1)} collective-permute-done((bf16[512,768]{1,0:T(8,128)(2,1)}, bf16[512,768]{1,0:T(8,128)(2,1)}, u32[]{:S(2)}, u32[]{:S(2)}) %collective-permute-start.15) | collective-permute-done | bytes 786464 | tf_op jit(solution)/shard_map/ppermute | solution.py:40
  296.9 2.1 collective-permute-start.16
  299.0 1.7 slice_add_fusion.1
  302.7 1.9 collective-permute-start.34
  304.6 6.5 %collective-permute-done.16 = bf16[256,768]{1,0:T(8,128)(2,1)S(1)} collective-permute-done((bf16[256,768]{1,0:T(8,128)(2,1)S(1)}, bf16[256,768]{1,0:T(8,128)(2,1)S(1)}, u32[]{:S(2)}, u32[]{:S(2)}) %collective-permute-start.16) | collective-permute-done | bytes 393248 | tf_op jit(solution)/shard_map/ppermute | solution.py:69
  312.0 15.3 %collective-permute-done.29 = bf16[256,1024]{1,0:T(8,128)(2,1)S(1)} collective-permute-done((bf16[256,1024]{1,0:T(8,128)(2,1)S(1)}, bf16[256,1024]{1,0:T(8,128)(2,1)S(1)}, u32[]{:S(2)}, u32[]{:S(2)}) %collective-permute-start.29) | collective-permute-done | bytes 524320 | tf_op jit(solution)/shard_map/ppermute | solution.py:69
  328.3 6.8 %collective-permute-done.34 = bf16[512,512]{1,0:T(8,128)(2,1)S(1)} collective-permute-done((bf16[512,512]{1,0:T(8,128)(2,1)S(1)}, bf16[512,512]{1,0:T(8,128)(2,1)S(1)}, u32[]{:S(2)}, u32[]{:S(2)}) %collective-permute-start.34) | collective-permute-done | bytes 524320 | tf_op jit(solution)/shard_map/ppermute | solution.py:69
  336.3 2.6 collective-permute-start.18
  338.9 17.2 %collective-permute-done.30 = bf16[128,1024]{1,0:T(8,128)(2,1)S(1)} collective-permute-done((bf16[128,1024]{1,0:T(8,128)(2,1)S(1)}, bf16[128,1024]{1,0:T(8,128)(2,1)S(1)}, u32[]{:S(2)}, u32[]{:S(2)}) %collective-permute-start.30) | collective-permute-done | bytes 262176 | tf_op jit(solution)/shard_map/ppermute | solution.py:69
  356.2 11.1 %collective-permute-done.35 = bf16[256,512]{1,0:T(8,128)(2,1)S(1)} collective-permute-done((bf16[256,512]{1,0:T(8,128)(2,1)S(1)}, bf16[256,512]{1,0:T(8,128)(2,1)S(1)}, u32[]{:S(2)}, u32[]{:S(2)}) %collective-permute-start.35) | collective-permute-done | bytes 262176 | tf_op jit(solution)/shard_map/ppermute | solution.py:69
  367.4 4.2 %collective-permute-done.18 = bf16[128,768]{1,0:T(8,128)(2,1)S(1)} collective-permute-done((bf16[128,768]{1,0:T(8,128)(2,1)S(1)}, bf16[128,768]{1,0:T(8,128)(2,1)S(1)}, u32[]{:S(2)}, u32[]{:S(2)}) %collective-permute-start.18) | collective-permute-done | bytes 196640 | tf_op jit(solution)/shard_map/ppermute | solution.py:69
  371.9 8.1 %collective-permute-done.31 = bf16[128,1024]{1,0:T(8,128)(2,1)S(1)} collective-permute-done((bf16[128,1024]{1,0:T(8,128)(2,1)S(1)}, bf16[128,1024]{1,0:T(8,128)(2,1)S(1)}, u32[]{:S(2)}, u32[]{:S(2)}) %collective-permute-start.31) | collective-permute-done | bytes 262176 | tf_op jit(solution)/shard_map/ppermute | solution.py:69
  380.2 3.1 collective-permute-done.36
  383.4 7.5 %collective-permute-done.19 = bf16[256,768]{1,0:T(8,128)(2,1)S(1)} collective-permute-done((bf16[256,768]{1,0:T(8,128)(2,1)S(1)}, bf16[256,768]{1,0:T(8,128)(2,1)S(1)}, u32[]{:S(2)}, u32[]{:S(2)}) %collective-permute-start.19) | collective-permute-done | bytes 393248 | tf_op jit(solution)/shard_map/ppermute | solution.py:69
  392.5 9.6 %collective-permute-done.32 = bf16[256,1024]{1,0:T(8,128)(2,1)S(1)} collective-permute-done((bf16[256,1024]{1,0:T(8,128)(2,1)S(1)}, bf16[256,1024]{1,0:T(8,128)(2,1)S(1)}, u32[]{:S(2)}, u32[]{:S(2)}) %collective-permute-start.32) | collective-permute-done | bytes 524320 | tf_op jit(solution)/shard_map/ppermute | solution.py:69
  404.0 7.3 %collective-permute-done.37 = bf16[512,512]{1,0:T(8,128)(2,1)S(1)} collective-permute-done((bf16[512,512]{1,0:T(8,128)(2,1)S(1)}, bf16[512,512]{1,0:T(8,128)(2,1)S(1)}, u32[]{:S(2)}, u32[]{:S(2)}) %collective-permute-start.37) | collective-permute-done | bytes 524320 | tf_op jit(solution)/shard_map/ppermute | solution.py:69
  (236 shorter events, 56.5 us)
Async XLA Ops:
  0.6 10.5 %copy-start = (s32[2,1024]{1,0:T(2,128)S(1)}, s32[2,1024]{1,0:T(2,128)}, u32[]{:S(2)}) copy-start(s32[2,1024]{1,0:T(2,128)} %param.16) | copy-start | bytes 24580
  0.7 7.4 %copy-start.27 = (bf16[2,64,1024]{2,1,0:T(8,128)(2,1)S(1)}, bf16[2,64,1024]{2,1,0:T(8,128)(2,1)}, u32[]{:S(2)}) copy-start(bf16[2,64,1024]{2,1,0:T(8,128)(2,1)} %param.29) | copy-start | bytes 786436
  1.9 34.0 %copy-start.18 = (bf16[512,256]{1,0:T(8,128)(2,1)}, bf16[512,256]{1,0:T(8,128)(2,1)S(1)}, u32[]{:S(2)}) copy-start(bf16[512,256]{1,0:T(8,128)(2,1)S(1)} %get-tuple-element.48) | copy-start | bytes 786436
  1.9 34.0 %copy-start.20 = (bf16[512,256]{1,0:T(8,128)(2,1)}, bf16[512,256]{1,0:T(8,128)(2,1)S(1)}, u32[]{:S(2)}) copy-start(bf16[512,256]{1,0:T(8,128)(2,1)S(1)} %get-tuple-element.49) | copy-start | bytes 786436
  1.9 34.0 %copy-start.22 = (bf16[512,256]{1,0:T(8,128)(2,1)}, bf16[512,256]{1,0:T(8,128)(2,1)S(1)}, u32[]{:S(2)}) copy-start(bf16[512,256]{1,0:T(8,128)(2,1)S(1)} %get-tuple-element.50) | copy-start | bytes 786436
  1.9 8.6 %copy-start.28 = (bf16[2,64,1024]{2,1,0:T(8,128)(2,1)S(1)}, bf16[2,64,1024]{2,1,0:T(8,128)(2,1)}, u32[]{:S(2)}) copy-start(bf16[2,64,1024]{2,1,0:T(8,128)(2,1)} %param.15) | copy-start | bytes 786436
  2.9 8.4 %copy-start.32 = (f32[1024]{0:T(1024)S(1)}, f32[1024]{0:T(1024)}, u32[]{:S(2)}) copy-start(f32[1024]{0:T(1024)} %param.22) | copy-start | bytes 12292
  2.9 8.4 %copy-start.33 = (f32[1024]{0:T(1024)S(1)}, f32[1024]{0:T(1024)}, u32[]{:S(2)}) copy-start(f32[1024]{0:T(1024)} %param.18) | copy-start | bytes 12292
  2.9 8.6 %copy-start.34 = (f32[1024]{0:T(1024)S(1)}, f32[1024]{0:T(1024)}, u32[]{:S(2)}) copy-start(f32[1024]{0:T(1024)} %param.24) | copy-start | bytes 12292
  2.9 8.6 %copy-start.35 = (f32[1024]{0:T(1024)S(1)}, f32[1024]{0:T(1024)}, u32[]{:S(2)}) copy-start(f32[1024]{0:T(1024)} %param.23) | copy-start | bytes 12292
  2.9 8.7 %copy-start.29 = (f32[1024]{0:T(1024)S(1)}, f32[1024]{0:T(1024)}, u32[]{:S(2)}) copy-start(f32[1024]{0:T(1024)} %param.17) | copy-start | bytes 12292
  2.9 9.7 %copy-start.30 = (f32[1024]{0:T(1024)S(1)}, f32[1024]{0:T(1024)}, u32[]{:S(2)}) copy-start(f32[1024]{0:T(1024)} %param.28) | copy-start | bytes 12292
  2.9 33.0 %collective-permute-start = (bf16[512,768]{1,0:T(8,128)(2,1)}, bf16[512,768]{1,0:T(8,128)(2,1)}, u32[]{:S(2)}, u32[]{:S(2)}) collective-permute-start(bf16[512,768]{1,0:T(8,128)(2,1)} %pad_maximum_fusion.3), channel_id=1, source_target_pairs={{0,16},{16,0},{1,17},{17,1},{2,18},{18,2},{3,19},{19,3},{4,20},{20... | collective-permute-start | bytes 2359304 | tf_op jit(solution)/shard_map/ppermute | solution.py:40
  5.9 27.9 %collective-permute-start.1 = (bf16[256,512]{1,0:T(8,128)(2,1)}, bf16[256,512]{1,0:T(8,128)(2,1)}, u32[]{:S(2)}, u32[]{:S(2)}) collective-permute-start(bf16[256,512]{1,0:T(8,128)(2,1)} %param.21), channel_id=1, source_target_pairs={{0,16},{16,0},{1,17},{17,1},{2,18},{18,2},{3,19},{19,3},{4,20},{20... | collective-permute-start | bytes 786440 | tf_op jit(solution)/shard_map/ppermute | solution.py:40
  6.0 108.6 %collective-permute-start.2 = (bf16[512,1024]{1,0:T(8,128)(2,1)}, bf16[512,1024]{1,0:T(8,128)(2,1)}, u32[]{:S(2)}, u32[]{:S(2)}) collective-permute-start(bf16[512,1024]{1,0:T(8,128)(2,1)} %param.25), channel_id=1, source_target_pairs={{0,16},{16,0},{1,17},{17,1},{2,18},{18,2},{3,19},{19,3},{4,20},{20... | collective-permute-start | bytes 3145736 | tf_op jit(solution)/shard_map/ppermute | solution.py:40
  7.9 112.1 %collective-permute-start.3 = (bf16[1024,512]{1,0:T(8,128)(2,1)}, bf16[1024,512]{1,0:T(8,128)(2,1)}, u32[]{:S(2)}, u32[]{:S(2)}) collective-permute-start(bf16[1024,512]{1,0:T(8,128)(2,1)} %param.27), channel_id=1, source_target_pairs={{0,16},{16,0},{1,17},{17,1},{2,18},{18,2},{3,19},{19,3},{4,20},{20... | collective-permute-start | bytes 3145736 | tf_op jit(solution)/shard_map/ppermute | solution.py:40
  8.2 117.2 %collective-permute-start.9 = (bf16[128,1024]{1,0:T(8,128)(2,1)S(1)}, bf16[128,1024]{1,0:T(8,128)(2,1)}, u32[]{:S(2)}, u32[]{:S(2)}) collective-permute-start(bf16[128,1024]{1,0:T(8,128)(2,1)S(1)} %get-tuple-element.29), channel_id=1, source_target_pairs={{0,1},{1,2},{2,3},{3,0},{4,5},{5,6},{6,7},{7,4},{8,9},{9,10},{10,1... | collective-permute-start | bytes 786440 | tf_op jit(solution)/shard_map/ppermute | solution.py:40
  10.5 19.0 %copy-start.31 = (f32[3,256]{1,0:T(4,128)S(1)}, f32[3,256]{1,0:T(4,128)}, u32[]{:S(2)}) copy-start(f32[3,256]{1,0:T(4,128)} %param.20) | copy-start | bytes 9220
  29.6 6.3 %copy-start.8 = (bf16[4,128,1024]{2,1,0:T(8,128)(2,1)S(1)}, bf16[4,128,1024]{2,1,0:T(8,128)(2,1)}, u32[]{:S(2)}) copy-start(bf16[4,128,1024]{2,1,0:T(8,128)(2,1)} %shard_map.254) | copy-start | bytes 3145732
  33.9 91.5 %collective-permute-start.8 = (bf16[128,1024]{1,0:T(8,128)(2,1)S(1)}, bf16[128,1024]{1,0:T(8,128)(2,1)}, u32[]{:S(2)}, u32[]{:S(2)}) collective-permute-start(bf16[128,1024]{1,0:T(8,128)(2,1)S(1)} %get-tuple-element.29), channel_id=1, source_target_pairs={{0,2},{1,3},{2,0},{3,1},{4,6},{5,7},{6,4},{7,5},{8,10},{9,11},{10,... | collective-permute-start | bytes 786440 | tf_op jit(solution)/shard_map/ppermute | solution.py:40
  35.9 89.5 %collective-permute-start.7 = (bf16[128,1024]{1,0:T(8,128)(2,1)S(1)}, bf16[128,1024]{1,0:T(8,128)(2,1)}, u32[]{:S(2)}, u32[]{:S(2)}) collective-permute-start(bf16[128,1024]{1,0:T(8,128)(2,1)S(1)} %get-tuple-element.29), channel_id=1, source_target_pairs={{0,3},{1,0},{2,1},{3,2},{4,7},{5,4},{6,5},{7,6},{8,11},{9,8},{10,9... | collective-permute-start | bytes 786440 | tf_op jit(solution)/shard_map/ppermute | solution.py:40
  80.5 16.3 %copy-start.14 = (bf16[2,2,4,64,1,128]{5,1,3,0,2,4:T(2,128)(2,1)}, bf16[2,2,4,64,1,128]{5,1,3,0,2,4:T(2,128)(2,1)S(1)}, u32[]{:S(2)}) copy-start(bf16[2,2,4,64,1,128]{5,1,3,0,2,4:T(2,128)(2,1)S(1)} %copy.82) | copy-start | bytes 786436
  120.0 5.4 %copy-start.37 = (f32[512,1024]{1,0:T(8,128)}, f32[512,1024]{1,0:T(8,128)S(1)}, u32[]{:S(2)}) copy-start(f32[512,1024]{1,0:T(8,128)S(1)} %fusion.69) | copy-start | bytes 6291460
  125.4 3.8 copy-start.25
  135.0 15.6 %copy-start.24 = (bf16[512,1024]{1,0:T(8,128)(2,1)S(1)}, bf16[512,1024]{1,0:T(8,128)(2,1)}, u32[]{:S(2)}) copy-start(bf16[512,1024]{1,0:T(8,128)(2,1)} %get-tuple-element.72) | copy-start | bytes 3145732
  150.6 6.8 %copy-start.38 = (f32[512,1024]{1,0:T(8,128)S(1)}, f32[512,1024]{1,0:T(8,128)}, u32[]{:S(2)}) copy-start(f32[512,1024]{1,0:T(8,128)} %copy-done.37) | copy-start | bytes 6291460
  150.7 11.3 %collective-permute-start.6 = (bf16[128,1024]{1,0:T(8,128)(2,1)S(1)}, bf16[128,1024]{1,0:T(8,128)(2,1)S(1)}, u32[]{:S(2)}, u32[]{:S(2)}) collective-permute-start(bf16[128,1024]{1,0:T(8,128)(2,1)S(1)} %get-tuple-element.44), channel_id=1, source_target_pairs={{0,3},{1,0},{2,1},{3,2},{4,7},{5,4},{6,5},{7,6},{8,11},{9,8},{10,9... | collective-permute-start | bytes 786440 | tf_op jit(solution)/shard_map/ppermute | solution.py:40
  152.6 12.8 %collective-permute-start.5 = (bf16[128,1024]{1,0:T(8,128)(2,1)S(1)}, bf16[128,1024]{1,0:T(8,128)(2,1)S(1)}, u32[]{:S(2)}, u32[]{:S(2)}) collective-permute-start(bf16[128,1024]{1,0:T(8,128)(2,1)S(1)} %get-tuple-element.45), channel_id=1, source_target_pairs={{0,2},{1,3},{2,0},{3,1},{4,6},{5,7},{6,4},{7,5},{8,10},{9,11},{10,... | collective-permute-start | bytes 786440 | tf_op jit(solution)/shard_map/ppermute | solution.py:40
  153.2 12.3 %collective-permute-start.4 = (bf16[128,1024]{1,0:T(8,128)(2,1)S(1)}, bf16[128,1024]{1,0:T(8,128)(2,1)S(1)}, u32[]{:S(2)}, u32[]{:S(2)}) collective-permute-start(bf16[128,1024]{1,0:T(8,128)(2,1)S(1)} %get-tuple-element.43), channel_id=1, source_target_pairs={{0,1},{1,2},{2,3},{3,0},{4,5},{5,6},{6,7},{7,4},{8,9},{9,10},{10,1... | collective-permute-start | bytes 786440 | tf_op jit(solution)/shard_map/ppermute | solution.py:40
  155.9 143.1 %collective-permute-start.28 = (bf16[512,1024]{1,0:T(8,128)(2,1)}, bf16[512,1024]{1,0:T(8,128)(2,1)}, u32[]{:S(2)}, u32[]{:S(2)}) collective-permute-start(bf16[512,1024]{1,0:T(8,128)(2,1)} %split.105), channel_id=1, source_target_pairs={{0,16},{16,0},{1,17},{17,1},{2,18},{18,2},{3,19},{19,3},{4,20},{20... | collective-permute-start | bytes 3145736 | tf_op jit(solution)/shard_map/ppermute | solution.py:40
  160.1 7.4 %copy-start.15 = (f32[1024,1024]{1,0:T(8,128)}, f32[1024,1024]{1,0:T(8,128)S(1)}, u32[]{:S(2)}) copy-start(f32[1024,1024]{1,0:T(8,128)S(1)} %fusion.40) | copy-start | bytes 12582916
  161.5 139.5 %collective-permute-start.33 = (bf16[1024,512]{1,0:T(8,128)(2,1)}, bf16[1024,512]{1,0:T(8,128)(2,1)}, u32[]{:S(2)}, u32[]{:S(2)}) collective-permute-start(bf16[1024,512]{1,0:T(8,128)(2,1)} %split.104), channel_id=1, source_target_pairs={{0,16},{16,0},{1,17},{17,1},{2,18},{18,2},{3,19},{19,3},{4,20},{20... | collective-permute-start | bytes 3145736 | tf_op jit(solution)/shard_map/ppermute | solution.py:40
  169.1 25.8 %copy-start.3 = (bf16[4,256,384]{2,1,0:T(8,128)(2,1)S(1)}, bf16[4,256,384]{2,1,0:T(8,128)(2,1)}, u32[]{:S(2)}) copy-start(bf16[4,256,384]{2,1,0:T(8,128)(2,1)} %shard_map.255.qkv_ref) | copy-start | bytes 2359300
  245.6 8.2 %collective-permute-start.10 = (f32[6,1024]{1,0:T(8,128)S(1)}, f32[6,1024]{1,0:T(8,128)S(1)}, u32[]{:S(2)}, u32[]{:S(2)}) collective-permute-start(f32[6,1024]{1,0:T(8,128)S(1)} %fusion.42), channel_id=1, source_target_pairs={{0,16},{16,0},{1,17},{17,1},{2,18},{18,2},{3,19},{19,3},{4,20},{20... | collective-permute-start | bytes 73736 | tf_op jit(solution)/shard_map/ppermute | solution.py:203
  249.7 7.8 %copy-start.11 = (f32[128,1024]{1,0:T(8,128)S(1)}, f32[128,1024]{1,0:T(8,128)}, u32[]{:S(2)}) copy-start(f32[128,1024]{1,0:T(8,128)} %copy-done.10) | copy-start | bytes 1572868
  249.7 7.8 %copy-start.13 = (f32[128,1024]{1,0:T(8,128)S(1)}, f32[128,1024]{1,0:T(8,128)}, u32[]{:S(2)}) copy-start(f32[128,1024]{1,0:T(8,128)} %copy-done.12) | copy-start | bytes 1572868
  249.7 15.1 %collective-permute-start.20 = (f32[1792]{0:T(1024)S(1)}, f32[1792]{0:T(1024)S(1)}, u32[]{:S(2)}, u32[]{:S(2)}) collective-permute-start(f32[1792]{0:T(1024)S(1)} %pad_maximum_fusion.14), channel_id=1, source_target_pairs={{0,16},{16,0},{1,17},{17,1},{2,18},{18,2},{3,19},{19,3},{4,20},{20... | collective-permute-start | bytes 21512 | tf_op jit(solution)/shard_map/ppermute | solution.py:203
  252.1 8.9 %collective-permute-start.23 = (bf16[256,512]{1,0:T(8,128)(2,1)S(1)}, bf16[256,512]{1,0:T(8,128)(2,1)S(1)}, u32[]{:S(2)}, u32[]{:S(2)}) collective-permute-start(bf16[256,512]{1,0:T(8,128)(2,1)S(1)} %split.107), channel_id=1, source_target_pairs={{0,16},{16,0},{1,17},{17,1},{2,18},{18,2},{3,19},{19,3},{4,20},{20... | collective-permute-start | bytes 786440 | tf_op jit(solution)/shard_map/ppermute | solution.py:40
  253.8 5.7 %collective-permute-start.11 = (f32[6,1024]{1,0:T(8,128)S(1)}, f32[6,1024]{1,0:T(8,128)S(1)}, u32[]{:S(2)}, u32[]{:S(2)}) collective-permute-start(f32[6,1024]{1,0:T(8,128)S(1)} %fusion.88), channel_id=1, source_target_pairs={{0,4},{4,0},{8,12},{12,8},{1,5},{5,1},{9,13},{13,9},{2,6},{6,2},{1... | collective-permute-start | bytes 73736 | tf_op jit(solution)/shard_map/ppermute | solution.py:203
  257.8 18.1 %copy-start.17 = (bf16[128,1024]{1,0:T(8,128)(2,1)S(1)}, bf16[128,1024]{1,0:T(8,128)(2,1)}, u32[]{:S(2)}) copy-start(bf16[128,1024]{1,0:T(8,128)(2,1)} %get-tuple-element.55) | copy-start | bytes 786436
  259.4 5.5 %collective-permute-start.12 = (f32[6,1024]{1,0:T(8,128)S(1)}, f32[6,1024]{1,0:T(8,128)S(1)}, u32[]{:S(2)}, u32[]{:S(2)}) collective-permute-start(f32[6,1024]{1,0:T(8,128)S(1)} %add.302), channel_id=1, source_target_pairs={{0,8},{4,12},{8,0},{12,4},{1,9},{5,13},{9,1},{13,5},{2,10},{6,14},... | collective-permute-start | bytes 73736 | tf_op jit(solution)/shard_map/ppermute | solution.py:203
  261.1 7.7 %collective-permute-start.24 = (bf16[128,512]{1,0:T(8,128)(2,1)S(1)}, bf16[128,512]{1,0:T(8,128)(2,1)S(1)}, u32[]{:S(2)}, u32[]{:S(2)}) collective-permute-start(bf16[128,512]{1,0:T(8,128)(2,1)S(1)} %dynamic-slice_convert_fusion.6), channel_id=1, source_target_pairs={{0,4},{4,0},{8,12},{12,8},{1,5},{5,1},{9,13},{13,9},{2,6},{6,2},{1... | collective-permute-start | bytes 393224 | tf_op jit(solution)/shard_map/ppermute | solution.py:69
  264.9 6.6 %collective-permute-start.21 = (f32[1792]{0:T(1024)S(1)}, f32[1792]{0:T(1024)S(1)}, u32[]{:S(2)}, u32[]{:S(2)}) collective-permute-start(f32[1792]{0:T(1024)S(1)} %fusion.58), channel_id=1, source_target_pairs={{0,4},{4,0},{8,12},{12,8},{1,5},{5,1},{9,13},{13,9},{2,6},{6,2},{1... | collective-permute-start | bytes 21512 | tf_op jit(solution)/shard_map/ppermute | solution.py:203
  265.0 7.8 %collective-permute-start.13 = (f32[6,1024]{1,0:T(8,128)S(1)}, f32[6,1024]{1,0:T(8,128)S(1)}, u32[]{:S(2)}, u32[]{:S(2)}) collective-permute-start(f32[6,1024]{1,0:T(8,128)S(1)} %add.303), channel_id=1, source_target_pairs={{0,1},{1,0},{2,3},{3,2},{4,5},{5,4},{6,7},{7,6},{8,9},{9,8},{10,11... | collective-permute-start | bytes 73736 | tf_op jit(solution)/shard_map/ppermute | solution.py:203
  268.9 5.5 %collective-permute-start.25 = (bf16[64,512]{1,0:T(8,128)(2,1)S(1)}, bf16[64,512]{1,0:T(8,128)(2,1)S(1)}, u32[]{:S(2)}, u32[]{:S(2)}) collective-permute-start(bf16[64,512]{1,0:T(8,128)(2,1)S(1)} %dynamic-slice_convert_fusion.7), channel_id=1, source_target_pairs={{0,8},{4,12},{8,0},{12,4},{1,9},{5,13},{9,1},{13,5},{2,10},{6,14},... | collective-permute-start | bytes 196616 | tf_op jit(solution)/shard_map/ppermute | solution.py:69
  271.4 6.3 %collective-permute-start.22 = (f32[1792]{0:T(1024)S(1)}, f32[1792]{0:T(1024)S(1)}, u32[]{:S(2)}, u32[]{:S(2)}) collective-permute-start(f32[1792]{0:T(1024)S(1)} %add.314), channel_id=1, source_target_pairs={{0,8},{4,12},{8,0},{12,4},{1,9},{5,13},{9,1},{13,5},{2,10},{6,14},... | collective-permute-start | bytes 21512 | tf_op jit(solution)/shard_map/ppermute | solution.py:203
  272.7 7.6 %collective-permute-start.14 = (f32[6,1024]{1,0:T(8,128)S(1)}, f32[6,1024]{1,0:T(8,128)S(1)}, u32[]{:S(2)}, u32[]{:S(2)}) collective-permute-start(f32[6,1024]{1,0:T(8,128)S(1)} %add.304), channel_id=1, source_target_pairs={{0,2},{1,3},{2,0},{3,1},{4,6},{5,7},{6,4},{7,5},{8,10},{9,11},{10,... | collective-permute-start | bytes 73736 | tf_op jit(solution)/shard_map/ppermute | solution.py:203
  274.4 5.9 %collective-permute-start.26 = (bf16[64,512]{1,0:T(8,128)(2,1)S(1)}, bf16[64,512]{1,0:T(8,128)(2,1)}, u32[]{:S(2)}, u32[]{:S(2)}) collective-permute-start(bf16[64,512]{1,0:T(8,128)(2,1)S(1)} %reduce-precision_convert_fusion.3), channel_id=1, source_target_pairs={{0,8},{4,12},{8,0},{12,4},{1,9},{5,13},{9,1},{13,5},{2,10},{6,14},... | collective-permute-start | bytes 196616 | tf_op jit(solution)/shard_map/ppermute | solution.py:69
  277.7 17.8 %collective-permute-start.15 = (bf16[512,768]{1,0:T(8,128)(2,1)}, bf16[512,768]{1,0:T(8,128)(2,1)}, u32[]{:S(2)}, u32[]{:S(2)}) collective-permute-start(bf16[512,768]{1,0:T(8,128)(2,1)} %split.106), channel_id=1, source_target_pairs={{0,16},{16,0},{1,17},{17,1},{2,18},{18,2},{3,19},{19,3},{4,20},{20... | collective-permute-start | bytes 2359304 | tf_op jit(solution)/shard_map/ppermute | solution.py:40
  281.2 5.3 %collective-permute-start.27 = (bf16[128,512]{1,0:T(8,128)(2,1)S(1)}, bf16[128,512]{1,0:T(8,128)(2,1)S(1)}, u32[]{:S(2)}, u32[]{:S(2)}) collective-permute-start(bf16[128,512]{1,0:T(8,128)(2,1)S(1)} %pad_maximum_fusion.13), channel_id=1, source_target_pairs={{0,4},{4,0},{8,12},{12,8},{1,5},{5,1},{9,13},{13,9},{2,6},{6,2},{1... | collective-permute-start | bytes 393224 | tf_op jit(solution)/shard_map/ppermute | solution.py:69
  287.4 11.6 %copy-start.7 = (f32[1024,1024]{1,0:T(8,128)S(1)}, f32[1024,1024]{1,0:T(8,128)}, u32[]{:S(2)}) copy-start(f32[1024,1024]{1,0:T(8,128)} %fusion.71) | copy-start | bytes 12582916
  296.9 4.1 copy-start.16
  296.9 14.2 %collective-permute-start.16 = (bf16[256,768]{1,0:T(8,128)(2,1)S(1)}, bf16[256,768]{1,0:T(8,128)(2,1)S(1)}, u32[]{:S(2)}, u32[]{:S(2)}) collective-permute-start(bf16[256,768]{1,0:T(8,128)(2,1)S(1)} %dynamic-slice_convert_fusion.2), channel_id=1, source_target_pairs={{0,4},{4,0},{8,12},{12,8},{1,5},{5,1},{9,13},{13,9},{2,6},{6,2},{1... | collective-permute-start | bytes 1179656 | tf_op jit(solution)/shard_map/ppermute | solution.py:69
  300.8 26.5 %collective-permute-start.29 = (bf16[256,1024]{1,0:T(8,128)(2,1)S(1)}, bf16[256,1024]{1,0:T(8,128)(2,1)S(1)}, u32[]{:S(2)}, u32[]{:S(2)}) collective-permute-start(bf16[256,1024]{1,0:T(8,128)(2,1)S(1)} %dynamic-slice_convert_fusion.1), channel_id=1, source_target_pairs={{0,4},{4,0},{8,12},{12,8},{1,5},{5,1},{9,13},{13,9},{2,6},{6,2},{1... | collective-permute-start | bytes 1572872 | tf_op jit(solution)/shard_map/ppermute | solution.py:69
  302.7 32.4 %collective-permute-start.34 = (bf16[512,512]{1,0:T(8,128)(2,1)S(1)}, bf16[512,512]{1,0:T(8,128)(2,1)S(1)}, u32[]{:S(2)}, u32[]{:S(2)}) collective-permute-start(bf16[512,512]{1,0:T(8,128)(2,1)S(1)} %dynamic-slice_convert_fusion), channel_id=1, source_target_pairs={{0,4},{4,0},{8,12},{12,8},{1,5},{5,1},{9,13},{13,9},{2,6},{6,2},{1... | collective-permute-start | bytes 1572872 | tf_op jit(solution)/shard_map/ppermute | solution.py:69
  311.3 25.0 %collective-permute-start.17 = (bf16[128,768]{1,0:T(8,128)(2,1)S(1)}, bf16[128,768]{1,0:T(8,128)(2,1)S(1)}, u32[]{:S(2)}, u32[]{:S(2)}) collective-permute-start(bf16[128,768]{1,0:T(8,128)(2,1)S(1)} %dynamic-slice_convert_fusion.5), channel_id=1, source_target_pairs={{0,8},{4,12},{8,0},{12,4},{1,9},{5,13},{9,1},{13,5},{2,10},{6,14},... | collective-permute-start | bytes 589832 | tf_op jit(solution)/shard_map/ppermute | solution.py:69
  327.5 28.6 %collective-permute-start.30 = (bf16[128,1024]{1,0:T(8,128)(2,1)S(1)}, bf16[128,1024]{1,0:T(8,128)(2,1)S(1)}, u32[]{:S(2)}, u32[]{:S(2)}) collective-permute-start(bf16[128,1024]{1,0:T(8,128)(2,1)S(1)} %dynamic-slice_convert_fusion.4), channel_id=1, source_target_pairs={{0,8},{4,12},{8,0},{12,4},{1,9},{5,13},{9,1},{13,5},{2,10},{6,14},... | collective-permute-start | bytes 786440 | tf_op jit(solution)/shard_map/ppermute | solution.py:69
  335.3 32.0 %collective-permute-start.35 = (bf16[256,512]{1,0:T(8,128)(2,1)S(1)}, bf16[256,512]{1,0:T(8,128)(2,1)S(1)}, u32[]{:S(2)}, u32[]{:S(2)}) collective-permute-start(bf16[256,512]{1,0:T(8,128)(2,1)S(1)} %dynamic-slice_convert_fusion.3), channel_id=1, source_target_pairs={{0,8},{4,12},{8,0},{12,4},{1,9},{5,13},{9,1},{13,5},{2,10},{6,14},... | collective-permute-start | bytes 786440 | tf_op jit(solution)/shard_map/ppermute | solution.py:69
  336.3 35.4 %collective-permute-start.18 = (bf16[128,768]{1,0:T(8,128)(2,1)S(1)}, bf16[128,768]{1,0:T(8,128)(2,1)S(1)}, u32[]{:S(2)}, u32[]{:S(2)}) collective-permute-start(bf16[128,768]{1,0:T(8,128)(2,1)S(1)} %reduce-precision_convert_fusion.2), channel_id=1, source_target_pairs={{0,8},{4,12},{8,0},{12,4},{1,9},{5,13},{9,1},{13,5},{2,10},{6,14},... | collective-permute-start | bytes 589832 | tf_op jit(solution)/shard_map/ppermute | solution.py:69
  356.1 23.9 %collective-permute-start.31 = (bf16[128,1024]{1,0:T(8,128)(2,1)S(1)}, bf16[128,1024]{1,0:T(8,128)(2,1)S(1)}, u32[]{:S(2)}, u32[]{:S(2)}) collective-permute-start(bf16[128,1024]{1,0:T(8,128)(2,1)S(1)} %reduce-precision_convert_fusion.1), channel_id=1, source_target_pairs={{0,8},{4,12},{8,0},{12,4},{1,9},{5,13},{9,1},{13,5},{2,10},{6,14},... | collective-permute-start | bytes 786440 | tf_op jit(solution)/shard_map/ppermute | solution.py:69
  367.4 15.9 %collective-permute-start.36 = (bf16[256,512]{1,0:T(8,128)(2,1)S(1)}, bf16[256,512]{1,0:T(8,128)(2,1)S(1)}, u32[]{:S(2)}, u32[]{:S(2)}) collective-permute-start(bf16[256,512]{1,0:T(8,128)(2,1)S(1)} %reduce-precision_convert_fusion), channel_id=1, source_target_pairs={{0,8},{4,12},{8,0},{12,4},{1,9},{5,13},{9,1},{13,5},{2,10},{6,14},... | collective-permute-start | bytes 786440 | tf_op jit(solution)/shard_map/ppermute | solution.py:69
  371.8 19.1 %collective-permute-start.19 = (bf16[256,768]{1,0:T(8,128)(2,1)S(1)}, bf16[256,768]{1,0:T(8,128)(2,1)S(1)}, u32[]{:S(2)}, u32[]{:S(2)}) collective-permute-start(bf16[256,768]{1,0:T(8,128)(2,1)S(1)} %pad_maximum_fusion.6), channel_id=1, source_target_pairs={{0,4},{4,0},{8,12},{12,8},{1,5},{5,1},{9,13},{13,9},{2,6},{6,2},{1... | collective-permute-start | bytes 1179656 | tf_op jit(solution)/shard_map/ppermute | solution.py:69
  380.1 22.0 %collective-permute-start.32 = (bf16[256,1024]{1,0:T(8,128)(2,1)S(1)}, bf16[256,1024]{1,0:T(8,128)(2,1)S(1)}, u32[]{:S(2)}, u32[]{:S(2)}) collective-permute-start(bf16[256,1024]{1,0:T(8,128)(2,1)S(1)} %pad_maximum_fusion.4), channel_id=1, source_target_pairs={{0,4},{4,0},{8,12},{12,8},{1,5},{5,1},{9,13},{13,9},{2,6},{6,2},{1... | collective-permute-start | bytes 1572872 | tf_op jit(solution)/shard_map/ppermute | solution.py:69
  383.4 27.9 %collective-permute-start.37 = (bf16[512,512]{1,0:T(8,128)(2,1)S(1)}, bf16[512,512]{1,0:T(8,128)(2,1)S(1)}, u32[]{:S(2)}, u32[]{:S(2)}) collective-permute-start(bf16[512,512]{1,0:T(8,128)(2,1)S(1)} %pad_maximum_fusion.5), channel_id=1, source_target_pairs={{0,4},{4,0},{8,12},{12,8},{1,5},{5,1},{9,13},{13,9},{2,6},{6,2},{1... | collective-permute-start | bytes 1572872 | tf_op jit(solution)/shard_map/ppermute | solution.py:69
  (13 other events, 23.9 us)

commit v3 on v2

--- a/solution.py
+++ b/solution.py
@@ -60,29 +60,36 @@
     return lax.reduce_precision(value, 8, 7).astype(BF16)
 
 
-def sum_everywhere(value, axis_name, axis):
-    count = lax.axis_size(axis_name)
-    index = lax.axis_index(axis_name)
+def weight_sum(full, dp_axis, ctx_axis):
+    dp_count = lax.axis_size("dp")
+    pieces = jnp.split(full, dp_count, axis=dp_axis)
+    sent = [piece.astype(BF16) for piece in pieces[1:]]
+    stages = [[shifted(piece, "dp", k + 1) for k, piece in enumerate(sent)]]
+    value = pieces[0]
+    for piece in stages[0]:
+        value = value + piece.astype(F32)
+    count = lax.axis_size("ctx")
+    index = lax.axis_index("ctx")
     steps = [1 << i for i in range(count.bit_length() - 1)]
 
     def swap(piece, step):
-        return lax.ppermute(piece, axis_name, [(i, i ^ step) for i in range(count)])
+        stages.append([lax.ppermute(piece, "ctx", [(i, i ^ step) for i in range(count)])])
+        return stages[-1][0]
 
     for step in steps:
         bit = lax.rem(index // step, 2)
-        size = value.shape[axis] // 2
-        other = lax.dynamic_slice_in_dim(value, (1 - bit) * size, size, axis).astype(BF16)
-        own = lax.dynamic_slice_in_dim(value, bit * size, size, axis)
+        size = value.shape[ctx_axis] // 2
+        other = lax.dynamic_slice_in_dim(value, (1 - bit) * size, size, ctx_axis).astype(BF16)
+        own = lax.dynamic_slice_in_dim(value, bit * size, size, ctx_axis)
         value = own + swap(other, step).astype(F32)
     value = rounded(value)
     for step in reversed(steps):
         bit = lax.rem(index // step, 2)
-        size = value.shape[axis]
         other = swap(value, step)
         low = jnp.where(bit == 0, value, other)
         high = jnp.where(bit == 0, other, value)
-        value = jnp.concatenate([low, high], axis=axis)
-    return value.astype(F32)
+        value = jnp.concatenate([low, high], axis=ctx_axis)
+    return value.astype(F32), sent, stages
 
 
 def greet(axis_name, count, index):
@@ -97,7 +104,8 @@
     pl.semaphore_wait(barrier, count - 1)
 
 
-def gather_kernel(axis_name, count, x_ref, o_ref, send_sem, recv_sem, own_sem):
+def gather_kernel(axis_name, count, x_ref, *refs):
+    o_ref, send_sem, recv_sem, own_sem = refs[-4:]
     index = lax.axis_index(axis_name)
     own = pltpu.make_async_copy(x_ref, o_ref.at[0], own_sem)
     own.start()
@@ -120,7 +128,8 @@
     own.wait()
 
 
-def scatter_kernel(axis_name, count, x_ref, o_ref, send_sem, recv_sem, own_sem):
+def scatter_kernel(axis_name, count, x_ref, *refs):
+    o_ref, send_sem, recv_sem, own_sem = refs[-4:]
     index = lax.axis_index(axis_name)
     own = pltpu.make_async_copy(x_ref.at[0], o_ref.at[0], own_sem)
     own.start()
@@ -143,7 +152,8 @@
     own.wait()
 
 
-def swap_kernel(axis_name, count, x_ref, o_ref, send_sem, recv_sem, own_sem):
+def swap_kernel(axis_name, count, x_ref, *refs):
+    o_ref, send_sem, recv_sem, own_sem = refs[-4:]
     index = lax.axis_index(axis_name)
     own = pltpu.make_async_copy(x_ref.at[index], o_ref.at[index], own_sem)
     own.start()
@@ -167,13 +177,13 @@
     own.wait()
 
 
-def exchange(kernel, value, axis_name, collective_id):
+def exchange(kernel, value, axis_name, collective_id, after=()):
     count = lax.axis_size(axis_name)
     shape = value.shape if value.ndim == 3 else (count,) + value.shape
     return pl.pallas_call(
         functools.partial(kernel, axis_name, count),
         out_shape=jax.ShapeDtypeStruct(shape, value.dtype),
-        in_specs=[pl.BlockSpec(memory_space=pl.ANY)],
+        in_specs=[pl.BlockSpec(memory_space=pl.ANY)] * (1 + len(after)),
         out_specs=pl.BlockSpec(memory_space=pl.ANY),
         scratch_shapes=[
             pltpu.SemaphoreType.DMA((count,)),
@@ -181,18 +191,19 @@
             pltpu.SemaphoreType.DMA,
         ],
         compiler_params=pltpu.CompilerParams(collective_id=collective_id, has_side_effects=True),
-        cost_estimate=pl.CostEstimate(flops=0, bytes_accessed=10 * 10**6, transcendentals=0),
-    )(value)
-
-
-def gathered(rows):
-    return exchange(gather_kernel, rows, "tp", 0).reshape(-1, rows.shape[1])
-
-
-def scattered_sum(partial_value):
+        cost_estimate=pl.CostEstimate(flops=0, bytes_accessed=50 * 10**6, transcendentals=0),
+    )(value, *after)
+
+
+def gathered(rows, collective_id, after=()):
+    return exchange(gather_kernel, rows, "tp", collective_id, after).reshape(-1, rows.shape[1])
+
+
+def scattered_sum(partial_value, collective_id, after=()):
     count = lax.axis_size("tp")
     pieces = partial_value.reshape(count, -1, partial_value.shape[1]).astype(BF16)
-    return jnp.sum(exchange(scatter_kernel, pieces, "tp", 1).astype(F32), axis=0)
+    received = exchange(scatter_kernel, pieces, "tp", collective_id, after)
+    return jnp.sum(received.astype(F32), axis=0)
 
 
 def sum_small(value, axis_names):
@@ -328,7 +339,7 @@
     ]
 
     normed_one, scaled_one, inverse_one = normalize(residual_in, ln1_gain, ln1_bias)
-    attn_rows = gathered(normed_one.astype(BF16))
+    attn_rows = gathered(normed_one.astype(BF16), 0)
     qkv_flat = jnp.concatenate([qkv_weight[:, c] for c in range(3)], axis=1)
     qkv_full = turned(qkv_flat, "dp", 0)
     out_full = turned(out_weight, "dp", 1)
@@ -373,10 +384,10 @@
         *places,
     )
     attended_flat = by_rows(exchange(swap_kernel, attended, "ctx", 3), 1)
-    branch = scattered_sum(dot(attended_flat, out_full, ((1,), (0,))))
+    branch = scattered_sum(dot(attended_flat, out_full, ((1,), (0,))), 1)
     middle = residual_in + branch + out_bias
     normed_two, scaled_two, inverse_two = normalize(middle, ln2_gain, ln2_bias)
-    mlp_rows = gathered(normed_two.astype(BF16))
+    mlp_rows = gathered(normed_two.astype(BF16), 0)
     upward = dot(mlp_rows, fc_full, ((1,), (0,))) + fc_bias
     hidden, gelu_back = jax.vjp(gelu_tanh, upward)
     hidden_low = hidden.astype(BF16)
@@ -384,25 +395,24 @@
     grad_hidden = dot(grad_rows, proj_full, ((1,), (1,)))
     grad_up = gelu_back(grad_hidden)[0].astype(BF16)
     fc_bias_part = jnp.sum(grad_up, axis=0, dtype=F32)
-    grad_normed_two = scattered_sum(dot(grad_up, fc_full, ((1,), (1,))))
+    proj_weight_grad, proj_sent, proj_stages = weight_sum(
+        dot(hidden_low, grad_rows, ((0,), (0,))), 1, 0
+    )
+    fc_weight_grad, fc_sent, fc_stages = weight_sum(dot(mlp_rows, grad_up, ((0,), (0,))), 0, 0)
+    grad_normed_two = scattered_sum(dot(grad_up, fc_full, ((1,), (1,))), 4, proj_sent)
     mlp_out = turned_sum(dot(hidden_low, proj_full, ((1,), (0,))), "tp", 0)
     block_out = turn((middle + mlp_out + proj_bias).astype(BF16), True)
 
-    def over_dp(full, axis):
-        return turned_sum(full, "dp", axis)
-
-    proj_grad = over_dp(dot(hidden_low, grad_rows, ((0,), (0,))), 1)
-    fc_grad = over_dp(dot(mlp_rows, grad_up, ((0,), (0,))), 0)
-    proj_weight_grad = sum_everywhere(proj_grad, "ctx", 0)
-    fc_weight_grad = sum_everywhere(fc_grad, "ctx", 0)
-
     grad_top = grad_low.astype(F32)
     grad_middle = grad_top + normalize_back(grad_normed_two, scaled_two, inverse_two, ln2_gain)
-    middle_rows = gathered(grad_middle.astype(BF16))
+    middle_rows = gathered(grad_middle.astype(BF16), 5, [*fc_sent, *proj_stages[0]])
     grad_attended = by_group(dot(middle_rows, out_full, ((1,), (1,))).astype(BF16), 1)
-    grad_attended = exchange(swap_kernel, grad_attended, "ctx", 3)
-    out_grad = over_dp(dot(attended_flat, middle_rows, ((0,), (0,))), 1)
-    out_weight_grad = sum_everywhere(out_grad, "ctx", 0)
+    grad_attended = exchange(
+        swap_kernel, grad_attended, "ctx", 6, [*fc_stages[0], *proj_stages[1]]
+    )
+    out_weight_grad, out_sent, out_stages = weight_sum(
+        dot(attended_flat, middle_rows, ((0,), (0,))), 1, 0
+    )
 
     (grad_groups,) = local_call(
         attend_back_kernel,
@@ -413,12 +423,18 @@
         log_totals,
         *places,
     )
-    grad_mixed = by_rows(exchange(swap_kernel, grad_groups, "ctx", 2), 3)
+    grad_groups = exchange(
+        swap_kernel, grad_groups, "ctx", 7, [*fc_stages[1], *proj_stages[2], *out_stages[0]]
+    )
+    grad_mixed = by_rows(grad_groups, 3)
     qkv_bias_part = jnp.sum(grad_mixed, axis=0, dtype=F32)
-    qkv_grad = over_dp(dot(attn_rows, grad_mixed, ((0,), (0,))), 0)
-    qkv_grad = sum_everywhere(qkv_grad, "ctx", 0)
+    qkv_grad, qkv_sent, _ = weight_sum(dot(attn_rows, grad_mixed, ((0,), (0,))), 0, 0)
     qkv_weight_grad = jnp.stack(jnp.split(qkv_grad, 3, axis=1), axis=1)
-    grad_normed_one = scattered_sum(dot(grad_mixed, qkv_full, ((1,), (1,))))
+    grad_normed_one = scattered_sum(
+        dot(grad_mixed, qkv_full, ((1,), (1,))),
+        8,
+        [*fc_stages[2], *proj_stages[3], *out_stages[1], *qkv_sent],
+    )
     tokens_grad = grad_middle + normalize_back(grad_normed_one, scaled_one, inverse_one, ln1_gain)
 
     shared = jnp.stack(

time: 419 us -> 404 us (0.964)
  waiting for transfers between devices: 117 us -> 68.6 us
  other arithmetic: 27.4 us -> 40 us
  local copies, waits for them, and re-layouts: 40 us -> 51.5 us
  starting transfers between devices: 41.4 us -> 50.6 us
    ppermute x16, waiting for transfers between devices: 104 us -> 42.7 us  [swap(): lax.ppermute(piece, 'ctx', [(i, i ^ step) for i in range(count)])]
    ppermute x8, waiting for transfers between devices: 1.61 us -> 21.7 us  [sum_small(): lax.ppermute(value, axis_name, [(i, i ^ step) for i in range(count)])]
    ppermute x14, waiting for transfers between devices: 11.6 us -> 4.22 us  [shifted(): lax.ppermute(value, axis_name, [(i, (i + step) % count) for i in range(co...]
    unnamed x83 -> x125, local copies, waits for them, and re-layouts: 11.8 us -> 18.2 us
    ppermute x8, starting transfers between devices: 9.32 us -> 14.9 us  [sum_small(): lax.ppermute(value, axis_name, [(i, i ^ step) for i in range(count)])]
    split x0 -> x4, local copies, waits for them, and re-layouts: none -> 4.85 us  [weight_sum(): pieces = jnp.split(full, dp_count, axis=dp_axis)]
    split x5 -> x1, local copies, waits for them, and re-layouts: 5.12 us -> 0.87 us  [turned_sum(): pieces = jnp.split(partial_value, count, axis=axis)]
  transfers between devices with their start and end apart: 38 -> 38, of which waited for: 17 -> 14; matrix products, arithmetic and copies ran while one was open for 19% -> 25% of each run, Pallas kernels for 33% -> 38%
where the time goes in v3:
time: 404 us; the launch traced here: 399 us
  Pallas kernels  152 us (38%)
  waiting for transfers between devices  68.6 us (17%)
  local copies, waits for them, and re-layouts  51.5 us (13%)
  starting transfers between devices  50.6 us (13%)
  other arithmetic  40 us (10%)
  matrix products  33.7 us (8%)
    pallas_call x10, Pallas kernels, exchange(): pl.pallas_call(functools.partial(kernel, axis_name, count), out_shape=jax...  142 us
    ppermute x16, waiting for transfers between devices, swap(): lax.ppermute(piece, 'ctx', [(i, i ^ step) for i in range(count)])  42.7 us
    dot_general x12, matrix products, dot(): lax.dot_general(a, b, (contract, ((), ())), preferred_element_type=F32)  33.7 us
    ppermute x8, waiting for transfers between devices, sum_small(): lax.ppermute(value, axis_name, [(i, i ^ step) for i in range(count)])  21.7 us
    ppermute x16, starting transfers between devices, swap(): lax.ppermute(piece, 'ctx', [(i, i ^ step) for i in range(count)])  19.5 us
    unnamed x125, local copies, waits for them, and re-layouts  18.2 us
    ppermute x14, starting transfers between devices, shifted(): lax.ppermute(value, axis_name, [(i, (i + step) % count) for i in range(co...  16.3 us
    ppermute x8, starting transfers between devices, sum_small(): lax.ppermute(value, axis_name, [(i, i ^ step) for i in range(count)])  14.9 us
  transfers between devices with their start and end apart: 38, of which 14 were waited for; matrix products, arithmetic and copies ran while one was open for 25% of the time, Pallas kernels for 38%

profile of v3, /device:TPU:0, one launch (start us, length us, event | category | flops | bytes accessed | tf_op | source)
XLA Modules:
  0.0 398.9 jit_solution(4697572730912952793)
XLA Ops:
  0.7 1.7 convert_reduce_fusion.8
  2.8 2.5 collective-permute-start.8
  11.8 2.3 constant_dynamic-update-slice_fusion.3
  16.8 14.7 %shard_map.254 = bf16[4,128,1024]{2,1,0:T(8,128)(2,1)} custom-call(bf16[128,1024]{1,0:T(8,128)(2,1)} %fusion.19.x_ref), custom_call_target="tpu_custom_call" | custom-call | bytes 50000000 | tf_op jit(solution)/shard_map/pallas_call | solution.py:183
  31.6 1.8 constant_dynamic-update-slice_fusion.1
  33.4 2.3 constant_dynamic-update-slice_fusion.5
  37.2 1.7 constant_dynamic-update-slice_fusion
  39.3 3.0 add_convert_fusion
  42.3 2.0 reshape.202
  46.3 15.0 %shard_map.255.qkv_ref = bf16[4,256,384]{2,1,0:T(8,128)(2,1)} custom-call(bf16[4,256,384]{2,1,0:T(8,128)(2,1)} %reshape.203.x_ref), custom_call_target="tpu_custom_call" | custom-call | bytes 50000000 | tf_op jit(solution)/shard_map/pallas_call | solution.py:183
  62.5 3.6 shard_map.256
  66.8 12.0 %shard_map.257 = bf16[4,256,128]{2,1,0:T(8,128)(2,1)} custom-call(bf16[4,256,128]{2,1,0:T(8,128)(2,1)} %copy-done.5), custom_call_target="tpu_custom_call" | custom-call | bytes 50000000 | tf_op jit(solution)/shard_map/pallas_call | solution.py:183
  80.2 2.5 convolution_convert_fusion.1.x_ref
  82.7 13.7 %shard_map.258 = bf16[4,128,1024]{2,1,0:T(8,128)(2,1)} custom-call(bf16[4,128,1024]{2,1,0:T(8,128)(2,1)} %convolution_convert_fusion.1.x_ref), custom_call_target="tpu_custom_call" | custom-call | bytes 50000000 | tf_op jit(solution)/shard_map/pallas_call | solution.py:183
  99.1 15.1 %shard_map.259 = bf16[4,128,1024]{2,1,0:T(8,128)(2,1)} custom-call(bf16[128,1024]{1,0:T(8,128)(2,1)} %add_convert_fusion.1.x_ref), custom_call_target="tpu_custom_call" | custom-call | bytes 50000000 | tf_op jit(solution)/shard_map/pallas_call | solution.py:183
  114.2 2.4 constant_dynamic-update-slice_fusion.2
  116.5 3.0 fusion.69
  120.9 2.9 fusion.68
  123.8 4.3 %convert_reduce_fusion.4 = (f32[1024]{0:T(1024)}, bf16[512,1024]{1,0:T(8,128)(2,1)S(1)}) fusion(f32[512,1024]{1,0:T(8,128)S(1)} %fusion.69, f32[1024]{0:T(1024)S(1)} %copy-done.59, bf16[1024,1024]{1,0:T(8,128)(2,1)S(1)} %constant_dynamic-update-slice_fusion.4, bf16[128,1024]{1,0:T(8,128)(2,1)} %collective-permute-done.9, ...), kind=kOutput, calls=%fused_computation.17 | convolution fusion | flops 1089993728 | bytes 6299648 | tf_op jit(solution)/shard_map/dot_general | solution.py:222
  128.2 2.3 convolution_convert_fusion
  130.4 3.5 fusion.70
  134.9 1.7 collective-permute-start.6
  138.1 2.7 fusion.40
  140.8 2.0 copy-done.20
  145.5 14.2 %shard_map.260 = bf16[4,128,1024]{2,1,0:T(8,128)(2,1)} custom-call(bf16[4,128,1024]{2,1,0:T(8,128)(2,1)} %bitcast.94, bf16[1024,512]{1,0:T(8,128)(2,1)} %split.105.refs_0_), custom_call_target="tpu_custom_call" | custom-call | bytes 50000000 | tf_op jit(solution)/shard_map/pallas_call | solution.py:183
  159.7 2.3 convert_reduce_fusion.2
  162.8 2.7 split.104.refs_0_
  167.1 2.4 fusion.61
  175.6 14.7 %shard_map.261 = bf16[4,128,1024]{2,1,0:T(8,128)(2,1)} custom-call(bf16[128,1024]{1,0:T(8,128)(2,1)} %convert_element_type.173.x_ref, bf16[512,1024]{1,0:T(8,128)(2,1)} %split.104.refs_0_, bf16[1024,512]{1,0:T(8,128)(2,1)} %copy-done.17), custom_call_target="tpu_custom_call" | custom-call | bytes 50000000 | tf_op jit(solution)/shard_map/pallas_call | solution.py:183
  190.3 1.7 fusion.37
  192.6 2.2 slice_add_fusion
  194.8 4.2 %collective-permute-done.15.refs_2_ = bf16[256,512]{1,0:T(8,128)(2,1)S(1)} collective-permute-done((bf16[256,512]{1,0:T(8,128)(2,1)S(1)}, bf16[256,512]{1,0:T(8,128)(2,1)S(1)}, u32[]{:S(2)}, u32[]{:S(2)}) %collective-permute-start.15) | collective-permute-done | bytes 262176 | tf_op jit(solution)/shard_map/ppermute | solution.py:40
  201.3 2.2 convolution_convert_fusion.2
  203.5 1.7 reshape.211
  205.2 1.8 copy.63
  209.5 1.8 collective-permute-start.13
  211.3 2.3 collective-permute-done.32
  213.6 1.8 collective-permute-start.33
  218.6 6.5 %collective-permute-done.33 = bf16[64,512]{1,0:T(8,128)(2,1)S(1)} collective-permute-done((bf16[64,512]{1,0:T(8,128)(2,1)S(1)}, bf16[64,512]{1,0:T(8,128)(2,1)S(1)}, u32[]{:S(2)}, u32[]{:S(2)}) %collective-permute-start.33) | collective-permute-done | bytes 65568 | tf_op jit(solution)/shard_map/ppermute | solution.py:76
  225.7 3.0 collective-permute-start.34
  232.8 14.4 %shard_map.262.ga_ref = bf16[4,256,128]{2,1,0:T(8,128)(2,1)} custom-call(bf16[4,256,128]{2,1,0:T(8,128)(2,1)} %bitcast.96, bf16[512,1024]{1,0:T(8,128)(2,1)} %collective-permute-done.11.refs_0_, bf16[512,512]{1,0:T(8,128)(2,1)} %collective-permute-done.12.refs_1_), custom_call_target="tpu_custom_call" | custom-call | bytes 50000000 | tf_op jit(solution)/shard_map/pallas_call | solution.py:183
  248.2 6.8 %shard_map.263.x_ref = bf16[4,256,384]{2,1,0:T(8,128)(2,1)S(1)} custom-call(bf16[4,256,384]{2,1,0:T(8,128)(2,1)S(1)} %copy-done.3, bf16[4,256,128]{2,1,0:T(8,128)(2,1)S(1)} %copy-done.6, f32[8,256]{1,0:T(8,128)S(1)} %get-tuple-element.17.log_ref, s32[4,256]{1,0:T(4,128)S(1)} %get-tuple-element.71.qpos_ref, s32[4,256]{1,0:T(4,128)S(1)} %reshape.205.qseg_ref, ...), custom_call_target="tpu_custom_call" | custom-call | flops 4000000000 | bytes 8000000 | tf_op jit(solution)/shard_map/pallas_call | solution.py:288
  257.7 15.7 %shard_map.264 = bf16[4,256,384]{2,1,0:T(8,128)(2,1)} custom-call(bf16[4,256,384]{2,1,0:T(8,128)(2,1)} %copy-done.4, bf16[256,1024]{1,0:T(8,128)(2,1)} %copy-done.26, bf16[256,512]{1,0:T(8,128)(2,1)} %collective-permute-done.14.refs_1_, bf16[256,512]{1,0:T(8,128)(2,1)} %copy-done.28), custom_call_target="tpu_custom_call" | custom-call | bytes 50000000 | tf_op jit(solution)/shard_map/pallas_call | solution.py:183
  273.3 2.4 reshape.214
  279.5 1.8 reduce-precision_convert_fusion.1
  281.2 3.1 collective-permute-start.17
  285.5 1.9 reduce-precision_convert_fusion
  288.7 3.4 collective-permute-start.30
  292.0 2.5 fusion.71
  296.4 3.5 collective-permute-start.31
  299.9 3.1 fusion.9.x_ref
  303.1 4.6 %collective-permute-done.31 = f32[1792]{0:T(1024)S(1)} collective-permute-done((f32[1792]{0:T(1024)S(1)}, f32[1792]{0:T(1024)S(1)}, u32[]{:S(2)}, u32[]{:S(2)}) %collective-permute-start.31) | collective-permute-done | bytes 7200 | tf_op jit(solution)/shard_map/ppermute | solution.py:214
  312.1 12.5 %shard_map.265 = bf16[4,128,1024]{2,1,0:T(8,128)(2,1)} custom-call(bf16[4,128,1024]{2,1,0:T(8,128)(2,1)} %fusion.9.x_ref, bf16[128,1024]{1,0:T(8,128)(2,1)} %copy-done.29, bf16[256,512]{1,0:T(8,128)(2,1)} %collective-permute-done.17.refs_1_, bf16[128,512]{1,0:T(8,128)(2,1)} %copy-done.37, bf16[512,768]{1,0:T(8,128)(2,1)} %split.106.refs_3_), custom_call_target="tpu_custom_call" | custom-call | bytes 50000000 | tf_op jit(solution)/shard_map/pallas_call | solution.py:183
  324.7 1.7 convert_reduce_fusion
  333.2 11.2 %collective-permute-done.20 = f32[6,1024]{1,0:T(8,128)S(1)} collective-permute-done((f32[6,1024]{1,0:T(8,128)S(1)}, f32[6,1024]{1,0:T(8,128)S(1)}, u32[]{:S(2)}, u32[]{:S(2)}) %collective-permute-start.20) | collective-permute-done | bytes 24608 | tf_op jit(solution)/shard_map/ppermute | solution.py:214
  344.3 3.4 collective-permute-start.21
  347.7 2.7 collective-permute-done.21
  352.6 1.8 collective-permute-start.23
  356.5 7.0 %collective-permute-done.25 = bf16[256,768]{1,0:T(8,128)(2,1)S(1)} collective-permute-done((bf16[256,768]{1,0:T(8,128)(2,1)S(1)}, bf16[256,768]{1,0:T(8,128)(2,1)S(1)}, u32[]{:S(2)}, u32[]{:S(2)}) %collective-permute-start.25) | collective-permute-done | bytes 393248 | tf_op jit(solution)/shard_map/ppermute | solution.py:76
  363.6 2.2 collective-permute-start.26
  366.4 8.7 %collective-permute-done.26 = bf16[128,768]{1,0:T(8,128)(2,1)S(1)} collective-permute-done((bf16[128,768]{1,0:T(8,128)(2,1)S(1)}, bf16[128,768]{1,0:T(8,128)(2,1)S(1)}, u32[]{:S(2)}, u32[]{:S(2)}) %collective-permute-start.26) | collective-permute-done | bytes 196640 | tf_op jit(solution)/shard_map/ppermute | solution.py:76
  376.5 1.6 maximum_convert_fusion.1
  378.1 7.6 %collective-permute-done.27 = bf16[128,768]{1,0:T(8,128)(2,1)S(1)} collective-permute-done((bf16[128,768]{1,0:T(8,128)(2,1)S(1)}, bf16[128,768]{1,0:T(8,128)(2,1)S(1)}, u32[]{:S(2)}, u32[]{:S(2)}) %collective-permute-start.27) | collective-permute-done | bytes 196640 | tf_op jit(solution)/shard_map/ppermute | solution.py:76
  387.6 9.2 %collective-permute-done.28 = bf16[256,768]{1,0:T(8,128)(2,1)S(1)} collective-permute-done((bf16[256,768]{1,0:T(8,128)(2,1)S(1)}, bf16[256,768]{1,0:T(8,128)(2,1)S(1)}, u32[]{:S(2)}, u32[]{:S(2)}) %collective-permute-start.28) | collective-permute-done | bytes 393248 | tf_op jit(solution)/shard_map/ppermute | solution.py:76
  (278 shorter events, 80.3 us)
Async XLA Ops:
  0.6 10.6 %copy-start = (s32[2,1024]{1,0:T(2,128)S(1)}, s32[2,1024]{1,0:T(2,128)}, u32[]{:S(2)}) copy-start(s32[2,1024]{1,0:T(2,128)} %param.16) | copy-start | bytes 24580
  0.7 10.7 %copy-start.40 = (bf16[2,64,1024]{2,1,0:T(8,128)(2,1)S(1)}, bf16[2,64,1024]{2,1,0:T(8,128)(2,1)}, u32[]{:S(2)}) copy-start(bf16[2,64,1024]{2,1,0:T(8,128)(2,1)} %param.15) | copy-start | bytes 786436
  2.4 121.4 %collective-permute-start.9 = (bf16[128,1024]{1,0:T(8,128)(2,1)S(1)}, bf16[128,1024]{1,0:T(8,128)(2,1)}, u32[]{:S(2)}, u32[]{:S(2)}) collective-permute-start(bf16[128,1024]{1,0:T(8,128)(2,1)S(1)} %get-tuple-element.29), channel_id=1, source_target_pairs={{0,1},{1,2},{2,3},{3,0},{4,5},{5,6},{6,7},{7,4},{8,9},{9,10},{10,1... | collective-permute-start | bytes 786440 | tf_op jit(solution)/shard_map/ppermute | solution.py:40
  2.8 121.0 %collective-permute-start.8 = (bf16[128,1024]{1,0:T(8,128)(2,1)S(1)}, bf16[128,1024]{1,0:T(8,128)(2,1)}, u32[]{:S(2)}, u32[]{:S(2)}) collective-permute-start(bf16[128,1024]{1,0:T(8,128)(2,1)S(1)} %get-tuple-element.29), channel_id=1, source_target_pairs={{0,2},{1,3},{2,0},{3,1},{4,6},{5,7},{6,4},{7,5},{8,10},{9,11},{10,... | collective-permute-start | bytes 786440 | tf_op jit(solution)/shard_map/ppermute | solution.py:40
  5.4 118.5 %collective-permute-start.7 = (bf16[128,1024]{1,0:T(8,128)(2,1)S(1)}, bf16[128,1024]{1,0:T(8,128)(2,1)}, u32[]{:S(2)}, u32[]{:S(2)}) collective-permute-start(bf16[128,1024]{1,0:T(8,128)(2,1)S(1)} %get-tuple-element.29), channel_id=1, source_target_pairs={{0,3},{1,0},{2,1},{3,2},{4,7},{5,4},{6,5},{7,6},{8,11},{9,8},{10,9... | collective-permute-start | bytes 786440 | tf_op jit(solution)/shard_map/ppermute | solution.py:40
  6.8 28.8 %collective-permute-start.1 = (bf16[256,512]{1,0:T(8,128)(2,1)}, bf16[256,512]{1,0:T(8,128)(2,1)}, u32[]{:S(2)}, u32[]{:S(2)}) collective-permute-start(bf16[256,512]{1,0:T(8,128)(2,1)} %param.21), channel_id=1, source_target_pairs={{0,16},{16,0},{1,17},{17,1},{2,18},{18,2},{3,19},{19,3},{4,20},{20... | collective-permute-start | bytes 786440 | tf_op jit(solution)/shard_map/ppermute | solution.py:40
  9.5 29.8 %copy-start.30 = (bf16[512,256]{1,0:T(8,128)(2,1)}, bf16[512,256]{1,0:T(8,128)(2,1)S(1)}, u32[]{:S(2)}) copy-start(bf16[512,256]{1,0:T(8,128)(2,1)S(1)} %get-tuple-element.48) | copy-start | bytes 786436
  9.5 29.8 %copy-start.32 = (bf16[512,256]{1,0:T(8,128)(2,1)}, bf16[512,256]{1,0:T(8,128)(2,1)S(1)}, u32[]{:S(2)}) copy-start(bf16[512,256]{1,0:T(8,128)(2,1)S(1)} %get-tuple-element.49) | copy-start | bytes 786436
  9.5 29.8 %copy-start.34 = (bf16[512,256]{1,0:T(8,128)(2,1)}, bf16[512,256]{1,0:T(8,128)(2,1)S(1)}, u32[]{:S(2)}) copy-start(bf16[512,256]{1,0:T(8,128)(2,1)S(1)} %get-tuple-element.50) | copy-start | bytes 786436
  10.5 28.3 %collective-permute-start = (bf16[512,768]{1,0:T(8,128)(2,1)}, bf16[512,768]{1,0:T(8,128)(2,1)}, u32[]{:S(2)}, u32[]{:S(2)}) collective-permute-start(bf16[512,768]{1,0:T(8,128)(2,1)} %pad_maximum_fusion.3), channel_id=1, source_target_pairs={{0,16},{16,0},{1,17},{17,1},{2,18},{18,2},{3,19},{19,3},{4,20},{20... | collective-permute-start | bytes 2359304 | tf_op jit(solution)/shard_map/ppermute | solution.py:40
  31.6 7.8 %copy-start.7 = (bf16[4,128,1024]{2,1,0:T(8,128)(2,1)S(1)}, bf16[4,128,1024]{2,1,0:T(8,128)(2,1)}, u32[]{:S(2)}) copy-start(bf16[4,128,1024]{2,1,0:T(8,128)(2,1)} %shard_map.254) | copy-start | bytes 3145732
  35.6 78.5 %collective-permute-start.2 = (bf16[512,1024]{1,0:T(8,128)(2,1)}, bf16[512,1024]{1,0:T(8,128)(2,1)}, u32[]{:S(2)}, u32[]{:S(2)}) collective-permute-start(bf16[512,1024]{1,0:T(8,128)(2,1)} %param.25), channel_id=1, source_target_pairs={{0,16},{16,0},{1,17},{17,1},{2,18},{18,2},{3,19},{19,3},{4,20},{20... | collective-permute-start | bytes 3145736 | tf_op jit(solution)/shard_map/ppermute | solution.py:40
  38.8 80.7 %collective-permute-start.3 = (bf16[1024,512]{1,0:T(8,128)(2,1)}, bf16[1024,512]{1,0:T(8,128)(2,1)}, u32[]{:S(2)}, u32[]{:S(2)}) collective-permute-start(bf16[1024,512]{1,0:T(8,128)(2,1)} %param.27), channel_id=1, source_target_pairs={{0,16},{16,0},{1,17},{17,1},{2,18},{18,2},{3,19},{19,3},{4,20},{20... | collective-permute-start | bytes 3145736 | tf_op jit(solution)/shard_map/ppermute | solution.py:40
  134.8 32.2 %collective-permute-start.4 = (bf16[128,1024]{1,0:T(8,128)(2,1)}, bf16[128,1024]{1,0:T(8,128)(2,1)}, u32[]{:S(2)}, u32[]{:S(2)}) collective-permute-start(bf16[128,1024]{1,0:T(8,128)(2,1)} %get-tuple-element.43), channel_id=1, source_target_pairs={{0,1},{1,2},{2,3},{3,0},{4,5},{5,6},{6,7},{7,4},{8,9},{9,10},{10,1... | collective-permute-start | bytes 786440 | tf_op jit(solution)/shard_map/ppermute | solution.py:40
  134.9 32.2 %collective-permute-start.6 = (bf16[128,1024]{1,0:T(8,128)(2,1)}, bf16[128,1024]{1,0:T(8,128)(2,1)}, u32[]{:S(2)}, u32[]{:S(2)}) collective-permute-start(bf16[128,1024]{1,0:T(8,128)(2,1)} %get-tuple-element.44), channel_id=1, source_target_pairs={{0,3},{1,0},{2,1},{3,2},{4,7},{5,4},{6,5},{7,6},{8,11},{9,8},{10,9... | collective-permute-start | bytes 786440 | tf_op jit(solution)/shard_map/ppermute | solution.py:40
  136.6 30.5 %collective-permute-start.5 = (bf16[128,1024]{1,0:T(8,128)(2,1)}, bf16[128,1024]{1,0:T(8,128)(2,1)}, u32[]{:S(2)}, u32[]{:S(2)}) collective-permute-start(bf16[128,1024]{1,0:T(8,128)(2,1)} %get-tuple-element.45), channel_id=1, source_target_pairs={{0,2},{1,3},{2,0},{3,1},{4,6},{5,7},{6,4},{7,5},{8,10},{9,11},{10,... | collective-permute-start | bytes 786440 | tf_op jit(solution)/shard_map/ppermute | solution.py:40
  143.9 27.2 %collective-permute-start.10 = (bf16[1024,512]{1,0:T(8,128)(2,1)}, bf16[1024,512]{1,0:T(8,128)(2,1)S(1)}, u32[]{:S(2)}, u32[]{:S(2)}) collective-permute-start(bf16[1024,512]{1,0:T(8,128)(2,1)} %split.105.refs_0_), channel_id=1, source_target_pairs={{0,16},{16,0},{1,17},{17,1},{2,18},{18,2},{3,19},{19,3},{4,20},{20... | collective-permute-start | bytes 3145736 | tf_op jit(solution)/shard_map/ppermute | solution.py:40
  165.5 27.1 %collective-permute-start.11 = (bf16[512,1024]{1,0:T(8,128)(2,1)}, bf16[512,1024]{1,0:T(8,128)(2,1)}, u32[]{:S(2)}, u32[]{:S(2)}) collective-permute-start(bf16[512,1024]{1,0:T(8,128)(2,1)} %split.104.refs_0_), channel_id=1, source_target_pairs={{0,16},{16,0},{1,17},{17,1},{2,18},{18,2},{3,19},{19,3},{4,20},{20... | collective-permute-start | bytes 3145736 | tf_op jit(solution)/shard_map/ppermute | solution.py:40
  174.3 41.1 %collective-permute-start.12 = (bf16[512,512]{1,0:T(8,128)(2,1)}, bf16[512,512]{1,0:T(8,128)(2,1)}, u32[]{:S(2)}, u32[]{:S(2)}) collective-permute-start(bf16[512,512]{1,0:T(8,128)(2,1)} %dynamic-slice_convert_fusion.1), channel_id=1, source_target_pairs={{0,4},{4,0},{8,12},{12,8},{1,5},{5,1},{9,13},{13,9},{2,6},{6,2},{1... | collective-permute-start | bytes 1572872 | tf_op jit(solution)/shard_map/ppermute | solution.py:76
  192.1 9.2 %copy-start.18 = (bf16[4,128,1024]{2,1,0:T(8,128)(2,1)S(1)}, bf16[4,128,1024]{2,1,0:T(8,128)(2,1)}, u32[]{:S(2)}) copy-start(bf16[4,128,1024]{2,1,0:T(8,128)(2,1)} %shard_map.261) | copy-start | bytes 3145732
  192.1 6.9 %collective-permute-start.15 = (bf16[256,512]{1,0:T(8,128)(2,1)S(1)}, bf16[256,512]{1,0:T(8,128)(2,1)S(1)}, u32[]{:S(2)}, u32[]{:S(2)}) collective-permute-start(bf16[256,512]{1,0:T(8,128)(2,1)S(1)} %split.107), channel_id=1, source_target_pairs={{0,16},{16,0},{1,17},{17,1},{2,18},{18,2},{3,19},{19,3},{4,20},{20... | collective-permute-start | bytes 786440 | tf_op jit(solution)/shard_map/ppermute | solution.py:40
  194.8 14.6 %copy-start.8 = (f32[512,1024]{1,0:T(8,128)}, f32[512,1024]{1,0:T(8,128)S(1)}, u32[]{:S(2)}) copy-start(f32[512,1024]{1,0:T(8,128)S(1)} %slice_add_fusion) | copy-start | bytes 6291460
  200.5 6.5 %collective-permute-start.18 = (bf16[128,512]{1,0:T(8,128)(2,1)}, bf16[128,512]{1,0:T(8,128)(2,1)S(1)}, u32[]{:S(2)}, u32[]{:S(2)}) collective-permute-start(bf16[128,512]{1,0:T(8,128)(2,1)} %dynamic-slice_convert_fusion.6), channel_id=1, source_target_pairs={{0,4},{4,0},{8,12},{12,8},{1,5},{5,1},{9,13},{13,9},{2,6},{6,2},{1... | collective-permute-start | bytes 393224 | tf_op jit(solution)/shard_map/ppermute | solution.py:76
  205.2 10.2 %copy-start.11 = (f32[1024,512]{1,0:T(8,128)S(1)}, f32[1024,512]{1,0:T(8,128)}, u32[]{:S(2)}) copy-start(f32[1024,512]{1,0:T(8,128)} %copy-done.10) | copy-start | bytes 6291460
  207.1 9.5 %copy-start.37 = (bf16[128,512]{1,0:T(8,128)(2,1)}, bf16[128,512]{1,0:T(8,128)(2,1)S(1)}, u32[]{:S(2)}) copy-start(bf16[128,512]{1,0:T(8,128)(2,1)S(1)} %collective-permute-done.18.refs_2_) | copy-start | bytes 393220
  208.1 5.5 %collective-permute-start.32 = (bf16[64,512]{1,0:T(8,128)(2,1)S(1)}, bf16[64,512]{1,0:T(8,128)(2,1)S(1)}, u32[]{:S(2)}, u32[]{:S(2)}) collective-permute-start(bf16[64,512]{1,0:T(8,128)(2,1)S(1)} %dynamic-slice_convert_fusion.7), channel_id=1, source_target_pairs={{0,8},{4,12},{8,0},{12,4},{1,9},{5,13},{9,1},{13,5},{2,10},{6,14},... | collective-permute-start | bytes 196616 | tf_op jit(solution)/shard_map/ppermute | solution.py:76
  209.4 20.8 %copy-start.9 = (f32[512,1024]{1,0:T(8,128)S(1)}, f32[512,1024]{1,0:T(8,128)}, u32[]{:S(2)}) copy-start(f32[512,1024]{1,0:T(8,128)} %copy-done.8) | copy-start | bytes 6291460
  209.5 20.8 %collective-permute-start.13 = (bf16[256,1024]{1,0:T(8,128)(2,1)S(1)}, bf16[256,1024]{1,0:T(8,128)(2,1)S(1)}, u32[]{:S(2)}, u32[]{:S(2)}) collective-permute-start(bf16[256,1024]{1,0:T(8,128)(2,1)S(1)} %dynamic-slice_convert_fusion), channel_id=1, source_target_pairs={{0,4},{4,0},{8,12},{12,8},{1,5},{5,1},{9,13},{13,9},{2,6},{6,2},{1... | collective-permute-start | bytes 1572872 | tf_op jit(solution)/shard_map/ppermute | solution.py:76
  213.6 11.4 %collective-permute-start.33 = (bf16[64,512]{1,0:T(8,128)(2,1)S(1)}, bf16[64,512]{1,0:T(8,128)(2,1)S(1)}, u32[]{:S(2)}, u32[]{:S(2)}) collective-permute-start(bf16[64,512]{1,0:T(8,128)(2,1)S(1)} %reduce-precision_convert_fusion.3), channel_id=1, source_target_pairs={{0,8},{4,12},{8,0},{12,4},{1,9},{5,13},{9,1},{13,5},{2,10},{6,14},... | collective-permute-start | bytes 196616 | tf_op jit(solution)/shard_map/ppermute | solution.py:76
  217.4 40.3 %collective-permute-start.14 = (bf16[256,512]{1,0:T(8,128)(2,1)}, bf16[256,512]{1,0:T(8,128)(2,1)}, u32[]{:S(2)}, u32[]{:S(2)}) collective-permute-start(bf16[256,512]{1,0:T(8,128)(2,1)} %dynamic-slice_convert_fusion.4), channel_id=1, source_target_pairs={{0,8},{4,12},{8,0},{12,4},{1,9},{5,13},{9,1},{13,5},{2,10},{6,14},... | collective-permute-start | bytes 786440 | tf_op jit(solution)/shard_map/ppermute | solution.py:76
  225.7 21.5 %copy-start.3 = (bf16[4,256,384]{2,1,0:T(8,128)(2,1)S(1)}, bf16[4,256,384]{2,1,0:T(8,128)(2,1)}, u32[]{:S(2)}) copy-start(bf16[4,256,384]{2,1,0:T(8,128)(2,1)} %shard_map.255.qkv_ref) | copy-start | bytes 2359300
  225.7 30.1 %collective-permute-start.34 = (bf16[128,512]{1,0:T(8,128)(2,1)}, bf16[128,512]{1,0:T(8,128)(2,1)}, u32[]{:S(2)}, u32[]{:S(2)}) collective-permute-start(bf16[128,512]{1,0:T(8,128)(2,1)} %pad_maximum_fusion.13), channel_id=1, source_target_pairs={{0,4},{4,0},{8,12},{12,8},{1,5},{5,1},{9,13},{13,9},{2,6},{6,2},{1... | collective-permute-start | bytes 393224 | tf_op jit(solution)/shard_map/ppermute | solution.py:76
  232.2 53.3 %collective-permute-start.16 = (bf16[128,1024]{1,0:T(8,128)(2,1)}, bf16[128,1024]{1,0:T(8,128)(2,1)S(1)}, u32[]{:S(2)}, u32[]{:S(2)}) collective-permute-start(bf16[128,1024]{1,0:T(8,128)(2,1)} %dynamic-slice_convert_fusion.3), channel_id=1, source_target_pairs={{0,8},{4,12},{8,0},{12,4},{1,9},{5,13},{9,1},{13,5},{2,10},{6,14},... | collective-permute-start | bytes 786440 | tf_op jit(solution)/shard_map/ppermute | solution.py:76
  278.2 6.6 %copy-start.47 = (f32[1024]{0:T(1024)S(1)}, f32[1024]{0:T(1024)}, u32[]{:S(2)}) copy-start(f32[1024]{0:T(1024)} %get-tuple-element.74) | copy-start | bytes 12292
  281.2 27.6 %collective-permute-start.17 = (bf16[256,512]{1,0:T(8,128)(2,1)}, bf16[256,512]{1,0:T(8,128)(2,1)}, u32[]{:S(2)}, u32[]{:S(2)}) collective-permute-start(bf16[256,512]{1,0:T(8,128)(2,1)} %reduce-precision_convert_fusion.1), channel_id=1, source_target_pairs={{0,8},{4,12},{8,0},{12,4},{1,9},{5,13},{9,1},{13,5},{2,10},{6,14},... | collective-permute-start | bytes 786440 | tf_op jit(solution)/shard_map/ppermute | solution.py:76
  284.9 3.7 collective-permute-start.29
  287.4 40.9 %collective-permute-start.35 = (bf16[128,1024]{1,0:T(8,128)(2,1)}, bf16[128,1024]{1,0:T(8,128)(2,1)}, u32[]{:S(2)}, u32[]{:S(2)}) collective-permute-start(bf16[128,1024]{1,0:T(8,128)(2,1)} %reduce-precision_convert_fusion), channel_id=1, source_target_pairs={{0,8},{4,12},{8,0},{12,4},{1,9},{5,13},{9,1},{13,5},{2,10},{6,14},... | collective-permute-start | bytes 786440 | tf_op jit(solution)/shard_map/ppermute | solution.py:76
  288.6 11.3 %copy-start.31 = (bf16[512,256]{1,0:T(8,128)(2,1)S(1)}, bf16[512,256]{1,0:T(8,128)(2,1)}, u32[]{:S(2)}) copy-start(bf16[512,256]{1,0:T(8,128)(2,1)} %copy-done.30) | copy-start | bytes 786436
  288.6 11.3 %copy-start.33 = (bf16[512,256]{1,0:T(8,128)(2,1)S(1)}, bf16[512,256]{1,0:T(8,128)(2,1)}, u32[]{:S(2)}) copy-start(bf16[512,256]{1,0:T(8,128)(2,1)} %copy-done.32) | copy-start | bytes 786436
  288.6 11.3 %copy-start.35 = (bf16[512,256]{1,0:T(8,128)(2,1)S(1)}, bf16[512,256]{1,0:T(8,128)(2,1)}, u32[]{:S(2)}) copy-start(bf16[512,256]{1,0:T(8,128)(2,1)} %copy-done.34) | copy-start | bytes 786436
  288.6 11.3 %copy-start.36 = (bf16[4,128,768]{2,1,0:T(8,128)(2,1)S(1)}, bf16[4,128,768]{2,1,0:T(8,128)(2,1)}, u32[]{:S(2)}) copy-start(bf16[4,128,768]{2,1,0:T(8,128)(2,1)} %dot_general.51) | copy-start | bytes 2359300
  288.7 7.7 %collective-permute-start.30 = (f32[1792]{0:T(1024)S(1)}, f32[1792]{0:T(1024)S(1)}, u32[]{:S(2)}, u32[]{:S(2)}) collective-permute-start(f32[1792]{0:T(1024)S(1)} %fusion.58), channel_id=1, source_target_pairs={{0,4},{4,0},{8,12},{12,8},{1,5},{5,1},{9,13},{13,9},{2,6},{6,2},{1... | collective-permute-start | bytes 21512 | tf_op jit(solution)/shard_map/ppermute | solution.py:214
  295.5 55.1 %collective-permute-start.24 = (bf16[512,768]{1,0:T(8,128)(2,1)}, bf16[512,768]{1,0:T(8,128)(2,1)}, u32[]{:S(2)}, u32[]{:S(2)}) collective-permute-start(bf16[512,768]{1,0:T(8,128)(2,1)} %split.106.refs_3_), channel_id=1, source_target_pairs={{0,16},{16,0},{1,17},{17,1},{2,18},{18,2},{3,19},{19,3},{4,20},{20... | collective-permute-start | bytes 2359304 | tf_op jit(solution)/shard_map/ppermute | solution.py:40
  296.4 11.2 %collective-permute-start.31 = (f32[1792]{0:T(1024)S(1)}, f32[1792]{0:T(1024)S(1)}, u32[]{:S(2)}, u32[]{:S(2)}) collective-permute-start(f32[1792]{0:T(1024)S(1)} %add.325), channel_id=1, source_target_pairs={{0,8},{4,12},{8,0},{12,4},{1,9},{5,13},{9,1},{13,5},{2,10},{6,14},... | collective-permute-start | bytes 21512 | tf_op jit(solution)/shard_map/ppermute | solution.py:214
  311.5 15.7 %copy-start.42 = (f32[1024]{0:T(1024)S(1)}, f32[1024]{0:T(1024)}, u32[]{:S(2)}) copy-start(f32[1024]{0:T(1024)} %copy-done.41) | copy-start | bytes 12292
  311.5 15.7 %copy-start.49 = (f32[128]{0:T(128)S(1)}, f32[128]{0:T(128)}, u32[]{:S(2)}) copy-start(f32[128]{0:T(128)} %copy-done.48) | copy-start | bytes 1540
  311.5 15.7 %copy-start.51 = (f32[128]{0:T(128)S(1)}, f32[128]{0:T(128)}, u32[]{:S(2)}) copy-start(f32[128]{0:T(128)} %copy-done.50) | copy-start | bytes 1540
  311.5 16.0 %copy-start.43 = (f32[1024]{0:T(1024)S(1)}, f32[1024]{0:T(1024)}, u32[]{:S(2)}) copy-start(f32[1024]{0:T(1024)} %get-tuple-element.28) | copy-start | bytes 12292
  311.5 16.0 %copy-start.44 = (f32[1024]{0:T(1024)S(1)}, f32[1024]{0:T(1024)}, u32[]{:S(2)}) copy-start(f32[1024]{0:T(1024)} %get-tuple-element.20) | copy-start | bytes 12292
  311.5 16.0 %copy-start.45 = (f32[1024]{0:T(1024)S(1)}, f32[1024]{0:T(1024)}, u32[]{:S(2)}) copy-start(f32[1024]{0:T(1024)} %get-tuple-element.18) | copy-start | bytes 12292
  311.5 16.0 %copy-start.46 = (f32[1024]{0:T(1024)S(1)}, f32[1024]{0:T(1024)}, u32[]{:S(2)}) copy-start(f32[1024]{0:T(1024)} %get-tuple-element.30) | copy-start | bytes 12292
  311.5 63.7 %collective-permute-start.37 = (bf16[512,512]{1,0:T(8,128)(2,1)}, bf16[512,512]{1,0:T(8,128)(2,1)}, u32[]{:S(2)}, u32[]{:S(2)}) collective-permute-start(bf16[512,512]{1,0:T(8,128)(2,1)} %pad_maximum_fusion.5), channel_id=1, source_target_pairs={{0,4},{4,0},{8,12},{12,8},{1,5},{5,1},{9,13},{13,9},{2,6},{6,2},{1... | collective-permute-start | bytes 1572872 | tf_op jit(solution)/shard_map/ppermute | solution.py:76
  327.6 4.0 collective-permute-start.19
  329.4 56.4 %collective-permute-start.36 = (bf16[256,1024]{1,0:T(8,128)(2,1)S(1)}, bf16[256,1024]{1,0:T(8,128)(2,1)S(1)}, u32[]{:S(2)}, u32[]{:S(2)}) collective-permute-start(bf16[256,1024]{1,0:T(8,128)(2,1)S(1)} %pad_maximum_fusion.4), channel_id=1, source_target_pairs={{0,4},{4,0},{8,12},{12,8},{1,5},{5,1},{9,13},{13,9},{2,6},{6,2},{1... | collective-permute-start | bytes 1572872 | tf_op jit(solution)/shard_map/ppermute | solution.py:76
  331.6 12.7 %collective-permute-start.20 = (f32[6,1024]{1,0:T(8,128)S(1)}, f32[6,1024]{1,0:T(8,128)S(1)}, u32[]{:S(2)}, u32[]{:S(2)}) collective-permute-start(f32[6,1024]{1,0:T(8,128)S(1)} %fusion.88), channel_id=1, source_target_pairs={{0,4},{4,0},{8,12},{12,8},{1,5},{5,1},{9,13},{13,9},{2,6},{6,2},{1... | collective-permute-start | bytes 73736 | tf_op jit(solution)/shard_map/ppermute | solution.py:214
  344.3 6.1 %collective-permute-start.21 = (f32[6,1024]{1,0:T(8,128)S(1)}, f32[6,1024]{1,0:T(8,128)S(1)}, u32[]{:S(2)}, u32[]{:S(2)}) collective-permute-start(f32[6,1024]{1,0:T(8,128)S(1)} %add.316), channel_id=1, source_target_pairs={{0,8},{4,12},{8,0},{12,4},{1,9},{5,13},{9,1},{13,5},{2,10},{6,14},... | collective-permute-start | bytes 73736 | tf_op jit(solution)/shard_map/ppermute | solution.py:214
  350.5 2.0 collective-permute-start.22
  352.0 11.5 %collective-permute-start.25 = (bf16[256,768]{1,0:T(8,128)(2,1)S(1)}, bf16[256,768]{1,0:T(8,128)(2,1)S(1)}, u32[]{:S(2)}, u32[]{:S(2)}) collective-permute-start(bf16[256,768]{1,0:T(8,128)(2,1)S(1)} %dynamic-slice_convert_fusion.2), channel_id=1, source_target_pairs={{0,4},{4,0},{8,12},{12,8},{1,5},{5,1},{9,13},{13,9},{2,6},{6,2},{1... | collective-permute-start | bytes 1179656 | tf_op jit(solution)/shard_map/ppermute | solution.py:76
  352.5 22.7 %copy-start.23 = (bf16[256,512]{1,0:T(8,128)(2,1)S(1)}, bf16[256,512]{1,0:T(8,128)(2,1)}, u32[]{:S(2)}) copy-start(bf16[256,512]{1,0:T(8,128)(2,1)} %copy-done.22) | copy-start | bytes 786436
  352.5 22.7 %copy-start.25 = (bf16[256,512]{1,0:T(8,128)(2,1)S(1)}, bf16[256,512]{1,0:T(8,128)(2,1)}, u32[]{:S(2)}) copy-start(bf16[256,512]{1,0:T(8,128)(2,1)} %copy-done.24) | copy-start | bytes 786436
  352.6 4.0 collective-permute-start.23
  363.6 11.4 %collective-permute-start.26 = (bf16[128,768]{1,0:T(8,128)(2,1)S(1)}, bf16[128,768]{1,0:T(8,128)(2,1)S(1)}, u32[]{:S(2)}, u32[]{:S(2)}) collective-permute-start(bf16[128,768]{1,0:T(8,128)(2,1)S(1)} %dynamic-slice_convert_fusion.5), channel_id=1, source_target_pairs={{0,8},{4,12},{8,0},{12,4},{1,9},{5,13},{9,1},{13,5},{2,10},{6,14},... | collective-permute-start | bytes 589832 | tf_op jit(solution)/shard_map/ppermute | solution.py:76
  375.1 10.5 %collective-permute-start.27 = (bf16[128,768]{1,0:T(8,128)(2,1)S(1)}, bf16[128,768]{1,0:T(8,128)(2,1)S(1)}, u32[]{:S(2)}, u32[]{:S(2)}) collective-permute-start(bf16[128,768]{1,0:T(8,128)(2,1)S(1)} %reduce-precision_convert_fusion.2), channel_id=1, source_target_pairs={{0,8},{4,12},{8,0},{12,4},{1,9},{5,13},{9,1},{13,5},{2,10},{6,14},... | collective-permute-start | bytes 589832 | tf_op jit(solution)/shard_map/ppermute | solution.py:76
  385.7 11.1 %collective-permute-start.28 = (bf16[256,768]{1,0:T(8,128)(2,1)S(1)}, bf16[256,768]{1,0:T(8,128)(2,1)S(1)}, u32[]{:S(2)}, u32[]{:S(2)}) collective-permute-start(bf16[256,768]{1,0:T(8,128)(2,1)S(1)} %pad_maximum_fusion.6), channel_id=1, source_target_pairs={{0,4},{4,0},{8,12},{12,8},{1,5},{5,1},{9,13},{13,9},{2,6},{6,2},{1... | collective-permute-start | bytes 1179656 | tf_op jit(solution)/shard_map/ppermute | solution.py:76
  (34 other events, 84.9 us)
